TPU v7x, 512 devices: a whole 4x8x8 slice. The times are simulated.
512 devices in a mesh: gx: 32 (over y, x), gy: 16 (over z, core).
Axes of the slice: x: 4, y: 8, z: 8, core: 2. Of those that a mesh axis runs over, the one named last changes fastest.
Arguments:
- material: int32 [4, 256, 2048], P(None, 'gx', 'gy'), may hold values from 0 to 3
- face_open: int32 [3, 4, 256, 2048], P(None, None, 'gx', 'gy'), may hold values from 1 to 64
Outputs:
- first_level: float32 [27, 2, 128, 1024], P(None, None, 'gx', 'gy')
- second_level: float32 [27, 1, 64, 512], P(None, None, 'gx', 'gy')
All inputs are finite; a program needn't handle non-finite values.
Results may differ from a plain program's by a relative error of at most 0.0003.
Values sent between devices are 32-bit elements; how exact they have to be, the bound alone decides.
No kernel may reach another device: no remote copies, remote signals or barrier semaphores. Data moves between devices by JAX's collectives and lax.ppermute only.
A program may use at most 64 MiB of HBM per device.

v0:
```python
import functools

import jax
import jax.numpy as jnp
from jax import lax
from jax.experimental import pallas as pl
from jax.experimental.pallas import tpu as pltpu
from jax.sharding import PartitionSpec as P

permit_levels = (1.0 / 80.0, 4.0 / 80.0, 20.0 / 80.0, 1.0)

ROWS, LANES = 8, 128


def permittivity(material):
    values = jnp.zeros(material.shape, jnp.float32)
    for material_id in range(4):
        values = values + jnp.where(material == material_id, permit_levels[material_id], 0.0)
    return values


def shifted(values, by_x, by_y):
    if by_x:
        values = pltpu.roll(values, (-by_x) % ROWS, 0)
    if by_y:
        values = pltpu.roll(values, (-by_y) % LANES, 1)
    return values


def pick_lanes(values, index):
    return jnp.take_along_axis(values, index, axis=1)


def times(a, b):
    if a is None:
        return b
    if b is None:
        return a
    return a * b


def minus(a, b):
    return (1.0 if a is None else a) - (1.0 if b is None else b)


def line_terms(lower, upper):
    total = lower + upper
    inverse = 1.0 / jnp.where(total > 0.0, total, 1.0)
    f = lower * inverse
    g = upper * inverse
    return f, g, lower * g, lower * f, upper * g


def first_operator(c, last_x, last_y, rows, lanes):
    lines = {}
    for z in range(4):
        for p in range(2):
            lines[1, z, p] = line_terms(c[1][z][0][p], c[1][z][1][p])
            lines[2, z, p] = line_terms(c[2][z][p][0], c[2][z][p][1])
    for zc in range(2):
        for px in range(2):
            for py in range(2):
                lines[0, zc, px, py] = line_terms(c[0][2 * zc][px][py], c[0][2 * zc + 1][px][py])

    rolled = {}

    def fraction(dim, zc, node, raised):
        pz, px, py = node
        if raised == 0:
            zc, raised = zc + 1, None
        if dim == 0:
            key = (0, zc, px, py)
        elif dim == 1:
            key = (1, 2 * zc + pz, py)
        else:
            key = (2, 2 * zc + pz, px)
        if raised is None:
            return lines[key][:2]
        if (key, raised) not in rolled:
            f = shifted(lines[key][0], int(raised == 1), int(raised == 2))
            rolled[key, raised] = (f, 1.0 - f)
        return rolled[key, raised]

    def transverse(d, zc, node, raised):
        dims = [dim for dim in range(3) if dim != d]
        entries = {(0, 0, 0): None}
        for dim in dims:
            if not node[dim]:
                continue
            pair = fraction(dim, zc, node, raised)
            fresh = {}
            for corner, weight in entries.items():
                for side in range(2):
                    moved = list(corner)
                    moved[dim] = side
                    if dim == 0 and side == 1 and zc == 1:
                        continue
                    fresh[tuple(moved)] = times(weight, pair[side])
            entries = fresh
        return entries

    sums = {}

    def put(zc, low, high, value):
        offset = tuple(b - a for a, b in zip(low, high))
        if offset < (0, 0, 0):
            low, high = high, low
            offset = tuple(-o for o in offset)
        if zc + low[0] > 1 or zc + high[0] > 1:
            return
        key = (offset, zc + low[0], low[1], low[2])
        sums[key] = sums[key] + value if key in sums else value

    for d in range(3):
        dims = [dim for dim in range(3) if dim != d]
        for zc in range(2):
            top = d == 0 and zc == 1
            for q1 in range(2):
                for q2 in range(2):
                    node = [0, 0, 0]
                    node[dims[0]], node[dims[1]] = q1, q2
                    odd = list(node)
                    odd[d] = 1
                    if d == 0:
                        key = (0, zc, node[1], node[2])
                    elif d == 1:
                        key = (1, 2 * zc + node[0], node[2])
                    else:
                        key = (2, 2 * zc + node[0], node[1])
                    _, _, s, h, k = lines[key]

                    def raised_corner(corner):
                        moved = list(corner)
                        moved[d] = 1
                        return tuple(moved)

                    zero = (0, 0, 0)
                    if not (q1 or q2):
                        put(zc, zero, zero, s)
                        if not top:
                            up = raised_corner(zero)
                            put(zc, up, up, s)
                            put(zc, zero, up, -s)
                        continue
                    alpha = transverse(d, zc, node, None)
                    beta = transverse(d, zc, odd, None)
                    corners = list(alpha)
                    delta = {t: minus(alpha[t], beta[t]) for t in corners}
                    for i, t in enumerate(corners):
                        s_alpha, h_delta = s * alpha[t], h * delta[t]
                        for u in corners[i:]:
                            put(zc, t, u, s_alpha * alpha[u] + h_delta * delta[u])
                    if top:
                        continue
                    gamma = transverse(d, zc, node, d)
                    epsilon = {t: minus(gamma[t], beta[t]) for t in corners}
                    for i, t in enumerate(corners):
                        s_gamma, k_epsilon = s * gamma[t], k * epsilon[t]
                        for u in corners[i:]:
                            put(zc, raised_corner(t), raised_corner(u), s_gamma * gamma[u] + k_epsilon * epsilon[u])
                    for t in corners:
                        s_delta, s_alpha = s * delta[t], s * alpha[t]
                        for u in corners:
                            put(zc, t, raised_corner(u), s_delta * epsilon[u] - s_alpha * gamma[u])

    drop_x = (rows == ROWS // 2 - 1) & last_x
    drop_y = (lanes == LANES // 2 - 1) & last_y

    def inside(values, offset):
        if offset[1] == 1 and offset[2] == 1:
            return jnp.where(drop_x | drop_y, 0.0, values)
        if offset[1] == 1:
            return jnp.where(drop_x, 0.0, values)
        if offset[2] == 1:
            return jnp.where(drop_y, 0.0, values)
        return values

    operator = {}
    keys = sorted({(offset, z) for offset, z, _, _ in sums})
    for offset, z in keys:
        total = None
        for ax in range(2):
            part = sums.get((offset, z, ax, 0))
            side = sums.get((offset, z, ax, 1))
            if side is not None:
                side = shifted(side, 0, -1)
                part = side if part is None else part + side
            if part is None:
                continue
            part = shifted(part, -ax, 0)
            total = part if total is None else total + part
        operator[offset, z] = inside(total, offset)
        if offset != (0, 0, 0):
            mirror = tuple(-o for o in offset)
            operator[mirror, z + offset[0]] = inside(shifted(total, -offset[1], -offset[2]), mirror)

    chain = [
        [lines[0, z, 0, 0][2] for z in range(2)],
        [lines[1, 2 * z, 0][2] for z in range(2)],
        [lines[2, 2 * z, 0][2] for z in range(2)],
    ]
    return operator, chain


def second_operator(operator, chain, last_x, last_y, rows, lanes):
    odd = {1: rows % 2 == 1, 2: lanes % 2 == 1}
    depth = line_terms(chain[0][0], chain[0][1])[0]
    down, up = {}, {}
    for d in (1, 2):
        for z in range(2):
            here = chain[d][z]
            before = shifted(here, -int(d == 1), -int(d == 2))
            f, g = line_terms(before, here)[:2]
            down[d, z] = jnp.where(odd[d], f, 1.0)
            up[d, z] = jnp.where(odd[d], g, 1.0)
    down_z = {0: down[1, 0], 1: down[1, 1] * depth}
    up_z = {0: up[1, 0], 1: up[1, 1] * depth}

    reaches = ((-1, -1), (0, -1), (0, 0), (0, 1), (1, 0), (1, 1))

    def factors(d, lower, upper):
        base = {}
        for j, o in reaches:
            source = lower if (j, o) in ((-1, -1), (0, 0), (0, 1)) else upper
            source = shifted(source, o if d == 1 else 0, o if d == 2 else 0)
            if (j, o) == (0, 1):
                source = jnp.where(odd[d], 0.0, source)
            if (j, o) == (1, 0):
                source = jnp.where(odd[d], source, 0.0)
            base[j, o] = source
        return {
            (j, o, across): shifted(base[j, o], 0 if d == 1 else across, across if d == 1 else 0)
            for j, o in reaches
            for across in (-1, 0, 1)
        }

    spread = {}
    for far in range(2):
        along_x = factors(1, down_z[far], up_z[far])
        along_y = factors(2, down[2, far], up[2, far])
        for jx, ox in reaches:
            for jy, oy in reaches:
                weight = along_x[jx, ox, oy] * along_y[jy, oy, ox]
                for z in range(2):
                    term = operator[(far - z, ox, oy), z] * weight
                    key = (z, jx, jy)
                    spread[key] = spread[key] + term if key in spread else term

    sides = {
        (z, d): {-1: up_z[z] if d == 1 else up[2, z], 0: depth if (d == 1 and z == 1) else None, 1: down_z[z] if d == 1 else down[2, z]}
        for z in range(2)
        for d in (1, 2)
    }
    own = {(z, mx, my): times(sides[z, 1][mx], sides[z, 2][my]) for z in range(2) for mx in (-1, 0, 1) for my in (-1, 0, 1)}

    def taken(offset):
        return [(m, offset + 1 if m == -1 else offset) for m in (-1, 0, 1) if m * offset != -1]

    drop_x = (rows == ROWS // 2 - 2) & last_x
    drop_y = (lanes == LANES // 2 - 2) & last_y
    results = {}
    for ox in (-1, 0, 1):
        for oy in (-1, 0, 1):
            total = None
            for my, jy in taken(oy):
                part = None
                for mx, jx in taken(ox):
                    term = times(own[0, mx, my], spread[0, jx, jy]) + times(own[1, mx, my], spread[1, jx, jy])
                    term = shifted(term, mx, 0)
                    part = term if part is None else part + term
                part = shifted(part, 0, my)
                total = part if total is None else total + part
            if ox == 1:
                total = jnp.where(drop_x, 0.0, total)
            if oy == 1:
                total = jnp.where(drop_y, 0.0, total)
            results[ox, oy] = total
    return results


def couplings_kernel(eps_ref, face_ref, own_ref, far_ref, near_ref):
    odd_x = lax.axis_index("gx") % 2 == 1
    for r in range(12):
        values = face_ref[r // 4, r % 4].astype(jnp.float32) / 64.0 * eps_ref[r % 4]
        own_ref[r] = values
        far_ref[r] = jnp.where(odd_x, values[4:8, :], values[0:4, :])
        near_ref[r] = jnp.where(odd_x, values[0:4, :], values[4:8, :])


def gather_kernel(own_ref, far_rows_ref, near_rows_ref, rows_ref, far_ref, near_ref, block):
    odd_x = lax.axis_index("gx") % 2 == 1
    odd_y = lax.axis_index("gy") % 2 == 1
    lanes = lax.broadcasted_iota(jnp.int32, (ROWS, LANES), 1)
    low = jnp.zeros((ROWS, LANES), jnp.float32)
    high = jnp.zeros((ROWS, LANES), jnp.float32)
    for r in range(12):
        block[r, 0:8, :] = own_ref[r]
        block[r, 8:12, :] = jnp.where(odd_x, far_rows_ref[r], near_rows_ref[r])
        block[r, 12:16, :] = jnp.where(odd_x, near_rows_ref[r], far_rows_ref[r])
        for px in range(2):
            k = 2 * r + px
            values = block[r, pl.ds(px, 8, stride=2), :]
            rows_ref[k] = values
            turned = pltpu.roll(values, (4 * k + 4) % LANES, 1)
            low = jnp.where((lanes >= 4 * k) & (lanes < 4 * k + 4), turned, low)
            high = jnp.where(lanes == 4 * k + 4, turned, high)
    far_ref[...] = jnp.where(odd_y, low, high)
    near_ref[...] = jnp.where(odd_y, high, low)


def operator_kernel(rows_ref, far_ref, near_ref, first_ref, second_ref):
    rows = lax.broadcasted_iota(jnp.int32, (ROWS, LANES), 0)
    lanes = lax.broadcasted_iota(jnp.int32, (ROWS, LANES), 1)
    last_x = lax.axis_index("gx") == lax.axis_size("gx") - 1
    last_y = lax.axis_index("gy") == lax.axis_size("gy") - 1

    odd_y = lax.axis_index("gy") % 2 == 1
    left = jnp.where(odd_y, near_ref[...], far_ref[...])
    right = jnp.where(odd_y, far_ref[...], near_ref[...])
    source = ((lanes + 2) % LANES // 2 * 4 + 2 * (lanes % 2)) % LANES
    above = pick_lanes(right, (2 * lanes + 4) % LANES)
    edge_even = jnp.where((lanes >= 64) & (lanes < 112), above, pick_lanes(left, source))
    edge_odd = pick_lanes(left, (source + 1) % LANES)
    at_even = (lanes >= 126) | (lanes == 64)
    at_odd = lanes >= 126
    even_lanes = (2 * lanes) % LANES
    odd_lanes = (2 * lanes + 1) % LANES

    c = [[[[None, None], [None, None]] for _ in range(4)] for _ in range(3)]
    for d in range(3):
        for z in range(4):
            for px in range(2):
                k = (d * 4 + z) * 2 + px
                values = rows_ref[k]
                c[d][z][px][0] = jnp.where(at_even, shifted(edge_even, 0, 2 * k), pick_lanes(values, even_lanes))
                c[d][z][px][1] = jnp.where(at_odd, shifted(edge_odd, 0, 2 * k), pick_lanes(values, odd_lanes))

    operator, chain = first_operator(c, last_x, last_y, rows, lanes)
    empty = jnp.zeros((ROWS, LANES), jnp.float32)
    full = {}
    for o in range(27):
        offset = (o // 9 - 1, o // 3 % 3 - 1, o % 3 - 1)
        for z in range(2):
            values = operator.get((offset, z), empty)
            full[offset, z] = values
            first_ref[o, z] = values[0:4, 0:64]

    results = second_operator(full, chain, last_x, last_y, rows, lanes)
    second_ref[...] = jnp.zeros(second_ref.shape, jnp.float32)
    for (ox, oy), values in results.items():
        o = 9 + (ox + 1) * 3 + oy + 1
        compact = pick_lanes(values, even_lanes)
        second_ref[o, 0, 0:1, :] = compact[0:1, 0:32]
        second_ref[o, 0, 1:2, :] = compact[2:3, 0:32]


def swapped(values, axis, first):
    pairs = [(i, i + 1) for i in range(first, lax.axis_size(axis) - 1, 2)]
    return lax.ppermute(values, axis, pairs + [(b, a) for a, b in pairs])


def body(material, face_open):
    whole = pl.BlockSpec(memory_space=pltpu.VMEM)
    page = jax.ShapeDtypeStruct((ROWS, LANES), jnp.float32)
    edge = jax.ShapeDtypeStruct((12, 4, LANES), jnp.float32)
    small = pltpu.CompilerParams(vmem_limit_bytes=1 << 20)
    own, far, near = pl.pallas_call(
        couplings_kernel,
        out_shape=(jax.ShapeDtypeStruct((12, ROWS, LANES), jnp.float32), edge, edge),
        in_specs=[whole] * 2,
        out_specs=(whole,) * 3,
        compiler_params=small,
        name="couplings",
    )(permittivity(material), face_open)
    far_rows = swapped(far, "gx", 1)
    near_rows = swapped(near, "gx", 0)
    rows, far, near = pl.pallas_call(
        gather_kernel,
        out_shape=(jax.ShapeDtypeStruct((24, ROWS, LANES), jnp.float32), page, page),
        in_specs=[whole] * 3,
        out_specs=(whole,) * 3,
        scratch_shapes=[pltpu.VMEM((12, 16, LANES), jnp.float32)],
        compiler_params=small,
        name="gather_rows",
    )(own, far_rows, near_rows)
    far_columns = swapped(far, "gy", 1)
    near_columns = swapped(near, "gy", 0)
    return pl.pallas_call(
        operator_kernel,
        out_shape=(
            jax.ShapeDtypeStruct((27, 2, 4, 64), jnp.float32),
            jax.ShapeDtypeStruct((27, 1, 2, 32), jnp.float32),
        ),
        in_specs=[whole] * 3,
        out_specs=(whole,) * 2,
        compiler_params=pltpu.CompilerParams(vmem_limit_bytes=2 << 20),
        name="operators",
    )(rows, far_columns, near_columns)


def solution(mesh):
    placed = (P(None, "gx", "gy"), P(None, None, "gx", "gy"))
    return jax.shard_map(
        body,
        mesh=mesh,
        in_specs=placed,
        out_specs=(P(None, None, "gx", "gy"), P(None, None, "gx", "gy")),
        check_vma=False,
    )
```

profile of v0, /device:TPU:249, one launch (start us, length us, event | category | flops | bytes accessed | tf_op | source)
XLA Modules:
  0.0 23.6 jit_solution(17409932116199423696)
XLA Ops:
  0.6 0.7 %select_add_fusion.eps_ref = f32[4,8,128]{2,1,0:T(8,128)S(1)} fusion(s32[4,8,128]{2,1,0:T(8,128)} %param.2), kind=kLoop, calls=%fused_computation | loop fusion | flops 45056 | bytes 32768 | tf_op jit(solution)/shard_map/add | solution.py:18
  1.4 0.0 copy-start
  1.4 0.8 %copy-done = s32[3,4,8,128]{3,2,1,0:T(8,128)S(1)} copy-done((s32[3,4,8,128]{3,2,1,0:T(8,128)S(1)}, s32[3,4,8,128]{3,2,1,0:T(8,128)}, u32[]{:S(2)}) %copy-start) | copy-done | bytes 49176
  2.2 5.2 %collective-permute-start = (f32[12,4,128]{2,1,0:T(4,128)S(1)}, f32[12,4,128]{2,1,0:T(4,128)S(1)}, u32[]{:S(2)}, u32[]{:S(2)}) collective-permute-start(f32[12,4,128]{2,1,0:T(4,128)S(1)} %get-tuple-element.9), channel_id=1, source_target_pairs={{16,32},{48,64},{80,96},{112,128},{144,160},{176,192},{208,224},{2... | collective-permute-start | bytes 73736 | tf_op jit(solution)/shard_map/ppermute | solution.py:359
  7.4 1.9 %collective-permute-start.1 = (f32[12,4,128]{2,1,0:T(4,128)S(1)}, f32[12,4,128]{2,1,0:T(4,128)S(1)}, u32[]{:S(2)}, u32[]{:S(2)}) collective-permute-start(f32[12,4,128]{2,1,0:T(4,128)S(1)} %get-tuple-element.10), channel_id=1, source_target_pairs={{0,16},{32,48},{64,80},{96,112},{128,144},{160,176},{192,208},{224... | collective-permute-start | bytes 73736 | tf_op jit(solution)/shard_map/ppermute | solution.py:359
  9.3 0.0 collective-permute-done.far_rows_ref
  9.3 2.6 %collective-permute-done.1.near_rows_ref = f32[12,4,128]{2,1,0:T(4,128)S(1)} collective-permute-done((f32[12,4,128]{2,1,0:T(4,128)S(1)}, f32[12,4,128]{2,1,0:T(4,128)S(1)}, u32[]{:S(2)}, u32[]{:S(2)}) %collective-permute-start.1) | collective-permute-done | bytes 24608 | tf_op jit(solution)/shard_map/ppermute | solution.py:359
  11.9 0.1 gather_rows.1
  12.1 7.2 %collective-permute-start.2 = (f32[8,128]{1,0:T(8,128)S(1)}, f32[8,128]{1,0:T(8,128)S(1)}, u32[]{:S(2)}, u32[]{:S(2)}) collective-permute-start(f32[8,128]{1,0:T(8,128)S(1)} %get-tuple-element.12), channel_id=1, source_target_pairs={{1,2},{3,4},{5,6},{7,8},{9,10},{11,12},{13,14},{2,1},{4,3},{6,5},{... | collective-permute-start | bytes 12296 | tf_op jit(solution)/shard_map/ppermute | solution.py:359
  19.3 1.9 %collective-permute-start.3 = (f32[8,128]{1,0:T(8,128)S(1)}, f32[8,128]{1,0:T(8,128)S(1)}, u32[]{:S(2)}, u32[]{:S(2)}) collective-permute-start(f32[8,128]{1,0:T(8,128)S(1)} %get-tuple-element.13), channel_id=1, source_target_pairs={{0,1},{2,3},{4,5},{6,7},{8,9},{10,11},{12,13},{14,15},{1,0},{3,2},... | collective-permute-start | bytes 12296 | tf_op jit(solution)/shard_map/ppermute | solution.py:359
  21.2 0.0 collective-permute-done.2.far_ref
  21.2 1.1 %collective-permute-done.3.near_ref = f32[8,128]{1,0:T(8,128)S(1)} collective-permute-done((f32[8,128]{1,0:T(8,128)S(1)}, f32[8,128]{1,0:T(8,128)S(1)}, u32[]{:S(2)}, u32[]{:S(2)}) %collective-permute-start.3) | collective-permute-done | bytes 4128 | tf_op jit(solution)/shard_map/ppermute | solution.py:359
  22.3 1.3 %operators.1 = (f32[27,2,4,64]{3,2,1,0:T(4,128)}, f32[27,1,2,32]{3,2,1,0:T(2,128)}) custom-call(f32[24,8,128]{2,1,0:T(8,128)S(1)} %get-tuple-element.11.rows_ref, f32[8,128]{1,0:T(8,128)S(1)} %collective-permute-done.2.far_ref, f32[8,128]{1,0:T(8,128)S(1)} %collective-permute-done.3.near_ref), custom_call_target="tpu_custom_call" | custom-call | tf_op jit(solution)/shard_map/operators/pallas_call | solution.py:388
  (1 shorter events, 0.0 us)
Async XLA Ops:
  1.4 0.8 %copy-start = (s32[3,4,8,128]{3,2,1,0:T(8,128)S(1)}, s32[3,4,8,128]{3,2,1,0:T(8,128)}, u32[]{:S(2)}) copy-start(s32[3,4,8,128]{3,2,1,0:T(8,128)} %face_ref.1) | copy-start | bytes 147460
  2.2 7.1 %collective-permute-start = (f32[12,4,128]{2,1,0:T(4,128)S(1)}, f32[12,4,128]{2,1,0:T(4,128)S(1)}, u32[]{:S(2)}, u32[]{:S(2)}) collective-permute-start(f32[12,4,128]{2,1,0:T(4,128)S(1)} %get-tuple-element.9), channel_id=1, source_target_pairs={{16,32},{48,64},{80,96},{112,128},{144,160},{176,192},{208,224},{2... | collective-permute-start | bytes 73736 | tf_op jit(solution)/shard_map/ppermute | solution.py:359
  7.4 4.6 %collective-permute-start.1 = (f32[12,4,128]{2,1,0:T(4,128)S(1)}, f32[12,4,128]{2,1,0:T(4,128)S(1)}, u32[]{:S(2)}, u32[]{:S(2)}) collective-permute-start(f32[12,4,128]{2,1,0:T(4,128)S(1)} %get-tuple-element.10), channel_id=1, source_target_pairs={{0,16},{32,48},{64,80},{96,112},{128,144},{160,176},{192,208},{224... | collective-permute-start | bytes 73736 | tf_op jit(solution)/shard_map/ppermute | solution.py:359
  12.1 9.1 %collective-permute-start.2 = (f32[8,128]{1,0:T(8,128)S(1)}, f32[8,128]{1,0:T(8,128)S(1)}, u32[]{:S(2)}, u32[]{:S(2)}) collective-permute-start(f32[8,128]{1,0:T(8,128)S(1)} %get-tuple-element.12), channel_id=1, source_target_pairs={{1,2},{3,4},{5,6},{7,8},{9,10},{11,12},{13,14},{2,1},{4,3},{6,5},{... | collective-permute-start | bytes 12296 | tf_op jit(solution)/shard_map/ppermute | solution.py:359
  19.3 3.1 %collective-permute-start.3 = (f32[8,128]{1,0:T(8,128)S(1)}, f32[8,128]{1,0:T(8,128)S(1)}, u32[]{:S(2)}, u32[]{:S(2)}) collective-permute-start(f32[8,128]{1,0:T(8,128)S(1)} %get-tuple-element.13), channel_id=1, source_target_pairs={{0,1},{2,3},{4,5},{6,7},{8,9},{10,11},{12,13},{14,15},{1,0},{3,2},... | collective-permute-start | bytes 12296 | tf_op jit(solution)/shard_map/ppermute | solution.py:359
where the time goes:
time: 23.9 us; the launch traced here: 23.6 us
  starting transfers between devices  16.2 us (68%)
  waiting for transfers between devices  3.76 us (16%)
  Pallas kernels  1.39 us (6%)
  local copies, waits for them, and re-layouts  0.79 us (3%)
  other arithmetic  0.73 us (3%)
  between operations  0.7 us (3%)
    ppermute x4, starting transfers between devices, swapped(): return lax.ppermute(values, axis, pairs + [(b, a) for a, b in pairs])  16.2 us
    ppermute x4, waiting for transfers between devices, swapped(): return lax.ppermute(values, axis, pairs + [(b, a) for a, b in pairs])  3.76 us
    pallas_call x1, Pallas kernels, body(): pl.pallas_call(operator_kernel, out_shape=(jax.ShapeDtypeStruct((27, 2, 4...  1.26 us
    unnamed x2, local copies, waits for them, and re-layouts  0.79 us
    add x1, other arithmetic, permittivity(): values + jnp.where(material == material_id, permit_levels[material_id], 0.0)  0.73 us
  transfers between devices with their start and end apart: 4, of which 2 were waited for; matrix products, arithmetic and copies ran while one was open for 0% of the time, Pallas kernels for 0%

commit v1 on v0

--- a/solution.py
+++ b/solution.py
@@ -278,10 +278,11 @@
     return results
 
 
-def couplings_kernel(eps_ref, face_ref, own_ref, far_ref, near_ref):
+def couplings_kernel(inputs_ref, own_ref, far_ref, near_ref):
     odd_x = lax.axis_index("gx") % 2 == 1
+    eps = [permittivity(inputs_ref[0, z] & 3) for z in range(4)]
     for r in range(12):
-        values = face_ref[r // 4, r % 4].astype(jnp.float32) / 64.0 * eps_ref[r % 4]
+        values = (inputs_ref[r // 4, r % 4] >> 2).astype(jnp.float32) / 64.0 * eps[r % 4]
         own_ref[r] = values
         far_ref[r] = jnp.where(odd_x, values[4:8, :], values[0:4, :])
         near_ref[r] = jnp.where(odd_x, values[0:4, :], values[4:8, :])
@@ -367,11 +368,11 @@
     own, far, near = pl.pallas_call(
         couplings_kernel,
         out_shape=(jax.ShapeDtypeStruct((12, ROWS, LANES), jnp.float32), edge, edge),
-        in_specs=[whole] * 2,
+        in_specs=[whole],
         out_specs=(whole,) * 3,
         compiler_params=small,
         name="couplings",
-    )(permittivity(material), face_open)
+    )(face_open * 4 + material[None])
     far_rows = swapped(far, "gx", 1)
     near_rows = swapped(near, "gx", 0)
     rows, far, near = pl.pallas_call(

time: 23.9 us -> 23.1 us (0.967)
  local copies, waits for them, and re-layouts: 0.79 us -> 0 us
    unnamed x2 -> x0, local copies, waits for them, and re-layouts: 0.79 us -> none
where the time goes in v1:
time: 23.1 us; the launch traced here: 22.9 us
  starting transfers between devices  16.2 us (70%)
  waiting for transfers between devices  3.76 us (16%)
  Pallas kernels  1.39 us (6%)
  other arithmetic  0.81 us (4%)
  between operations  0.69 us (3%)
    ppermute x4, starting transfers between devices, swapped(): return lax.ppermute(values, axis, pairs + [(b, a) for a, b in pairs])  16.2 us
    ppermute x4, waiting for transfers between devices, swapped(): return lax.ppermute(values, axis, pairs + [(b, a) for a, b in pairs])  3.76 us
    pallas_call x1, Pallas kernels, body(): pl.pallas_call(operator_kernel, out_shape=(jax.ShapeDtypeStruct((27, 2, 4...  1.26 us
    add x1, other arithmetic, body(): face_open * 4 + material[None]  0.81 us
  transfers between devices with their start and end apart: 4, of which 2 were waited for; matrix products, arithmetic and copies ran while one was open for 0% of the time, Pallas kernels for 0%

profile of v1, /device:TPU:249, one launch (start us, length us, event | category | flops | bytes accessed | tf_op | source)
XLA Modules:
  0.0 22.9 jit_solution(8950171731503770205)
XLA Ops:
  0.6 0.8 %multiply_add_fusion.inputs_ref = s32[3,4,8,128]{3,2,1,0:T(8,128)S(1)} fusion(s32[3,4,8,128]{3,2,1,0:T(8,128)} %param.3, s32[4,8,128]{2,1,0:T(8,128)} %param.2), kind=kLoop, calls=%fused_computation | loop fusion | flops 24576 | bytes 114688 | tf_op jit(solution)/shard_map/add | solution.py:375
  1.5 5.2 %collective-permute-start = (f32[12,4,128]{2,1,0:T(4,128)S(1)}, f32[12,4,128]{2,1,0:T(4,128)S(1)}, u32[]{:S(2)}, u32[]{:S(2)}) collective-permute-start(f32[12,4,128]{2,1,0:T(4,128)S(1)} %get-tuple-element.9), channel_id=1, source_target_pairs={{16,32},{48,64},{80,96},{112,128},{144,160},{176,192},{208,224},{2... | collective-permute-start | bytes 73736 | tf_op jit(solution)/shard_map/ppermute | solution.py:360
  6.6 1.9 %collective-permute-start.1 = (f32[12,4,128]{2,1,0:T(4,128)S(1)}, f32[12,4,128]{2,1,0:T(4,128)S(1)}, u32[]{:S(2)}, u32[]{:S(2)}) collective-permute-start(f32[12,4,128]{2,1,0:T(4,128)S(1)} %get-tuple-element.10), channel_id=1, source_target_pairs={{0,16},{32,48},{64,80},{96,112},{128,144},{160,176},{192,208},{224... | collective-permute-start | bytes 73736 | tf_op jit(solution)/shard_map/ppermute | solution.py:360
  8.6 0.0 collective-permute-done.far_rows_ref
  8.6 2.6 %collective-permute-done.1.near_rows_ref = f32[12,4,128]{2,1,0:T(4,128)S(1)} collective-permute-done((f32[12,4,128]{2,1,0:T(4,128)S(1)}, f32[12,4,128]{2,1,0:T(4,128)S(1)}, u32[]{:S(2)}, u32[]{:S(2)}) %collective-permute-start.1) | collective-permute-done | bytes 24608 | tf_op jit(solution)/shard_map/ppermute | solution.py:360
  11.2 0.1 gather_rows.1
  11.3 7.2 %collective-permute-start.2 = (f32[8,128]{1,0:T(8,128)S(1)}, f32[8,128]{1,0:T(8,128)S(1)}, u32[]{:S(2)}, u32[]{:S(2)}) collective-permute-start(f32[8,128]{1,0:T(8,128)S(1)} %get-tuple-element.12), channel_id=1, source_target_pairs={{1,2},{3,4},{5,6},{7,8},{9,10},{11,12},{13,14},{2,1},{4,3},{6,5},{... | collective-permute-start | bytes 12296 | tf_op jit(solution)/shard_map/ppermute | solution.py:360
  18.5 1.9 %collective-permute-start.3 = (f32[8,128]{1,0:T(8,128)S(1)}, f32[8,128]{1,0:T(8,128)S(1)}, u32[]{:S(2)}, u32[]{:S(2)}) collective-permute-start(f32[8,128]{1,0:T(8,128)S(1)} %get-tuple-element.13), channel_id=1, source_target_pairs={{0,1},{2,3},{4,5},{6,7},{8,9},{10,11},{12,13},{14,15},{1,0},{3,2},... | collective-permute-start | bytes 12296 | tf_op jit(solution)/shard_map/ppermute | solution.py:360
  20.5 0.0 collective-permute-done.2.far_ref
  20.5 1.1 %collective-permute-done.3.near_ref = f32[8,128]{1,0:T(8,128)S(1)} collective-permute-done((f32[8,128]{1,0:T(8,128)S(1)}, f32[8,128]{1,0:T(8,128)S(1)}, u32[]{:S(2)}, u32[]{:S(2)}) %collective-permute-start.3) | collective-permute-done | bytes 4128 | tf_op jit(solution)/shard_map/ppermute | solution.py:360
  21.6 1.3 %operators.1 = (f32[27,2,4,64]{3,2,1,0:T(4,128)}, f32[27,1,2,32]{3,2,1,0:T(2,128)}) custom-call(f32[24,8,128]{2,1,0:T(8,128)S(1)} %get-tuple-element.11.rows_ref, f32[8,128]{1,0:T(8,128)S(1)} %collective-permute-done.2.far_ref, f32[8,128]{1,0:T(8,128)S(1)} %collective-permute-done.3.near_ref), custom_call_target="tpu_custom_call" | custom-call | tf_op jit(solution)/shard_map/operators/pallas_call | solution.py:389
  (1 shorter events, 0.0 us)
Async XLA Ops:
  1.5 7.1 %collective-permute-start = (f32[12,4,128]{2,1,0:T(4,128)S(1)}, f32[12,4,128]{2,1,0:T(4,128)S(1)}, u32[]{:S(2)}, u32[]{:S(2)}) collective-permute-start(f32[12,4,128]{2,1,0:T(4,128)S(1)} %get-tuple-element.9), channel_id=1, source_target_pairs={{16,32},{48,64},{80,96},{112,128},{144,160},{176,192},{208,224},{2... | collective-permute-start | bytes 73736 | tf_op jit(solution)/shard_map/ppermute | solution.py:360
  6.6 4.6 %collective-permute-start.1 = (f32[12,4,128]{2,1,0:T(4,128)S(1)}, f32[12,4,128]{2,1,0:T(4,128)S(1)}, u32[]{:S(2)}, u32[]{:S(2)}) collective-permute-start(f32[12,4,128]{2,1,0:T(4,128)S(1)} %get-tuple-element.10), channel_id=1, source_target_pairs={{0,16},{32,48},{64,80},{96,112},{128,144},{160,176},{192,208},{224... | collective-permute-start | bytes 73736 | tf_op jit(solution)/shard_map/ppermute | solution.py:360
  11.3 9.1 %collective-permute-start.2 = (f32[8,128]{1,0:T(8,128)S(1)}, f32[8,128]{1,0:T(8,128)S(1)}, u32[]{:S(2)}, u32[]{:S(2)}) collective-permute-start(f32[8,128]{1,0:T(8,128)S(1)} %get-tuple-element.12), channel_id=1, source_target_pairs={{1,2},{3,4},{5,6},{7,8},{9,10},{11,12},{13,14},{2,1},{4,3},{6,5},{... | collective-permute-start | bytes 12296 | tf_op jit(solution)/shard_map/ppermute | solution.py:360
  18.5 3.1 %collective-permute-start.3 = (f32[8,128]{1,0:T(8,128)S(1)}, f32[8,128]{1,0:T(8,128)S(1)}, u32[]{:S(2)}, u32[]{:S(2)}) collective-permute-start(f32[8,128]{1,0:T(8,128)S(1)} %get-tuple-element.13), channel_id=1, source_target_pairs={{0,1},{2,3},{4,5},{6,7},{8,9},{10,11},{12,13},{14,15},{1,0},{3,2},... | collective-permute-start | bytes 12296 | tf_op jit(solution)/shard_map/ppermute | solution.py:360

commit v2 on v1

--- a/solution.py
+++ b/solution.py
@@ -279,62 +279,66 @@
 
 
 def couplings_kernel(inputs_ref, own_ref, far_ref, near_ref):
-    odd_x = lax.axis_index("gx") % 2 == 1
+    odd_y = lax.axis_index("gy") % 2 == 1
+    lanes = lax.broadcasted_iota(jnp.int32, (ROWS, LANES), 1)
+    low = jnp.zeros((ROWS, LANES), jnp.float32)
+    high = jnp.zeros((ROWS, LANES), jnp.float32)
     eps = [permittivity(inputs_ref[0, z] & 3) for z in range(4)]
     for r in range(12):
         values = (inputs_ref[r // 4, r % 4] >> 2).astype(jnp.float32) / 64.0 * eps[r % 4]
         own_ref[r] = values
+        turned = pltpu.roll(values, 4 * r + 4, 1)
+        low = jnp.where((lanes >= 4 * r) & (lanes < 4 * r + 4), turned, low)
+        high = jnp.where(lanes == 4 * r + 4, turned, high)
+    far_ref[...] = jnp.where(odd_y, low, high)
+    near_ref[...] = jnp.where(odd_y, high, low)
+
+
+def beside(far_ref, near_ref):
+    odd_y = lax.axis_index("gy") % 2 == 1
+    far, near = far_ref[...], near_ref[...]
+    return jnp.where(odd_y, near, far), jnp.where(odd_y, far, near)
+
+
+def edges_kernel(own_ref, far_columns_ref, near_columns_ref, far_ref, near_ref):
+    odd_x = lax.axis_index("gx") % 2 == 1
+    tiles = [own_ref[r] for r in range(12)] + list(beside(far_columns_ref, near_columns_ref))
+    for r, values in enumerate(tiles):
         far_ref[r] = jnp.where(odd_x, values[4:8, :], values[0:4, :])
         near_ref[r] = jnp.where(odd_x, values[0:4, :], values[4:8, :])
 
 
-def gather_kernel(own_ref, far_rows_ref, near_rows_ref, rows_ref, far_ref, near_ref, block):
-    odd_x = lax.axis_index("gx") % 2 == 1
-    odd_y = lax.axis_index("gy") % 2 == 1
-    lanes = lax.broadcasted_iota(jnp.int32, (ROWS, LANES), 1)
-    low = jnp.zeros((ROWS, LANES), jnp.float32)
-    high = jnp.zeros((ROWS, LANES), jnp.float32)
-    for r in range(12):
-        block[r, 0:8, :] = own_ref[r]
-        block[r, 8:12, :] = jnp.where(odd_x, far_rows_ref[r], near_rows_ref[r])
-        block[r, 12:16, :] = jnp.where(odd_x, near_rows_ref[r], far_rows_ref[r])
-        for px in range(2):
-            k = 2 * r + px
-            values = block[r, pl.ds(px, 8, stride=2), :]
-            rows_ref[k] = values
-            turned = pltpu.roll(values, (4 * k + 4) % LANES, 1)
-            low = jnp.where((lanes >= 4 * k) & (lanes < 4 * k + 4), turned, low)
-            high = jnp.where(lanes == 4 * k + 4, turned, high)
-    far_ref[...] = jnp.where(odd_y, low, high)
-    near_ref[...] = jnp.where(odd_y, high, low)
-
-
-def operator_kernel(rows_ref, far_ref, near_ref, first_ref, second_ref):
+def operator_kernel(own_ref, far_columns_ref, near_columns_ref, far_ref, near_ref, first_ref, second_ref, block):
     rows = lax.broadcasted_iota(jnp.int32, (ROWS, LANES), 0)
     lanes = lax.broadcasted_iota(jnp.int32, (ROWS, LANES), 1)
+    odd_x = lax.axis_index("gx") % 2 == 1
     last_x = lax.axis_index("gx") == lax.axis_size("gx") - 1
     last_y = lax.axis_index("gy") == lax.axis_size("gy") - 1
 
-    odd_y = lax.axis_index("gy") % 2 == 1
-    left = jnp.where(odd_y, near_ref[...], far_ref[...])
-    right = jnp.where(odd_y, far_ref[...], near_ref[...])
+    tiles = [own_ref[r] for r in range(12)] + list(beside(far_columns_ref, near_columns_ref))
+    for r, values in enumerate(tiles):
+        block[r, 0:8, :] = values
+        block[r, 8:12, :] = jnp.where(odd_x, far_ref[r], near_ref[r])
+        block[r, 12:16, :] = jnp.where(odd_x, near_ref[r], far_ref[r])
+
     source = ((lanes + 2) % LANES // 2 * 4 + 2 * (lanes % 2)) % LANES
-    above = pick_lanes(right, (2 * lanes + 4) % LANES)
-    edge_even = jnp.where((lanes >= 64) & (lanes < 112), above, pick_lanes(left, source))
-    edge_odd = pick_lanes(left, (source + 1) % LANES)
     at_even = (lanes >= 126) | (lanes == 64)
     at_odd = lanes >= 126
     even_lanes = (2 * lanes) % LANES
     odd_lanes = (2 * lanes + 1) % LANES
 
     c = [[[[None, None], [None, None]] for _ in range(4)] for _ in range(3)]
-    for d in range(3):
-        for z in range(4):
-            for px in range(2):
-                k = (d * 4 + z) * 2 + px
-                values = rows_ref[k]
-                c[d][z][px][0] = jnp.where(at_even, shifted(edge_even, 0, 2 * k), pick_lanes(values, even_lanes))
-                c[d][z][px][1] = jnp.where(at_odd, shifted(edge_odd, 0, 2 * k), pick_lanes(values, odd_lanes))
+    for px in range(2):
+        left = block[12, pl.ds(px, 8, stride=2), :]
+        right = block[13, pl.ds(px, 8, stride=2), :]
+        above = pick_lanes(right, (2 * lanes + 4) % LANES)
+        edge_even = jnp.where((lanes >= 64) & (lanes < 112), above, pick_lanes(left, source))
+        edge_odd = pick_lanes(left, (source + 1) % LANES)
+        for r in range(12):
+            values = block[r, pl.ds(px, 8, stride=2), :]
+            planes = c[r // 4][r % 4][px]
+            planes[0] = jnp.where(at_even, shifted(edge_even, 0, 2 * r), pick_lanes(values, even_lanes))
+            planes[1] = jnp.where(at_odd, shifted(edge_odd, 0, 2 * r), pick_lanes(values, odd_lanes))
 
     operator, chain = first_operator(c, last_x, last_y, rows, lanes)
     empty = jnp.zeros((ROWS, LANES), jnp.float32)
@@ -363,40 +367,40 @@
 def body(material, face_open):
     whole = pl.BlockSpec(memory_space=pltpu.VMEM)
     page = jax.ShapeDtypeStruct((ROWS, LANES), jnp.float32)
-    edge = jax.ShapeDtypeStruct((12, 4, LANES), jnp.float32)
+    edge = jax.ShapeDtypeStruct((14, 4, LANES), jnp.float32)
     small = pltpu.CompilerParams(vmem_limit_bytes=1 << 20)
     own, far, near = pl.pallas_call(
         couplings_kernel,
-        out_shape=(jax.ShapeDtypeStruct((12, ROWS, LANES), jnp.float32), edge, edge),
+        out_shape=(jax.ShapeDtypeStruct((12, ROWS, LANES), jnp.float32), page, page),
         in_specs=[whole],
         out_specs=(whole,) * 3,
         compiler_params=small,
         name="couplings",
     )(face_open * 4 + material[None])
+    far_columns = swapped(far, "gy", 1)
+    near_columns = swapped(near, "gy", 0)
+    far, near = pl.pallas_call(
+        edges_kernel,
+        out_shape=(edge, edge),
+        in_specs=[whole] * 3,
+        out_specs=(whole,) * 2,
+        compiler_params=small,
+        name="edges",
+    )(own, far_columns, near_columns)
     far_rows = swapped(far, "gx", 1)
     near_rows = swapped(near, "gx", 0)
-    rows, far, near = pl.pallas_call(
-        gather_kernel,
-        out_shape=(jax.ShapeDtypeStruct((24, ROWS, LANES), jnp.float32), page, page),
-        in_specs=[whole] * 3,
-        out_specs=(whole,) * 3,
-        scratch_shapes=[pltpu.VMEM((12, 16, LANES), jnp.float32)],
-        compiler_params=small,
-        name="gather_rows",
-    )(own, far_rows, near_rows)
-    far_columns = swapped(far, "gy", 1)
-    near_columns = swapped(near, "gy", 0)
     return pl.pallas_call(
         operator_kernel,
         out_shape=(
             jax.ShapeDtypeStruct((27, 2, 4, 64), jnp.float32),
             jax.ShapeDtypeStruct((27, 1, 2, 32), jnp.float32),
         ),
-        in_specs=[whole] * 3,
+        in_specs=[whole] * 5,
         out_specs=(whole,) * 2,
+        scratch_shapes=[pltpu.VMEM((14, 16, LANES), jnp.float32)],
         compiler_params=pltpu.CompilerParams(vmem_limit_bytes=2 << 20),
         name="operators",
-    )(rows, far_columns, near_columns)
+    )(own, far_columns, near_columns, far_rows, near_rows)
 
 
 def solution(mesh):

time: 23.1 us -> 22.6 us (0.978)
  the two profiles are of different devices: /device:TPU:249 before, /device:TPU:248 now
where the time goes in v2:
time: 22.6 us; the launch traced here: 22.4 us
  starting transfers between devices  14.9 us (66%)
  waiting for transfers between devices  4.63 us (20%)
  Pallas kernels  1.35 us (6%)
  other arithmetic  0.81 us (4%)
  between operations  0.68 us (3%)
    ppermute x4, starting transfers between devices, swapped(): return lax.ppermute(values, axis, pairs + [(b, a) for a, b in pairs])  14.9 us
    ppermute x4, waiting for transfers between devices, swapped(): return lax.ppermute(values, axis, pairs + [(b, a) for a, b in pairs])  4.63 us
    pallas_call x1, Pallas kernels, body(): pl.pallas_call(operator_kernel, out_shape=(jax.ShapeDtypeStruct((27, 2, 4...  1.25 us
    add x1, other arithmetic, body(): face_open * 4 + material[None]  0.81 us
  transfers between devices with their start and end apart: 4, of which 3 were waited for; matrix products, arithmetic and copies ran while one was open for 0% of the time, Pallas kernels for 0%

profile of v2, /device:TPU:248, one launch (start us, length us, event | category | flops | bytes accessed | tf_op | source)
XLA Modules:
  0.0 22.4 jit_solution(7286993246026174706)
XLA Ops:
  0.6 0.8 %multiply_add_fusion.inputs_ref = s32[3,4,8,128]{3,2,1,0:T(8,128)S(1)} fusion(s32[3,4,8,128]{3,2,1,0:T(8,128)} %param.3, s32[4,8,128]{2,1,0:T(8,128)} %param.2), kind=kLoop, calls=%fused_computation | loop fusion | flops 24576 | bytes 114688 | tf_op jit(solution)/shard_map/add | solution.py:379
  1.4 0.1 couplings.1
  1.5 1.9 %collective-permute-start = (f32[8,128]{1,0:T(8,128)S(1)}, f32[8,128]{1,0:T(8,128)S(1)}, u32[]{:S(2)}, u32[]{:S(2)}) collective-permute-start(f32[8,128]{1,0:T(8,128)S(1)} %get-tuple-element.8), channel_id=1, source_target_pairs={{1,2},{3,4},{5,6},{7,8},{9,10},{11,12},{13,14},{2,1},{4,3},{6,5},{... | collective-permute-start | bytes 12296 | tf_op jit(solution)/shard_map/ppermute | solution.py:364
  3.5 5.6 %collective-permute-start.1 = (f32[8,128]{1,0:T(8,128)S(1)}, f32[8,128]{1,0:T(8,128)S(1)}, u32[]{:S(2)}, u32[]{:S(2)}) collective-permute-start(f32[8,128]{1,0:T(8,128)S(1)} %get-tuple-element.9), channel_id=1, source_target_pairs={{0,1},{2,3},{4,5},{6,7},{8,9},{10,11},{12,13},{14,15},{1,0},{3,2},... | collective-permute-start | bytes 12296 | tf_op jit(solution)/shard_map/ppermute | solution.py:364
  9.1 0.0 collective-permute-done.far_columns_ref
  9.1 0.8 %collective-permute-done.1.near_columns_ref = f32[8,128]{1,0:T(8,128)S(1)} collective-permute-done((f32[8,128]{1,0:T(8,128)S(1)}, f32[8,128]{1,0:T(8,128)S(1)}, u32[]{:S(2)}, u32[]{:S(2)}) %collective-permute-start.1) | collective-permute-done | bytes 4128 | tf_op jit(solution)/shard_map/ppermute | solution.py:364
  9.9 5.5 %collective-permute-start.2 = (f32[14,4,128]{2,1,0:T(4,128)S(1)}, f32[14,4,128]{2,1,0:T(4,128)S(1)}, u32[]{:S(2)}, u32[]{:S(2)}) collective-permute-start(f32[14,4,128]{2,1,0:T(4,128)S(1)} %get-tuple-element.10), channel_id=1, source_target_pairs={{16,32},{48,64},{80,96},{112,128},{144,160},{176,192},{208,224},{2... | collective-permute-start | bytes 86024 | tf_op jit(solution)/shard_map/ppermute | solution.py:364
  15.3 1.9 %collective-permute-start.3 = (f32[14,4,128]{2,1,0:T(4,128)S(1)}, f32[14,4,128]{2,1,0:T(4,128)S(1)}, u32[]{:S(2)}, u32[]{:S(2)}) collective-permute-start(f32[14,4,128]{2,1,0:T(4,128)S(1)} %get-tuple-element.11), channel_id=1, source_target_pairs={{0,16},{32,48},{64,80},{96,112},{128,144},{160,176},{192,208},{224... | collective-permute-start | bytes 86024 | tf_op jit(solution)/shard_map/ppermute | solution.py:364
  17.3 0.5 %collective-permute-done.2.far_ref = f32[14,4,128]{2,1,0:T(4,128)S(1)} collective-permute-done((f32[14,4,128]{2,1,0:T(4,128)S(1)}, f32[14,4,128]{2,1,0:T(4,128)S(1)}, u32[]{:S(2)}, u32[]{:S(2)}) %collective-permute-start.2) | collective-permute-done | bytes 28704 | tf_op jit(solution)/shard_map/ppermute | solution.py:364
  17.8 3.3 %collective-permute-done.3.near_ref = f32[14,4,128]{2,1,0:T(4,128)S(1)} collective-permute-done((f32[14,4,128]{2,1,0:T(4,128)S(1)}, f32[14,4,128]{2,1,0:T(4,128)S(1)}, u32[]{:S(2)}, u32[]{:S(2)}) %collective-permute-start.3) | collective-permute-done | bytes 28704 | tf_op jit(solution)/shard_map/ppermute | solution.py:364
  21.1 1.2 %operators.1 = (f32[27,2,4,64]{3,2,1,0:T(4,128)}, f32[27,1,2,32]{3,2,1,0:T(2,128)}) custom-call(f32[12,8,128]{2,1,0:T(8,128)S(1)} %get-tuple-element.7.own_ref, f32[8,128]{1,0:T(8,128)S(1)} %collective-permute-done.far_columns_ref, f32[8,128]{1,0:T(8,128)S(1)} %collective-permute-done.1.near_columns_ref, f32[14,4,128]{2,1,0:T(4,128)S(1)} %collective-permute-done.2.far_ref, ...), custom_call_target="tpu_custom_call" | custom-call | tf_op jit(solution)/shard_map/operators/pallas_call | solution.py:392
  (1 shorter events, 0.0 us)
Async XLA Ops:
  1.5 7.5 %collective-permute-start = (f32[8,128]{1,0:T(8,128)S(1)}, f32[8,128]{1,0:T(8,128)S(1)}, u32[]{:S(2)}, u32[]{:S(2)}) collective-permute-start(f32[8,128]{1,0:T(8,128)S(1)} %get-tuple-element.8), channel_id=1, source_target_pairs={{1,2},{3,4},{5,6},{7,8},{9,10},{11,12},{13,14},{2,1},{4,3},{6,5},{... | collective-permute-start | bytes 12296 | tf_op jit(solution)/shard_map/ppermute | solution.py:364
  3.5 6.4 %collective-permute-start.1 = (f32[8,128]{1,0:T(8,128)S(1)}, f32[8,128]{1,0:T(8,128)S(1)}, u32[]{:S(2)}, u32[]{:S(2)}) collective-permute-start(f32[8,128]{1,0:T(8,128)S(1)} %get-tuple-element.9), channel_id=1, source_target_pairs={{0,1},{2,3},{4,5},{6,7},{8,9},{10,11},{12,13},{14,15},{1,0},{3,2},... | collective-permute-start | bytes 12296 | tf_op jit(solution)/shard_map/ppermute | solution.py:364
  9.9 7.9 %collective-permute-start.2 = (f32[14,4,128]{2,1,0:T(4,128)S(1)}, f32[14,4,128]{2,1,0:T(4,128)S(1)}, u32[]{:S(2)}, u32[]{:S(2)}) collective-permute-start(f32[14,4,128]{2,1,0:T(4,128)S(1)} %get-tuple-element.10), channel_id=1, source_target_pairs={{16,32},{48,64},{80,96},{112,128},{144,160},{176,192},{208,224},{2... | collective-permute-start | bytes 86024 | tf_op jit(solution)/shard_map/ppermute | solution.py:364
  15.3 5.8 %collective-permute-start.3 = (f32[14,4,128]{2,1,0:T(4,128)S(1)}, f32[14,4,128]{2,1,0:T(4,128)S(1)}, u32[]{:S(2)}, u32[]{:S(2)}) collective-permute-start(f32[14,4,128]{2,1,0:T(4,128)S(1)} %get-tuple-element.11), channel_id=1, source_target_pairs={{0,16},{32,48},{64,80},{96,112},{128,144},{160,176},{192,208},{224... | collective-permute-start | bytes 86024 | tf_op jit(solution)/shard_map/ppermute | solution.py:364

commit v3 on v2

--- a/solution.py
+++ b/solution.py
@@ -278,7 +278,7 @@
     return results
 
 
-def couplings_kernel(inputs_ref, own_ref, far_ref, near_ref):
+def couplings_kernel(inputs_ref, own_ref, near_ref, far_ref):
     odd_y = lax.axis_index("gy") % 2 == 1
     lanes = lax.broadcasted_iota(jnp.int32, (ROWS, LANES), 1)
     low = jnp.zeros((ROWS, LANES), jnp.float32)
@@ -294,28 +294,28 @@
     near_ref[...] = jnp.where(odd_y, high, low)
 
 
-def beside(far_ref, near_ref):
+def beside(near_ref, far_ref):
     odd_y = lax.axis_index("gy") % 2 == 1
     far, near = far_ref[...], near_ref[...]
     return jnp.where(odd_y, near, far), jnp.where(odd_y, far, near)
 
 
-def edges_kernel(own_ref, far_columns_ref, near_columns_ref, far_ref, near_ref):
+def edges_kernel(own_ref, near_columns_ref, far_columns_ref, far_ref, near_ref):
     odd_x = lax.axis_index("gx") % 2 == 1
-    tiles = [own_ref[r] for r in range(12)] + list(beside(far_columns_ref, near_columns_ref))
+    tiles = [own_ref[r] for r in range(12)] + list(beside(near_columns_ref, far_columns_ref))
     for r, values in enumerate(tiles):
         far_ref[r] = jnp.where(odd_x, values[4:8, :], values[0:4, :])
         near_ref[r] = jnp.where(odd_x, values[0:4, :], values[4:8, :])
 
 
-def operator_kernel(own_ref, far_columns_ref, near_columns_ref, far_ref, near_ref, first_ref, second_ref, block):
+def operator_kernel(own_ref, near_columns_ref, far_columns_ref, far_ref, near_ref, first_ref, second_ref, block):
     rows = lax.broadcasted_iota(jnp.int32, (ROWS, LANES), 0)
     lanes = lax.broadcasted_iota(jnp.int32, (ROWS, LANES), 1)
     odd_x = lax.axis_index("gx") % 2 == 1
     last_x = lax.axis_index("gx") == lax.axis_size("gx") - 1
     last_y = lax.axis_index("gy") == lax.axis_size("gy") - 1
 
-    tiles = [own_ref[r] for r in range(12)] + list(beside(far_columns_ref, near_columns_ref))
+    tiles = [own_ref[r] for r in range(12)] + list(beside(near_columns_ref, far_columns_ref))
     for r, values in enumerate(tiles):
         block[r, 0:8, :] = values
         block[r, 8:12, :] = jnp.where(odd_x, far_ref[r], near_ref[r])
@@ -369,7 +369,7 @@
     page = jax.ShapeDtypeStruct((ROWS, LANES), jnp.float32)
     edge = jax.ShapeDtypeStruct((14, 4, LANES), jnp.float32)
     small = pltpu.CompilerParams(vmem_limit_bytes=1 << 20)
-    own, far, near = pl.pallas_call(
+    own, near, far = pl.pallas_call(
         couplings_kernel,
         out_shape=(jax.ShapeDtypeStruct((12, ROWS, LANES), jnp.float32), page, page),
         in_specs=[whole],
@@ -377,8 +377,8 @@
         compiler_params=small,
         name="couplings",
     )(face_open * 4 + material[None])
+    near_columns = swapped(near, "gy", 0)
     far_columns = swapped(far, "gy", 1)
-    near_columns = swapped(near, "gy", 0)
     far, near = pl.pallas_call(
         edges_kernel,
         out_shape=(edge, edge),
@@ -386,7 +386,7 @@
         out_specs=(whole,) * 2,
         compiler_params=small,
         name="edges",
-    )(own, far_columns, near_columns)
+    )(own, near_columns, far_columns)
     far_rows = swapped(far, "gx", 1)
     near_rows = swapped(near, "gx", 0)
     return pl.pallas_call(
@@ -400,7 +400,7 @@
         scratch_shapes=[pltpu.VMEM((14, 16, LANES), jnp.float32)],
         compiler_params=pltpu.CompilerParams(vmem_limit_bytes=2 << 20),
         name="operators",
-    )(own, far_columns, near_columns, far_rows, near_rows)
+    )(own, near_columns, far_columns, far_rows, near_rows)
 
 
 def solution(mesh):

time: 22.6 us -> 22.3 us (0.987)
  the two profiles are of different devices: /device:TPU:248 before, /device:TPU:312 now
where the time goes in v3:
time: 22.3 us; the launch traced here: 22.1 us
  starting transfers between devices  11.2 us (50%)
  waiting for transfers between devices  8.04 us (36%)
  Pallas kernels  1.35 us (6%)
  other arithmetic  0.81 us (4%)
  between operations  0.68 us (3%)
    ppermute x4, starting transfers between devices, swapped(): return lax.ppermute(values, axis, pairs + [(b, a) for a, b in pairs])  11.2 us
    ppermute x4, waiting for transfers between devices, swapped(): return lax.ppermute(values, axis, pairs + [(b, a) for a, b in pairs])  8.04 us
    pallas_call x1, Pallas kernels, body(): pl.pallas_call(operator_kernel, out_shape=(jax.ShapeDtypeStruct((27, 2, 4...  1.25 us
    add x1, other arithmetic, body(): face_open * 4 + material[None]  0.81 us
  transfers between devices with their start and end apart: 4, of which 3 were waited for; matrix products, arithmetic and copies ran while one was open for 0% of the time, Pallas kernels for 0%

profile of v3, /device:TPU:312, one launch (start us, length us, event | category | flops | bytes accessed | tf_op | source)
XLA Modules:
  0.0 22.1 jit_solution(3265513018334343136)
XLA Ops:
  0.6 0.8 %multiply_add_fusion.inputs_ref = s32[3,4,8,128]{3,2,1,0:T(8,128)S(1)} fusion(s32[3,4,8,128]{3,2,1,0:T(8,128)} %param.3, s32[4,8,128]{2,1,0:T(8,128)} %param.2), kind=kLoop, calls=%fused_computation | loop fusion | flops 24576 | bytes 114688 | tf_op jit(solution)/shard_map/add | solution.py:379
  1.4 0.1 couplings.1
  1.5 1.9 %collective-permute-start = (f32[8,128]{1,0:T(8,128)S(1)}, f32[8,128]{1,0:T(8,128)S(1)}, u32[]{:S(2)}, u32[]{:S(2)}) collective-permute-start(f32[8,128]{1,0:T(8,128)S(1)} %get-tuple-element.8), channel_id=1, source_target_pairs={{0,1},{2,3},{4,5},{6,7},{8,9},{10,11},{12,13},{14,15},{1,0},{3,2},... | collective-permute-start | bytes 12296 | tf_op jit(solution)/shard_map/ppermute | solution.py:364
  3.5 1.9 %collective-permute-start.1 = (f32[8,128]{1,0:T(8,128)S(1)}, f32[8,128]{1,0:T(8,128)S(1)}, u32[]{:S(2)}, u32[]{:S(2)}) collective-permute-start(f32[8,128]{1,0:T(8,128)S(1)} %get-tuple-element.9), channel_id=1, source_target_pairs={{1,2},{3,4},{5,6},{7,8},{9,10},{11,12},{13,14},{2,1},{4,3},{6,5},{... | collective-permute-start | bytes 12296 | tf_op jit(solution)/shard_map/ppermute | solution.py:364
  5.4 0.0 collective-permute-done.near_columns_ref
  5.4 4.2 %collective-permute-done.1.far_columns_ref = f32[8,128]{1,0:T(8,128)S(1)} collective-permute-done((f32[8,128]{1,0:T(8,128)S(1)}, f32[8,128]{1,0:T(8,128)S(1)}, u32[]{:S(2)}, u32[]{:S(2)}) %collective-permute-start.1) | collective-permute-done | bytes 4128 | tf_op jit(solution)/shard_map/ppermute | solution.py:364
  9.6 5.5 %collective-permute-start.2 = (f32[14,4,128]{2,1,0:T(4,128)S(1)}, f32[14,4,128]{2,1,0:T(4,128)S(1)}, u32[]{:S(2)}, u32[]{:S(2)}) collective-permute-start(f32[14,4,128]{2,1,0:T(4,128)S(1)} %get-tuple-element.10), channel_id=1, source_target_pairs={{16,32},{48,64},{80,96},{112,128},{144,160},{176,192},{208,224},{2... | collective-permute-start | bytes 86024 | tf_op jit(solution)/shard_map/ppermute | solution.py:364
  15.1 1.9 %collective-permute-start.3 = (f32[14,4,128]{2,1,0:T(4,128)S(1)}, f32[14,4,128]{2,1,0:T(4,128)S(1)}, u32[]{:S(2)}, u32[]{:S(2)}) collective-permute-start(f32[14,4,128]{2,1,0:T(4,128)S(1)} %get-tuple-element.11), channel_id=1, source_target_pairs={{0,16},{32,48},{64,80},{96,112},{128,144},{160,176},{192,208},{224... | collective-permute-start | bytes 86024 | tf_op jit(solution)/shard_map/ppermute | solution.py:364
  17.0 0.5 %collective-permute-done.2.far_ref = f32[14,4,128]{2,1,0:T(4,128)S(1)} collective-permute-done((f32[14,4,128]{2,1,0:T(4,128)S(1)}, f32[14,4,128]{2,1,0:T(4,128)S(1)}, u32[]{:S(2)}, u32[]{:S(2)}) %collective-permute-start.2) | collective-permute-done | bytes 28704 | tf_op jit(solution)/shard_map/ppermute | solution.py:364
  17.5 3.3 %collective-permute-done.3.near_ref = f32[14,4,128]{2,1,0:T(4,128)S(1)} collective-permute-done((f32[14,4,128]{2,1,0:T(4,128)S(1)}, f32[14,4,128]{2,1,0:T(4,128)S(1)}, u32[]{:S(2)}, u32[]{:S(2)}) %collective-permute-start.3) | collective-permute-done | bytes 28704 | tf_op jit(solution)/shard_map/ppermute | solution.py:364
  20.8 1.2 %operators.1 = (f32[27,2,4,64]{3,2,1,0:T(4,128)}, f32[27,1,2,32]{3,2,1,0:T(2,128)}) custom-call(f32[12,8,128]{2,1,0:T(8,128)S(1)} %get-tuple-element.7.own_ref, f32[8,128]{1,0:T(8,128)S(1)} %collective-permute-done.near_columns_ref, f32[8,128]{1,0:T(8,128)S(1)} %collective-permute-done.1.far_columns_ref, f32[14,4,128]{2,1,0:T(4,128)S(1)} %collective-permute-done.2.far_ref, ...), custom_call_target="tpu_custom_call" | custom-call | tf_op jit(solution)/shard_map/operators/pallas_call | solution.py:392
  (1 shorter events, 0.0 us)
Async XLA Ops:
  1.5 3.9 %collective-permute-start = (f32[8,128]{1,0:T(8,128)S(1)}, f32[8,128]{1,0:T(8,128)S(1)}, u32[]{:S(2)}, u32[]{:S(2)}) collective-permute-start(f32[8,128]{1,0:T(8,128)S(1)} %get-tuple-element.8), channel_id=1, source_target_pairs={{0,1},{2,3},{4,5},{6,7},{8,9},{10,11},{12,13},{14,15},{1,0},{3,2},... | collective-permute-start | bytes 12296 | tf_op jit(solution)/shard_map/ppermute | solution.py:364
  3.5 6.1 %collective-permute-start.1 = (f32[8,128]{1,0:T(8,128)S(1)}, f32[8,128]{1,0:T(8,128)S(1)}, u32[]{:S(2)}, u32[]{:S(2)}) collective-permute-start(f32[8,128]{1,0:T(8,128)S(1)} %get-tuple-element.9), channel_id=1, source_target_pairs={{1,2},{3,4},{5,6},{7,8},{9,10},{11,12},{13,14},{2,1},{4,3},{6,5},{... | collective-permute-start | bytes 12296 | tf_op jit(solution)/shard_map/ppermute | solution.py:364
  9.6 7.9 %collective-permute-start.2 = (f32[14,4,128]{2,1,0:T(4,128)S(1)}, f32[14,4,128]{2,1,0:T(4,128)S(1)}, u32[]{:S(2)}, u32[]{:S(2)}) collective-permute-start(f32[14,4,128]{2,1,0:T(4,128)S(1)} %get-tuple-element.10), channel_id=1, source_target_pairs={{16,32},{48,64},{80,96},{112,128},{144,160},{176,192},{208,224},{2... | collective-permute-start | bytes 86024 | tf_op jit(solution)/shard_map/ppermute | solution.py:364
  15.1 5.8 %collective-permute-start.3 = (f32[14,4,128]{2,1,0:T(4,128)S(1)}, f32[14,4,128]{2,1,0:T(4,128)S(1)}, u32[]{:S(2)}, u32[]{:S(2)}) collective-permute-start(f32[14,4,128]{2,1,0:T(4,128)S(1)} %get-tuple-element.11), channel_id=1, source_target_pairs={{0,16},{32,48},{64,80},{96,112},{128,144},{160,176},{192,208},{224... | collective-permute-start | bytes 86024 | tf_op jit(solution)/shard_map/ppermute | solution.py:364

commit v4 on v3

--- a/solution.py
+++ b/solution.py
@@ -51,7 +51,20 @@
     return f, g, lower * g, lower * f, upper * g
 
 
-def first_operator(c, last_x, last_y, rows, lanes):
+def edge_masks(last_x, last_y, rows, lanes, step):
+    return (rows == ROWS // 2 - step) & last_x, (lanes == LANES // 2 - step) & last_y
+
+
+def dropped(values, offset_x, offset_y, masks):
+    if offset_x == 1:
+        values = jnp.where(masks[0], 0.0, values)
+    if offset_y == 1:
+        values = jnp.where(masks[1], 0.0, values)
+    return values
+
+
+def first_operator(c, masks, hold=None):
+    factors = {}
     lines = {}
     for z in range(4):
         for p in range(2):
@@ -158,22 +171,14 @@
                         s_gamma, k_epsilon = s * gamma[t], k * epsilon[t]
                         for u in corners[i:]:
                             put(zc, raised_corner(t), raised_corner(u), s_gamma * gamma[u] + k_epsilon * epsilon[u])
+                    waiting = hold is not None and d == 1
                     for t in corners:
-                        s_delta, s_alpha = s * delta[t], s * alpha[t]
+                        s_delta, s_beta = s * delta[t], s * beta[t]
+                        if waiting:
+                            factors[zc, q1, q2, t] = s_beta
+                            s_beta = jnp.where(hold, 0.0, s_beta)
                         for u in corners:
-                            put(zc, t, raised_corner(u), s_delta * epsilon[u] - s_alpha * gamma[u])
-
-    drop_x = (rows == ROWS // 2 - 1) & last_x
-    drop_y = (lanes == LANES // 2 - 1) & last_y
-
-    def inside(values, offset):
-        if offset[1] == 1 and offset[2] == 1:
-            return jnp.where(drop_x | drop_y, 0.0, values)
-        if offset[1] == 1:
-            return jnp.where(drop_x, 0.0, values)
-        if offset[2] == 1:
-            return jnp.where(drop_y, 0.0, values)
-        return values
+                            put(zc, t, raised_corner(u), -(s_delta * beta[u] + s_beta * gamma[u]))
 
     operator = {}
     keys = sorted({(offset, z) for offset, z, _, _ in sums})
@@ -189,20 +194,39 @@
                 continue
             part = shifted(part, -ax, 0)
             total = part if total is None else total + part
-        operator[offset, z] = inside(total, offset)
+        operator[offset, z] = dropped(total, *offset[1:], masks)
         if offset != (0, 0, 0):
             mirror = tuple(-o for o in offset)
-            operator[mirror, z + offset[0]] = inside(shifted(total, -offset[1], -offset[2]), mirror)
+            operator[mirror, z + offset[0]] = dropped(shifted(total, -offset[1], -offset[2]), *mirror[1:], masks)
 
     chain = [
         [lines[0, z, 0, 0][2] for z in range(2)],
         [lines[1, 2 * z, 0][2] for z in range(2)],
         [lines[2, 2 * z, 0][2] for z in range(2)],
     ]
-    return operator, chain
-
-
-def second_operator(operator, chain, last_x, last_y, rows, lanes):
+    return operator, chain, factors
+
+
+reaches = ((-1, -1), (0, -1), (0, 0), (0, 1), (1, 0), (1, 1))
+
+
+def taken(offset):
+    return [(m, offset + 1 if m == -1 else offset) for m in (-1, 0, 1) if m * offset != -1]
+
+
+def from_below(j, o):
+    return (j, o) in ((-1, -1), (0, 0), (0, 1))
+
+
+def reaching(j, o, source, odd):
+    if (j, o) == (0, 1):
+        return jnp.where(odd, 0.0, source)
+    if (j, o) == (1, 0):
+        return jnp.where(odd, source, 0.0)
+    return source
+
+
+def second_operator(operator, chain, rows, lanes, hold=None):
     odd = {1: rows % 2 == 1, 2: lanes % 2 == 1}
     depth = line_terms(chain[0][0], chain[0][1])[0]
     down, up = {}, {}
@@ -216,17 +240,13 @@
     down_z = {0: down[1, 0], 1: down[1, 1] * depth}
     up_z = {0: up[1, 0], 1: up[1, 1] * depth}
 
-    reaches = ((-1, -1), (0, -1), (0, 0), (0, 1), (1, 0), (1, 1))
-
     def factors(d, lower, upper):
         base = {}
         for j, o in reaches:
-            source = lower if (j, o) in ((-1, -1), (0, 0), (0, 1)) else upper
-            source = shifted(source, o if d == 1 else 0, o if d == 2 else 0)
-            if (j, o) == (0, 1):
-                source = jnp.where(odd[d], 0.0, source)
-            if (j, o) == (1, 0):
-                source = jnp.where(odd[d], source, 0.0)
+            source = lower if from_below(j, o) else upper
+            source = reaching(j, o, shifted(source, o if d == 1 else 0, o if d == 2 else 0), odd[d])
+            if hold is not None and d == 1 and (j, o) == (1, 1):
+                source = jnp.where(hold, 0.0, source)
             base[j, o] = source
         return {
             (j, o, across): shifted(base[j, o], 0 if d == 1 else across, across if d == 1 else 0)
@@ -253,11 +273,6 @@
     }
     own = {(z, mx, my): times(sides[z, 1][mx], sides[z, 2][my]) for z in range(2) for mx in (-1, 0, 1) for my in (-1, 0, 1)}
 
-    def taken(offset):
-        return [(m, offset + 1 if m == -1 else offset) for m in (-1, 0, 1) if m * offset != -1]
-
-    drop_x = (rows == ROWS // 2 - 2) & last_x
-    drop_y = (lanes == LANES // 2 - 2) & last_y
     results = {}
     for ox in (-1, 0, 1):
         for oy in (-1, 0, 1):
@@ -270,12 +285,8 @@
                     part = term if part is None else part + term
                 part = shifted(part, 0, my)
                 total = part if total is None else total + part
-            if ox == 1:
-                total = jnp.where(drop_x, 0.0, total)
-            if oy == 1:
-                total = jnp.where(drop_y, 0.0, total)
             results[ox, oy] = total
-    return results
+    return results, own
 
 
 def couplings_kernel(inputs_ref, own_ref, near_ref, far_ref):
@@ -308,55 +319,192 @@
         near_ref[r] = jnp.where(odd_x, values[0:4, :], values[4:8, :])
 
 
-def operator_kernel(own_ref, near_columns_ref, far_columns_ref, far_ref, near_ref, first_ref, second_ref, block):
-    rows = lax.broadcasted_iota(jnp.int32, (ROWS, LANES), 0)
-    lanes = lax.broadcasted_iota(jnp.int32, (ROWS, LANES), 1)
-    odd_x = lax.axis_index("gx") % 2 == 1
-    last_x = lax.axis_index("gx") == lax.axis_size("gx") - 1
-    last_y = lax.axis_index("gy") == lax.axis_size("gy") - 1
-
-    tiles = [own_ref[r] for r in range(12)] + list(beside(near_columns_ref, far_columns_ref))
-    for r, values in enumerate(tiles):
-        block[r, 0:8, :] = values
-        block[r, 8:12, :] = jnp.where(odd_x, far_ref[r], near_ref[r])
-        block[r, 12:16, :] = jnp.where(odd_x, near_ref[r], far_ref[r])
-
+def lane_picks(lanes):
     source = ((lanes + 2) % LANES // 2 * 4 + 2 * (lanes % 2)) % LANES
-    at_even = (lanes >= 126) | (lanes == 64)
-    at_odd = lanes >= 126
-    even_lanes = (2 * lanes) % LANES
-    odd_lanes = (2 * lanes + 1) % LANES
-
+    return source, (2 * lanes) % LANES, (lanes >= 126) | (lanes == 64), lanes >= 126
+
+
+def columns_beside(left, right, lanes, source):
+    above = pick_lanes(right, (2 * lanes + 4) % LANES)
+    even = jnp.where((lanes >= 64) & (lanes < 112), above, pick_lanes(left, source))
+    return even, pick_lanes(left, (source + 1) % LANES)
+
+
+def split_lanes(values, r, edges, picks):
+    _, even_lanes, at_even, at_odd = picks
+    even = jnp.where(at_even, shifted(edges[0], 0, 2 * r), pick_lanes(values, even_lanes))
+    odd = jnp.where(at_odd, shifted(edges[1], 0, 2 * r), pick_lanes(values, even_lanes + 1))
+    return even, odd
+
+
+def split_couplings(block, lanes):
+    picks = lane_picks(lanes)
     c = [[[[None, None], [None, None]] for _ in range(4)] for _ in range(3)]
     for px in range(2):
         left = block[12, pl.ds(px, 8, stride=2), :]
         right = block[13, pl.ds(px, 8, stride=2), :]
-        above = pick_lanes(right, (2 * lanes + 4) % LANES)
-        edge_even = jnp.where((lanes >= 64) & (lanes < 112), above, pick_lanes(left, source))
-        edge_odd = pick_lanes(left, (source + 1) % LANES)
+        edges = columns_beside(left, right, lanes, picks[0])
         for r in range(12):
             values = block[r, pl.ds(px, 8, stride=2), :]
-            planes = c[r // 4][r % 4][px]
-            planes[0] = jnp.where(at_even, shifted(edge_even, 0, 2 * r), pick_lanes(values, even_lanes))
-            planes[1] = jnp.where(at_odd, shifted(edge_odd, 0, 2 * r), pick_lanes(values, odd_lanes))
-
-    operator, chain = first_operator(c, last_x, last_y, rows, lanes)
+            c[r // 4][r % 4][px][:] = split_lanes(values, r, edges, picks)
+    return c
+
+
+def places():
+    rows = lax.broadcasted_iota(jnp.int32, (ROWS, LANES), 0)
+    lanes = lax.broadcasted_iota(jnp.int32, (ROWS, LANES), 1)
+    last_x = lax.axis_index("gx") == lax.axis_size("gx") - 1
+    last_y = lax.axis_index("gy") == lax.axis_size("gy") - 1
+    return rows, lanes, last_x, last_y
+
+
+def operators(block, first_ref, second_ref, hold_row=None):
+    rows, lanes, last_x, last_y = places()
+    hold = None if hold_row is None else rows == hold_row
+    c = split_couplings(block, lanes)
+    operator, chain, factors = first_operator(c, edge_masks(last_x, last_y, rows, lanes, 1), hold)
     empty = jnp.zeros((ROWS, LANES), jnp.float32)
     full = {}
     for o in range(27):
         offset = (o // 9 - 1, o // 3 % 3 - 1, o % 3 - 1)
         for z in range(2):
-            values = operator.get((offset, z), empty)
-            full[offset, z] = values
-            first_ref[o, z] = values[0:4, 0:64]
-
-    results = second_operator(full, chain, last_x, last_y, rows, lanes)
+            full[offset, z] = operator.get((offset, z), empty)
+            first_ref[o, z] = full[offset, z][0:4, 0:64]
+    results, own = second_operator(full, chain, rows, lanes, hold)
+    masks = edge_masks(last_x, last_y, rows, lanes, 2)
     second_ref[...] = jnp.zeros(second_ref.shape, jnp.float32)
     for (ox, oy), values in results.items():
-        o = 9 + (ox + 1) * 3 + oy + 1
-        compact = pick_lanes(values, even_lanes)
-        second_ref[o, 0, 0:1, :] = compact[0:1, 0:32]
-        second_ref[o, 0, 1:2, :] = compact[2:3, 0:32]
+        compact = pick_lanes(dropped(values, ox, oy, masks), (2 * lanes) % LANES)
+        second_ref[9 + (ox + 1) * 3 + oy + 1, 0, 0:1, :] = compact[0:1, 0:32]
+        second_ref[9 + (ox + 1) * 3 + oy + 1, 0, 1:2, :] = compact[2:3, 0:32]
+    return operator, factors, results, own
+
+
+fix_entries = [((oz, 1, oy), z) for z in (0, 1) for oz in (-z, 1 - z) for oy in (-1, 0, 1)]
+fix_factors = [
+    (zc, qz, qy, (tz, 0, ty))
+    for zc in (0, 1)
+    for qz in (0, 1)
+    for qy in (0, 1)
+    if qz or qy
+    for tz in range(1 + (qz if zc == 0 else 0))
+    for ty in range(1 + qy)
+]
+fix_sides = [(z, 1, my) for z in (0, 1) for my in (-1, 0, 1)]
+fix_results = [(1, oy) for oy in (-1, 0, 1)]
+fix_count = len(fix_entries) + len(fix_factors) + len(fix_sides) + len(fix_results)
+
+
+def early_kernel(own_ref, near_columns_ref, far_columns_ref, far_ref, first_ref, second_ref, kept_ref, block):
+    tiles = [own_ref[r] for r in range(12)] + list(beside(near_columns_ref, far_columns_ref))
+    for r, values in enumerate(tiles):
+        block[r, 0:8, :] = values
+        block[r, 8:12, :] = jnp.zeros((4, LANES), jnp.float32)
+        block[r, 12:16, :] = far_ref[r]
+    operator, factors, results, own = operators(block, first_ref, second_ref, ROWS // 2 - 1)
+    kept = [operator[e] for e in fix_entries] + [factors[e] for e in fix_factors]
+    kept += [own[e] for e in fix_sides] + [results[e] for e in fix_results]
+    for i, values in enumerate(kept):
+        kept_ref[i] = values
+
+
+def add_row_above(near_ref, early_second_ref, kept_ref, first_ref, second_ref):
+    rows, lanes, last_x, last_y = places()
+    kept = {e: kept_ref[i] for i, e in enumerate(fix_entries + fix_factors + fix_sides + fix_results)}
+
+    def row(r):
+        return jnp.broadcast_to(near_ref[r, 0:1, :], (ROWS, LANES))
+
+    picks = lane_picks(lanes)
+    edges = columns_beside(row(12), row(13), lanes, picks[0])
+    c = {(d, z): split_lanes(row(d * 4 + z), d * 4 + z, edges, picks) for d in (0, 2) for z in range(4)}
+    line_y = {z: line_terms(*c[2, z]) for z in range(4)}
+    line_z = {(zc, py): line_terms(c[0, 2 * zc][py], c[0, 2 * zc + 1][py]) for zc in range(2) for py in range(2)}
+
+    sums = {}
+    for zc, qz, qy, t in fix_factors:
+        pair_z = line_z[zc, qy][:2] if qz else (None,)
+        pair_y = line_y[2 * zc + qz][:2] if qy else (None,)
+        for uz in range(1 + (qz if zc == 0 else 0)):
+            for uy in range(1 + qy):
+                key = ((uz - t[0], 1, uy - t[2]), zc + t[0], t[2])
+                term = kept[zc, qz, qy, t] * times(pair_z[uz], pair_y[uy])
+                sums[key] = sums[key] + term if key in sums else term
+    masks = edge_masks(last_x, last_y, rows, lanes, 1)
+    entries = {}
+    for offset, z in fix_entries:
+        total = kept[offset, z]
+        if (offset, z, 0) in sums:
+            total = total - sums[offset, z, 0]
+        if (offset, z, 1) in sums:
+            total = total - shifted(sums[offset, z, 1], 0, -1)
+        entries[offset, z] = dropped(total, *offset[1:], masks)
+        whole = jnp.where(rows == ROWS // 2 - 1, entries[offset, z], kept[offset, z])
+        first_ref[(offset[0] + 1) * 3 + offset[2] + 1, z] = whole[0:4, 0:64]
+    for offset, z in (((-1, 1), 0), ((1, 1), 1)):
+        for oy in range(3):
+            first_ref[(offset[0] + 1) * 3 + oy, z] = jnp.zeros((4, 64), jnp.float32)
+
+    depth = line_terms(line_z[0, 0][2], line_z[1, 0][2])[0]
+    odd = lanes % 2 == 1
+    spread = {}
+    for far in range(2):
+        here = line_y[2 * far][2]
+        f, g = line_terms(shifted(here, 0, -1), here)[:2]
+        down, up = jnp.where(odd, f, 1.0), jnp.where(odd, g, 1.0)
+        if far == 1:
+            down, up = down * depth, up * depth
+        for jy, oy in reaches:
+            weight = reaching(jy, oy, shifted(down if from_below(jy, oy) else up, 0, oy), odd)
+            for z in range(2):
+                term = entries[(far - z, 1, oy), z] * weight
+                spread[z, jy] = spread[z, jy] + term if (z, jy) in spread else term
+    masks = edge_masks(last_x, last_y, rows, lanes, 2)
+    for oy in (-1, 0, 1):
+        total = None
+        for my, jy in taken(oy):
+            part = shifted(kept[0, 1, my] * spread[0, jy] + kept[1, 1, my] * spread[1, jy], 0, my)
+            total = part if total is None else total + part
+        total = dropped(kept[1, oy] + shifted(total, 1, 0), 1, oy, masks)
+        compact = pick_lanes(total, (2 * lanes) % LANES)
+        second_ref[oy + 1, 0, 0:1, :] = early_second_ref[16 + oy, 0, 0:1, :]
+        second_ref[oy + 1, 0, 1:2, :] = compact[2:3, 0:32]
+
+
+def last_kernel(
+    own_ref, near_columns_ref, far_columns_ref, far_ref, early_first_ref, early_second_ref, kept_ref, near_ref,
+    first_hbm, second_hbm, block, first_ref, second_ref, first_fix, second_fix, sems,
+):
+    odd_x = lax.axis_index("gx") % 2 == 1
+
+    def send(parts):
+        copies = [pltpu.make_async_copy(source, target, sems.at[i]) for i, source, target in parts]
+        for copy in copies:
+            copy.start()
+        return copies
+
+    @pl.when(odd_x)
+    def _():
+        tiles = [own_ref[r] for r in range(12)] + list(beside(near_columns_ref, far_columns_ref))
+        for r, values in enumerate(tiles):
+            block[r, 0:8, :] = values
+            block[r, 8:12, :] = far_ref[r]
+            block[r, 12:16, :] = near_ref[r]
+        operators(block, first_ref, second_ref)
+        for copy in send([(0, first_ref, first_hbm), (1, second_ref, second_hbm)]):
+            copy.wait()
+
+    @pl.when(jnp.logical_not(odd_x))
+    def _():
+        parts = [(oz, early_first_ref.at[pl.ds(oz * 9, 6)], first_hbm.at[pl.ds(oz * 9, 6)]) for oz in range(3)]
+        parts.append((3, early_second_ref.at[pl.ds(0, 15)], second_hbm.at[pl.ds(0, 15)]))
+        parts.append((4, early_second_ref.at[pl.ds(18, 9)], second_hbm.at[pl.ds(18, 9)]))
+        copies = send(parts)
+        add_row_above(near_ref, early_second_ref, kept_ref, first_fix, second_fix)
+        parts = [(5 + oz, first_fix.at[pl.ds(oz * 3, 3)], first_hbm.at[pl.ds(oz * 9 + 6, 3)]) for oz in range(3)]
+        parts.append((8, second_fix, second_hbm.at[pl.ds(15, 3)]))
+        for copy in copies + send(parts):
+            copy.wait()
 
 
 def swapped(values, axis, first):
@@ -389,18 +537,36 @@
     )(own, near_columns, far_columns)
     far_rows = swapped(far, "gx", 1)
     near_rows = swapped(near, "gx", 0)
+    first = jax.ShapeDtypeStruct((27, 2, 4, 64), jnp.float32)
+    second = jax.ShapeDtypeStruct((27, 1, 2, 32), jnp.float32)
+    large = pltpu.CompilerParams(vmem_limit_bytes=3 << 20)
+    block = pltpu.VMEM((14, 16, LANES), jnp.float32)
+    early = pl.pallas_call(
+        early_kernel,
+        out_shape=(first, second, jax.ShapeDtypeStruct((fix_count, ROWS, LANES), jnp.float32)),
+        in_specs=[whole] * 4,
+        out_specs=(whole,) * 3,
+        scratch_shapes=[block],
+        compiler_params=large,
+        cost_estimate=pl.CostEstimate(flops=3 << 20, bytes_accessed=1 << 20, transcendentals=0),
+        name="early",
+    )(own, near_columns, far_columns, far_rows)
     return pl.pallas_call(
-        operator_kernel,
-        out_shape=(
-            jax.ShapeDtypeStruct((27, 2, 4, 64), jnp.float32),
-            jax.ShapeDtypeStruct((27, 1, 2, 32), jnp.float32),
-        ),
-        in_specs=[whole] * 5,
-        out_specs=(whole,) * 2,
-        scratch_shapes=[pltpu.VMEM((14, 16, LANES), jnp.float32)],
-        compiler_params=pltpu.CompilerParams(vmem_limit_bytes=2 << 20),
-        name="operators",
-    )(own, near_columns, far_columns, far_rows, near_rows)
+        last_kernel,
+        out_shape=(first, second),
+        in_specs=[whole] * 8,
+        out_specs=(pl.BlockSpec(memory_space=pltpu.HBM),) * 2,
+        scratch_shapes=[
+            block,
+            pltpu.VMEM(first.shape, jnp.float32),
+            pltpu.VMEM(second.shape, jnp.float32),
+            pltpu.VMEM((9, 2, 4, 64), jnp.float32),
+            pltpu.VMEM((3, 1, 2, 32), jnp.float32),
+            pltpu.SemaphoreType.DMA((9,)),
+        ],
+        compiler_params=large,
+        name="last",
+    )(own, near_columns, far_columns, far_rows, *early, near_rows)
 
 
 def solution(mesh):

time: 22.3 us -> 22.2 us (level)
  waiting for transfers between devices: 8.04 us -> 7.36 us
  Pallas kernels: 1.35 us -> 1.9 us
    ppermute x4, waiting for transfers between devices: 8.04 us -> 7.36 us  [swapped(): return lax.ppermute(values, axis, pairs + [(b, a) for a, b in pairs])]
    pallas_call x1 -> x2, Pallas kernels: 1.25 us -> 1.8 us  [the longest x1 1.13 us: body(): pl.pallas_call(last_kernel, out_shape=(first, second), in_specs=[whole] *...]
  transfers between devices with their start and end apart: 4 -> 4, of which waited for: 3 -> 3; matrix products, arithmetic and copies ran while one was open for 0% -> 0% of each run, Pallas kernels for 0% -> 3%
where the time goes in v4:
time: 22.2 us; the launch traced here: 22 us
  starting transfers between devices  11.2 us (50%)
  waiting for transfers between devices  7.36 us (33%)
  Pallas kernels  1.9 us (9%)
  other arithmetic  0.81 us (4%)
  between operations  0.69 us (3%)
    ppermute x4, starting transfers between devices, swapped(): return lax.ppermute(values, axis, pairs + [(b, a) for a, b in pairs])  11.2 us
    ppermute x4, waiting for transfers between devices, swapped(): return lax.ppermute(values, axis, pairs + [(b, a) for a, b in pairs])  7.36 us
    pallas_call x1, Pallas kernels, body(): pl.pallas_call(last_kernel, out_shape=(first, second), in_specs=[whole] *...  1.13 us
    add x1, other arithmetic, body(): face_open * 4 + material[None]  0.81 us
    pallas_call x1, Pallas kernels, body(): pl.pallas_call(early_kernel, out_shape=(first, second, jax.ShapeDtypeStru...  0.67 us
  transfers between devices with their start and end apart: 4, of which 3 were waited for; matrix products, arithmetic and copies ran while one was open for 0% of the time, Pallas kernels for 3%

profile of v4, /device:TPU:312, one launch (start us, length us, event | category | flops | bytes accessed | tf_op | source)
XLA Modules:
  0.0 22.0 jit_solution(7763464644627903367)
XLA Ops:
  0.6 0.8 %multiply_add_fusion.inputs_ref = s32[3,4,8,128]{3,2,1,0:T(8,128)S(1)} fusion(s32[3,4,8,128]{3,2,1,0:T(8,128)} %param.3, s32[4,8,128]{2,1,0:T(8,128)} %param.2), kind=kLoop, calls=%fused_computation | loop fusion | flops 24576 | bytes 114688 | tf_op jit(solution)/shard_map/add | solution.py:527
  1.4 0.1 couplings.1
  1.5 1.9 %collective-permute-start = (f32[8,128]{1,0:T(8,128)S(1)}, f32[8,128]{1,0:T(8,128)S(1)}, u32[]{:S(2)}, u32[]{:S(2)}) collective-permute-start(f32[8,128]{1,0:T(8,128)S(1)} %get-tuple-element.11), channel_id=1, source_target_pairs={{0,1},{2,3},{4,5},{6,7},{8,9},{10,11},{12,13},{14,15},{1,0},{3,2},... | collective-permute-start | bytes 12296 | tf_op jit(solution)/shard_map/ppermute | solution.py:512
  3.5 1.9 %collective-permute-start.1 = (f32[8,128]{1,0:T(8,128)S(1)}, f32[8,128]{1,0:T(8,128)S(1)}, u32[]{:S(2)}, u32[]{:S(2)}) collective-permute-start(f32[8,128]{1,0:T(8,128)S(1)} %get-tuple-element.12), channel_id=1, source_target_pairs={{1,2},{3,4},{5,6},{7,8},{9,10},{11,12},{13,14},{2,1},{4,3},{6,5},{... | collective-permute-start | bytes 12296 | tf_op jit(solution)/shard_map/ppermute | solution.py:512
  5.4 0.0 collective-permute-done.near_columns_ref
  5.4 4.2 %collective-permute-done.1.far_columns_ref = f32[8,128]{1,0:T(8,128)S(1)} collective-permute-done((f32[8,128]{1,0:T(8,128)S(1)}, f32[8,128]{1,0:T(8,128)S(1)}, u32[]{:S(2)}, u32[]{:S(2)}) %collective-permute-start.1) | collective-permute-done | bytes 4128 | tf_op jit(solution)/shard_map/ppermute | solution.py:512
  9.6 5.5 %collective-permute-start.2 = (f32[14,4,128]{2,1,0:T(4,128)S(1)}, f32[14,4,128]{2,1,0:T(4,128)S(1)}, u32[]{:S(2)}, u32[]{:S(2)}) collective-permute-start(f32[14,4,128]{2,1,0:T(4,128)S(1)} %get-tuple-element.13), channel_id=1, source_target_pairs={{16,32},{48,64},{80,96},{112,128},{144,160},{176,192},{208,224},{2... | collective-permute-start | bytes 86024 | tf_op jit(solution)/shard_map/ppermute | solution.py:512
  15.1 1.9 %collective-permute-start.3 = (f32[14,4,128]{2,1,0:T(4,128)S(1)}, f32[14,4,128]{2,1,0:T(4,128)S(1)}, u32[]{:S(2)}, u32[]{:S(2)}) collective-permute-start(f32[14,4,128]{2,1,0:T(4,128)S(1)} %get-tuple-element.17), channel_id=1, source_target_pairs={{0,16},{32,48},{64,80},{96,112},{128,144},{160,176},{192,208},{224... | collective-permute-start | bytes 86024 | tf_op jit(solution)/shard_map/ppermute | solution.py:512
  17.0 0.5 %collective-permute-done.2.far_ref = f32[14,4,128]{2,1,0:T(4,128)S(1)} collective-permute-done((f32[14,4,128]{2,1,0:T(4,128)S(1)}, f32[14,4,128]{2,1,0:T(4,128)S(1)}, u32[]{:S(2)}, u32[]{:S(2)}) %collective-permute-start.2) | collective-permute-done | bytes 28704 | tf_op jit(solution)/shard_map/ppermute | solution.py:512
  17.5 0.7 %early.1 = (f32[27,2,4,64]{3,2,1,0:T(4,128)S(1)}, f32[27,1,2,32]{3,2,1,0:T(2,128)S(1)}, f32[34,8,128]{2,1,0:T(8,128)S(1)}) custom-call(f32[12,8,128]{2,1,0:T(8,128)S(1)} %get-tuple-element.10.own_ref, f32[8,128]{1,0:T(8,128)S(1)} %collective-permute-done.near_columns_ref, f32[8,128]{1,0:T(8,128)S(1)} %collective-permute-done.1.far_columns_ref, ...), custom_call_target="tpu_custom_call" | custom-call | flops 3145728 | bytes 1048576 | tf_op jit(solution)/shard_map/early/pallas_call | solution.py:544
  18.2 2.7 %collective-permute-done.3.near_ref = f32[14,4,128]{2,1,0:T(4,128)S(1)} collective-permute-done((f32[14,4,128]{2,1,0:T(4,128)S(1)}, f32[14,4,128]{2,1,0:T(4,128)S(1)}, u32[]{:S(2)}, u32[]{:S(2)}) %collective-permute-start.3) | collective-permute-done | bytes 28704 | tf_op jit(solution)/shard_map/ppermute | solution.py:512
  20.8 1.1 %last.1 = (f32[27,2,4,64]{3,2,1,0:T(4,128)}, f32[27,1,2,32]{3,2,1,0:T(2,128)}) custom-call(f32[12,8,128]{2,1,0:T(8,128)S(1)} %get-tuple-element.10.own_ref, f32[8,128]{1,0:T(8,128)S(1)} %collective-permute-done.near_columns_ref, f32[8,128]{1,0:T(8,128)S(1)} %collective-permute-done.1.far_columns_ref, f32[14,4,128]{2,1,0:T(4,128)S(1)} %collective-permute-done.2.far_ref, ...), custom_call_target="tpu_custom_call" | custom-call | tf_op jit(solution)/shard_map/last/pallas_call | solution.py:554
  (1 shorter events, 0.0 us)
Async XLA Ops:
  1.5 3.9 %collective-permute-start = (f32[8,128]{1,0:T(8,128)S(1)}, f32[8,128]{1,0:T(8,128)S(1)}, u32[]{:S(2)}, u32[]{:S(2)}) collective-permute-start(f32[8,128]{1,0:T(8,128)S(1)} %get-tuple-element.11), channel_id=1, source_target_pairs={{0,1},{2,3},{4,5},{6,7},{8,9},{10,11},{12,13},{14,15},{1,0},{3,2},... | collective-permute-start | bytes 12296 | tf_op jit(solution)/shard_map/ppermute | solution.py:512
  3.5 6.1 %collective-permute-start.1 = (f32[8,128]{1,0:T(8,128)S(1)}, f32[8,128]{1,0:T(8,128)S(1)}, u32[]{:S(2)}, u32[]{:S(2)}) collective-permute-start(f32[8,128]{1,0:T(8,128)S(1)} %get-tuple-element.12), channel_id=1, source_target_pairs={{1,2},{3,4},{5,6},{7,8},{9,10},{11,12},{13,14},{2,1},{4,3},{6,5},{... | collective-permute-start | bytes 12296 | tf_op jit(solution)/shard_map/ppermute | solution.py:512
  9.6 7.9 %collective-permute-start.2 = (f32[14,4,128]{2,1,0:T(4,128)S(1)}, f32[14,4,128]{2,1,0:T(4,128)S(1)}, u32[]{:S(2)}, u32[]{:S(2)}) collective-permute-start(f32[14,4,128]{2,1,0:T(4,128)S(1)} %get-tuple-element.13), channel_id=1, source_target_pairs={{16,32},{48,64},{80,96},{112,128},{144,160},{176,192},{208,224},{2... | collective-permute-start | bytes 86024 | tf_op jit(solution)/shard_map/ppermute | solution.py:512
  15.1 5.8 %collective-permute-start.3 = (f32[14,4,128]{2,1,0:T(4,128)S(1)}, f32[14,4,128]{2,1,0:T(4,128)S(1)}, u32[]{:S(2)}, u32[]{:S(2)}) collective-permute-start(f32[14,4,128]{2,1,0:T(4,128)S(1)} %get-tuple-element.17), channel_id=1, source_target_pairs={{0,16},{32,48},{64,80},{96,112},{128,144},{160,176},{192,208},{224... | collective-permute-start | bytes 86024 | tf_op jit(solution)/shard_map/ppermute | solution.py:512

commit v5 on v4

--- a/solution.py
+++ b/solution.py
@@ -369,7 +369,7 @@
         offset = (o // 9 - 1, o // 3 % 3 - 1, o % 3 - 1)
         for z in range(2):
             full[offset, z] = operator.get((offset, z), empty)
-            first_ref[o, z] = full[offset, z][0:4, 0:64]
+            first_ref[o // 9, o % 9, z] = full[offset, z][0:4, 0:64]
     results, own = second_operator(full, chain, rows, lanes, hold)
     masks = edge_masks(last_x, last_y, rows, lanes, 2)
     second_ref[...] = jnp.zeros(second_ref.shape, jnp.float32)
@@ -377,7 +377,7 @@
         compact = pick_lanes(dropped(values, ox, oy, masks), (2 * lanes) % LANES)
         second_ref[9 + (ox + 1) * 3 + oy + 1, 0, 0:1, :] = compact[0:1, 0:32]
         second_ref[9 + (ox + 1) * 3 + oy + 1, 0, 1:2, :] = compact[2:3, 0:32]
-    return operator, factors, results, own
+    return operator, factors, own
 
 
 fix_entries = [((oz, 1, oy), z) for z in (0, 1) for oz in (-z, 1 - z) for oy in (-1, 0, 1)]
@@ -391,8 +391,7 @@
     for ty in range(1 + qy)
 ]
 fix_sides = [(z, 1, my) for z in (0, 1) for my in (-1, 0, 1)]
-fix_results = [(1, oy) for oy in (-1, 0, 1)]
-fix_count = len(fix_entries) + len(fix_factors) + len(fix_sides) + len(fix_results)
+fix_count = len(fix_entries) + len(fix_factors) + len(fix_sides)
 
 
 def early_kernel(own_ref, near_columns_ref, far_columns_ref, far_ref, first_ref, second_ref, kept_ref, block):
@@ -401,23 +400,32 @@
         block[r, 0:8, :] = values
         block[r, 8:12, :] = jnp.zeros((4, LANES), jnp.float32)
         block[r, 12:16, :] = far_ref[r]
-    operator, factors, results, own = operators(block, first_ref, second_ref, ROWS // 2 - 1)
+    operator, factors, own = operators(block, first_ref, second_ref, ROWS // 2 - 1)
     kept = [operator[e] for e in fix_entries] + [factors[e] for e in fix_factors]
-    kept += [own[e] for e in fix_sides] + [results[e] for e in fix_results]
+    kept += [own[e] for e in fix_sides]
     for i, values in enumerate(kept):
         kept_ref[i] = values
 
 
-def add_row_above(near_ref, early_second_ref, kept_ref, first_ref, second_ref):
+def add_row_above(near_ref, early_second_ref, kept_ref, first_ref, second_ref, send_first):
     rows, lanes, last_x, last_y = places()
-    kept = {e: kept_ref[i] for i, e in enumerate(fix_entries + fix_factors + fix_sides + fix_results)}
+    kept = {e: kept_ref[i] for i, e in enumerate(fix_entries + fix_factors + fix_sides)}
 
     def row(r):
         return jnp.broadcast_to(near_ref[r, 0:1, :], (ROWS, LANES))
 
-    picks = lane_picks(lanes)
-    edges = columns_beside(row(12), row(13), lanes, picks[0])
-    c = {(d, z): split_lanes(row(d * 4 + z), d * 4 + z, edges, picks) for d in (0, 2) for z in range(4)}
+    _, even_lanes, at_even, at_odd = lane_picks(lanes)
+    left, right = row(12), row(13)
+    in_left = 2 * (lanes % 2)
+    c = {}
+    for d in (0, 2):
+        for z in range(4):
+            r = d * 4 + z
+            values = row(r)
+            below = [pick_lanes(left, in_left + (4 * r + py)) for py in range(2)]
+            above = pick_lanes(right, jnp.full((ROWS, LANES), 4 * r + 4, jnp.int32))
+            even = jnp.where(at_even, jnp.where(at_odd, below[0], above), pick_lanes(values, even_lanes))
+            c[d, z] = (even, jnp.where(at_odd, below[1], pick_lanes(values, even_lanes + 1)))
     line_y = {z: line_terms(*c[2, z]) for z in range(4)}
     line_z = {(zc, py): line_terms(c[0, 2 * zc][py], c[0, 2 * zc + 1][py]) for zc in range(2) for py in range(2)}
 
@@ -440,35 +448,43 @@
             total = total - shifted(sums[offset, z, 1], 0, -1)
         entries[offset, z] = dropped(total, *offset[1:], masks)
         whole = jnp.where(rows == ROWS // 2 - 1, entries[offset, z], kept[offset, z])
-        first_ref[(offset[0] + 1) * 3 + offset[2] + 1, z] = whole[0:4, 0:64]
-    for offset, z in (((-1, 1), 0), ((1, 1), 1)):
+        first_ref[offset[0] + 1, offset[2] + 1, z] = whole[0:4, 0:64]
+    for oz, z in ((0, 0), (2, 1)):
         for oy in range(3):
-            first_ref[(offset[0] + 1) * 3 + oy, z] = jnp.zeros((4, 64), jnp.float32)
-
-    depth = line_terms(line_z[0, 0][2], line_z[1, 0][2])[0]
+            first_ref[oz, oy, z] = jnp.zeros((4, 64), jnp.float32)
+    send_first()
+
+    near_y = {(far, j): shifted(line_y[2 * far][2], 0, j) for far in range(2) for j in (-2, -1, 0, 1)}
+    near_z = {(z, j): shifted(line_z[z, 0][2], 0, j) for z in range(2) for j in (-1, 0, 1)}
     odd = lanes % 2 == 1
     spread = {}
     for far in range(2):
-        here = line_y[2 * far][2]
-        f, g = line_terms(shifted(here, 0, -1), here)[:2]
-        down, up = jnp.where(odd, f, 1.0), jnp.where(odd, g, 1.0)
-        if far == 1:
-            down, up = down * depth, up * depth
+        weights = {}
+        for oy in (-1, 0, 1):
+            f, g = line_terms(near_y[far, oy - 1], near_y[far, oy])[:2]
+            there = odd if oy == 0 else ~odd
+            pair = jnp.where(there, f, 1.0), jnp.where(there, g, 1.0)
+            if far == 1:
+                depth = line_terms(near_z[0, oy], near_z[1, oy])[0]
+                pair = pair[0] * depth, pair[1] * depth
+            weights[oy] = pair
         for jy, oy in reaches:
-            weight = reaching(jy, oy, shifted(down if from_below(jy, oy) else up, 0, oy), odd)
+            weight = reaching(jy, oy, weights[oy][0 if from_below(jy, oy) else 1], odd)
             for z in range(2):
                 term = entries[(far - z, 1, oy), z] * weight
                 spread[z, jy] = spread[z, jy] + term if (z, jy) in spread else term
-    masks = edge_masks(last_x, last_y, rows, lanes, 2)
     for oy in (-1, 0, 1):
         total = None
         for my, jy in taken(oy):
-            part = shifted(kept[0, 1, my] * spread[0, jy] + kept[1, 1, my] * spread[1, jy], 0, my)
+            part = kept[0, 1, my] * spread[0, jy] + kept[1, 1, my] * spread[1, jy]
+            part = pick_lanes(part, (2 * lanes + my) % LANES)
             total = part if total is None else total + part
-        total = dropped(kept[1, oy] + shifted(total, 1, 0), 1, oy, masks)
-        compact = pick_lanes(total, (2 * lanes) % LANES)
+        total = jnp.where(last_x, 0.0, total)
+        if oy == 1:
+            total = jnp.where((lanes == LANES // 4 - 1) & last_y, 0.0, total)
         second_ref[oy + 1, 0, 0:1, :] = early_second_ref[16 + oy, 0, 0:1, :]
-        second_ref[oy + 1, 0, 1:2, :] = compact[2:3, 0:32]
+        row_two = early_second_ref[16 + oy, 0, 1:2, :]
+        second_ref[oy + 1, 0, 1:2, :] = row_two + total[ROWS // 2 - 1:ROWS // 2, 0:32]
 
 
 def last_kernel(
@@ -496,14 +512,17 @@
 
     @pl.when(jnp.logical_not(odd_x))
     def _():
-        parts = [(oz, early_first_ref.at[pl.ds(oz * 9, 6)], first_hbm.at[pl.ds(oz * 9, 6)]) for oz in range(3)]
-        parts.append((3, early_second_ref.at[pl.ds(0, 15)], second_hbm.at[pl.ds(0, 15)]))
-        parts.append((4, early_second_ref.at[pl.ds(18, 9)], second_hbm.at[pl.ds(18, 9)]))
-        copies = send(parts)
-        add_row_above(near_ref, early_second_ref, kept_ref, first_fix, second_fix)
-        parts = [(5 + oz, first_fix.at[pl.ds(oz * 3, 3)], first_hbm.at[pl.ds(oz * 9 + 6, 3)]) for oz in range(3)]
-        parts.append((8, second_fix, second_hbm.at[pl.ds(15, 3)]))
-        for copy in copies + send(parts):
+        copies = send([
+            (0, early_first_ref.at[:, pl.ds(0, 6)], first_hbm.at[:, pl.ds(0, 6)]),
+            (1, early_second_ref.at[pl.ds(0, 15)], second_hbm.at[pl.ds(0, 15)]),
+            (2, early_second_ref.at[pl.ds(18, 9)], second_hbm.at[pl.ds(18, 9)]),
+        ])
+
+        def send_first():
+            copies.extend(send([(3, first_fix, first_hbm.at[:, pl.ds(6, 3)])]))
+
+        add_row_above(near_ref, early_second_ref, kept_ref, first_fix, second_fix, send_first)
+        for copy in copies + send([(4, second_fix, second_hbm.at[pl.ds(15, 3)])]):
             copy.wait()
 
 
@@ -537,7 +556,7 @@
     )(own, near_columns, far_columns)
     far_rows = swapped(far, "gx", 1)
     near_rows = swapped(near, "gx", 0)
-    first = jax.ShapeDtypeStruct((27, 2, 4, 64), jnp.float32)
+    first = jax.ShapeDtypeStruct((3, 9, 2, 4, 64), jnp.float32)
     second = jax.ShapeDtypeStruct((27, 1, 2, 32), jnp.float32)
     large = pltpu.CompilerParams(vmem_limit_bytes=3 << 20)
     block = pltpu.VMEM((14, 16, LANES), jnp.float32)
@@ -551,7 +570,7 @@
         cost_estimate=pl.CostEstimate(flops=3 << 20, bytes_accessed=1 << 20, transcendentals=0),
         name="early",
     )(own, near_columns, far_columns, far_rows)
-    return pl.pallas_call(
+    first_level, second_level = pl.pallas_call(
         last_kernel,
         out_shape=(first, second),
         in_specs=[whole] * 8,
@@ -560,13 +579,14 @@
             block,
             pltpu.VMEM(first.shape, jnp.float32),
             pltpu.VMEM(second.shape, jnp.float32),
-            pltpu.VMEM((9, 2, 4, 64), jnp.float32),
+            pltpu.VMEM((3, 3, 2, 4, 64), jnp.float32),
             pltpu.VMEM((3, 1, 2, 32), jnp.float32),
-            pltpu.SemaphoreType.DMA((9,)),
+            pltpu.SemaphoreType.DMA((5,)),
         ],
         compiler_params=large,
         name="last",
     )(own, near_columns, far_columns, far_rows, *early, near_rows)
+    return first_level.reshape(27, 2, 4, 64), second_level
 
 
 def solution(mesh):

time: 22.2 us -> 22 us (level)
  no operation moved by 1% of the time
where the time goes in v5:
time: 22 us; the launch traced here: 21.8 us
  starting transfers between devices  11.2 us (51%)
  waiting for transfers between devices  7.36 us (33%)
  Pallas kernels  1.73 us (8%)
  other arithmetic  0.81 us (4%)
  between operations  0.69 us (3%)
    ppermute x4, starting transfers between devices, swapped(): return lax.ppermute(values, axis, pairs + [(b, a) for a, b in pairs])  11.2 us
    ppermute x4, waiting for transfers between devices, swapped(): return lax.ppermute(values, axis, pairs + [(b, a) for a, b in pairs])  7.36 us
    pallas_call x1, Pallas kernels, body(): pl.pallas_call(last_kernel, out_shape=(first, second), in_specs=[whole] *...  0.96 us
    add x1, other arithmetic, body(): face_open * 4 + material[None]  0.81 us
    pallas_call x1, Pallas kernels, body(): pl.pallas_call(early_kernel, out_shape=(first, second, jax.ShapeDtypeStru...  0.67 us
  transfers between devices with their start and end apart: 4, of which 3 were waited for; matrix products, arithmetic and copies ran while one was open for 0% of the time, Pallas kernels for 3%

profile of v5, /device:TPU:312, one launch (start us, length us, event | category | flops | bytes accessed | tf_op | source)
XLA Modules:
  0.0 21.8 jit_solution(10464001607471977142)
XLA Ops:
  0.6 0.8 %multiply_add_fusion.inputs_ref = s32[3,4,8,128]{3,2,1,0:T(8,128)S(1)} fusion(s32[3,4,8,128]{3,2,1,0:T(8,128)} %param.3, s32[4,8,128]{2,1,0:T(8,128)} %param.2), kind=kLoop, calls=%fused_computation | loop fusion | flops 24576 | bytes 114688 | tf_op jit(solution)/shard_map/add | solution.py:546
  1.4 0.1 couplings.1
  1.5 1.9 %collective-permute-start = (f32[8,128]{1,0:T(8,128)S(1)}, f32[8,128]{1,0:T(8,128)S(1)}, u32[]{:S(2)}, u32[]{:S(2)}) collective-permute-start(f32[8,128]{1,0:T(8,128)S(1)} %get-tuple-element.13), channel_id=1, source_target_pairs={{0,1},{2,3},{4,5},{6,7},{8,9},{10,11},{12,13},{14,15},{1,0},{3,2},... | collective-permute-start | bytes 12296 | tf_op jit(solution)/shard_map/ppermute | solution.py:531
  3.5 1.9 %collective-permute-start.1 = (f32[8,128]{1,0:T(8,128)S(1)}, f32[8,128]{1,0:T(8,128)S(1)}, u32[]{:S(2)}, u32[]{:S(2)}) collective-permute-start(f32[8,128]{1,0:T(8,128)S(1)} %get-tuple-element.14), channel_id=1, source_target_pairs={{1,2},{3,4},{5,6},{7,8},{9,10},{11,12},{13,14},{2,1},{4,3},{6,5},{... | collective-permute-start | bytes 12296 | tf_op jit(solution)/shard_map/ppermute | solution.py:531
  5.4 0.0 collective-permute-done.near_columns_ref
  5.4 4.2 %collective-permute-done.1.far_columns_ref = f32[8,128]{1,0:T(8,128)S(1)} collective-permute-done((f32[8,128]{1,0:T(8,128)S(1)}, f32[8,128]{1,0:T(8,128)S(1)}, u32[]{:S(2)}, u32[]{:S(2)}) %collective-permute-start.1) | collective-permute-done | bytes 4128 | tf_op jit(solution)/shard_map/ppermute | solution.py:531
  9.6 5.5 %collective-permute-start.2 = (f32[14,4,128]{2,1,0:T(4,128)S(1)}, f32[14,4,128]{2,1,0:T(4,128)S(1)}, u32[]{:S(2)}, u32[]{:S(2)}) collective-permute-start(f32[14,4,128]{2,1,0:T(4,128)S(1)} %get-tuple-element.15), channel_id=1, source_target_pairs={{16,32},{48,64},{80,96},{112,128},{144,160},{176,192},{208,224},{2... | collective-permute-start | bytes 86024 | tf_op jit(solution)/shard_map/ppermute | solution.py:531
  15.1 1.9 %collective-permute-start.3 = (f32[14,4,128]{2,1,0:T(4,128)S(1)}, f32[14,4,128]{2,1,0:T(4,128)S(1)}, u32[]{:S(2)}, u32[]{:S(2)}) collective-permute-start(f32[14,4,128]{2,1,0:T(4,128)S(1)} %get-tuple-element.19), channel_id=1, source_target_pairs={{0,16},{32,48},{64,80},{96,112},{128,144},{160,176},{192,208},{224... | collective-permute-start | bytes 86024 | tf_op jit(solution)/shard_map/ppermute | solution.py:531
  17.0 0.5 %collective-permute-done.2.far_ref = f32[14,4,128]{2,1,0:T(4,128)S(1)} collective-permute-done((f32[14,4,128]{2,1,0:T(4,128)S(1)}, f32[14,4,128]{2,1,0:T(4,128)S(1)}, u32[]{:S(2)}, u32[]{:S(2)}) %collective-permute-start.2) | collective-permute-done | bytes 28704 | tf_op jit(solution)/shard_map/ppermute | solution.py:531
  17.5 0.7 %early.1 = (f32[3,9,2,4,64]{4,3,2,1,0:T(4,128)S(1)}, f32[27,1,2,32]{3,2,1,0:T(2,128)S(1)}, f32[31,8,128]{2,1,0:T(8,128)S(1)}) custom-call(f32[12,8,128]{2,1,0:T(8,128)S(1)} %get-tuple-element.12.own_ref, f32[8,128]{1,0:T(8,128)S(1)} %collective-permute-done.near_columns_ref, f32[8,128]{1,0:T(8,128)S(1)} %collective-permute-done.1.far_columns_ref, ...), custom_call_target="tpu_custom_call" | custom-call | flops 3145728 | bytes 1048576 | tf_op jit(solution)/shard_map/early/pallas_call | solution.py:563
  18.2 2.7 %collective-permute-done.3.near_ref = f32[14,4,128]{2,1,0:T(4,128)S(1)} collective-permute-done((f32[14,4,128]{2,1,0:T(4,128)S(1)}, f32[14,4,128]{2,1,0:T(4,128)S(1)}, u32[]{:S(2)}, u32[]{:S(2)}) %collective-permute-start.3) | collective-permute-done | bytes 28704 | tf_op jit(solution)/shard_map/ppermute | solution.py:531
  20.8 1.0 %last.1 = (f32[3,9,2,4,64]{4,3,2,1,0:T(4,128)}, f32[27,1,2,32]{3,2,1,0:T(2,128)}) custom-call(f32[12,8,128]{2,1,0:T(8,128)S(1)} %get-tuple-element.12.own_ref, f32[8,128]{1,0:T(8,128)S(1)} %collective-permute-done.near_columns_ref, f32[8,128]{1,0:T(8,128)S(1)} %collective-permute-done.1.far_columns_ref, f32[14,4,128]{2,1,0:T(4,128)S(1)} %collective-permute-done.2.far_ref, ...), custom_call_target="tpu_custom_call" | custom-call | tf_op jit(solution)/shard_map/last/pallas_call | solution.py:573
  (1 shorter events, 0.0 us)
Async XLA Ops:
  1.5 3.9 %collective-permute-start = (f32[8,128]{1,0:T(8,128)S(1)}, f32[8,128]{1,0:T(8,128)S(1)}, u32[]{:S(2)}, u32[]{:S(2)}) collective-permute-start(f32[8,128]{1,0:T(8,128)S(1)} %get-tuple-element.13), channel_id=1, source_target_pairs={{0,1},{2,3},{4,5},{6,7},{8,9},{10,11},{12,13},{14,15},{1,0},{3,2},... | collective-permute-start | bytes 12296 | tf_op jit(solution)/shard_map/ppermute | solution.py:531
  3.5 6.1 %collective-permute-start.1 = (f32[8,128]{1,0:T(8,128)S(1)}, f32[8,128]{1,0:T(8,128)S(1)}, u32[]{:S(2)}, u32[]{:S(2)}) collective-permute-start(f32[8,128]{1,0:T(8,128)S(1)} %get-tuple-element.14), channel_id=1, source_target_pairs={{1,2},{3,4},{5,6},{7,8},{9,10},{11,12},{13,14},{2,1},{4,3},{6,5},{... | collective-permute-start | bytes 12296 | tf_op jit(solution)/shard_map/ppermute | solution.py:531
  9.6 7.9 %collective-permute-start.2 = (f32[14,4,128]{2,1,0:T(4,128)S(1)}, f32[14,4,128]{2,1,0:T(4,128)S(1)}, u32[]{:S(2)}, u32[]{:S(2)}) collective-permute-start(f32[14,4,128]{2,1,0:T(4,128)S(1)} %get-tuple-element.15), channel_id=1, source_target_pairs={{16,32},{48,64},{80,96},{112,128},{144,160},{176,192},{208,224},{2... | collective-permute-start | bytes 86024 | tf_op jit(solution)/shard_map/ppermute | solution.py:531
  15.1 5.8 %collective-permute-start.3 = (f32[14,4,128]{2,1,0:T(4,128)S(1)}, f32[14,4,128]{2,1,0:T(4,128)S(1)}, u32[]{:S(2)}, u32[]{:S(2)}) collective-permute-start(f32[14,4,128]{2,1,0:T(4,128)S(1)} %get-tuple-element.19), channel_id=1, source_target_pairs={{0,16},{32,48},{64,80},{96,112},{128,144},{160,176},{192,208},{224... | collective-permute-start | bytes 86024 | tf_op jit(solution)/shard_map/ppermute | solution.py:531

commit v6 on v5

--- a/solution.py
+++ b/solution.py
@@ -2,6 +2,7 @@
 
 import jax
 import jax.numpy as jnp
+import numpy as np
 from jax import lax
 from jax.experimental import pallas as pl
 from jax.experimental.pallas import tpu as pltpu
@@ -289,8 +290,23 @@
     return results, own
 
 
-def couplings_kernel(inputs_ref, own_ref, near_ref, far_ref):
-    odd_y = lax.axis_index("gy") % 2 == 1
+def swap_order(row, edge, half, where):
+    below_half, inner, at_half = (where(test, 1, 0) for test in (edge < half, row > 0, edge == half))
+    cores_first, border = inner * below_half, inner * at_half
+    order = cores_first * (edge % 2) + (1 - cores_first) * (1 - edge % 2)
+    return border * 2 + (1 - border) * order
+
+
+def own_swaps():
+    row, column, size = lax.axis_index("gx"), lax.axis_index("gy"), lax.axis_size("gy")
+
+    def order(edge):
+        return swap_order(row, edge, size // 2, jnp.where)
+
+    return jnp.where(column > 0, order(column - 1 + (column == 0)), -1), jnp.where(column < size - 1, order(column), -1)
+
+
+def couplings_kernel(inputs_ref, own_ref, *message_refs):
     lanes = lax.broadcasted_iota(jnp.int32, (ROWS, LANES), 1)
     low = jnp.zeros((ROWS, LANES), jnp.float32)
     high = jnp.zeros((ROWS, LANES), jnp.float32)
@@ -301,19 +317,24 @@
         turned = pltpu.roll(values, 4 * r + 4, 1)
         low = jnp.where((lanes >= 4 * r) & (lanes < 4 * r + 4), turned, low)
         high = jnp.where(lanes == 4 * r + 4, turned, high)
-    far_ref[...] = jnp.where(odd_y, low, high)
-    near_ref[...] = jnp.where(odd_y, high, low)
-
-
-def beside(near_ref, far_ref):
-    odd_y = lax.axis_index("gy") % 2 == 1
-    far, near = far_ref[...], near_ref[...]
-    return jnp.where(odd_y, near, far), jnp.where(odd_y, far, near)
-
-
-def edges_kernel(own_ref, near_columns_ref, far_columns_ref, far_ref, near_ref):
+    _, above = own_swaps()
+    for k, ref in enumerate(message_refs):
+        ref[...] = jnp.where(above == k, low, high)
+
+
+def beside(column_refs):
+    sides = []
+    for swap in own_swaps():
+        values = jnp.zeros((ROWS, LANES), jnp.float32)
+        for k, ref in enumerate(column_refs):
+            values = jnp.where(swap == k, ref[...], values)
+        sides.append(values)
+    return sides
+
+
+def edges_kernel(own_ref, first_columns_ref, second_columns_ref, third_columns_ref, far_ref, near_ref):
     odd_x = lax.axis_index("gx") % 2 == 1
-    tiles = [own_ref[r] for r in range(12)] + list(beside(near_columns_ref, far_columns_ref))
+    tiles = [own_ref[r] for r in range(12)] + beside((first_columns_ref, second_columns_ref, third_columns_ref))
     for r, values in enumerate(tiles):
         far_ref[r] = jnp.where(odd_x, values[4:8, :], values[0:4, :])
         near_ref[r] = jnp.where(odd_x, values[0:4, :], values[4:8, :])
@@ -394,8 +415,11 @@
 fix_count = len(fix_entries) + len(fix_factors) + len(fix_sides)
 
 
-def early_kernel(own_ref, near_columns_ref, far_columns_ref, far_ref, first_ref, second_ref, kept_ref, block):
-    tiles = [own_ref[r] for r in range(12)] + list(beside(near_columns_ref, far_columns_ref))
+def early_kernel(
+    own_ref, first_columns_ref, second_columns_ref, third_columns_ref, far_ref,
+    first_ref, second_ref, kept_ref, block,
+):
+    tiles = [own_ref[r] for r in range(12)] + beside((first_columns_ref, second_columns_ref, third_columns_ref))
     for r, values in enumerate(tiles):
         block[r, 0:8, :] = values
         block[r, 8:12, :] = jnp.zeros((4, LANES), jnp.float32)
@@ -488,7 +512,8 @@
 
 
 def last_kernel(
-    own_ref, near_columns_ref, far_columns_ref, far_ref, early_first_ref, early_second_ref, kept_ref, near_ref,
+    own_ref, first_columns_ref, second_columns_ref, third_columns_ref, far_ref,
+    early_first_ref, early_second_ref, kept_ref, near_ref,
     first_hbm, second_hbm, block, first_ref, second_ref, first_fix, second_fix, sems,
 ):
     odd_x = lax.axis_index("gx") % 2 == 1
@@ -501,7 +526,7 @@
 
     @pl.when(odd_x)
     def _():
-        tiles = [own_ref[r] for r in range(12)] + list(beside(near_columns_ref, far_columns_ref))
+        tiles = [own_ref[r] for r in range(12)] + beside((first_columns_ref, second_columns_ref, third_columns_ref))
         for r, values in enumerate(tiles):
             block[r, 0:8, :] = values
             block[r, 8:12, :] = far_ref[r]
@@ -531,29 +556,39 @@
     return lax.ppermute(values, axis, pairs + [(b, a) for a, b in pairs])
 
 
+def swapped_columns(values, which):
+    count_x, count_y = lax.axis_size("gx"), lax.axis_size("gy")
+    pairs = [
+        (row * count_y + edge, row * count_y + edge + 1)
+        for row in range(count_x)
+        for edge in range(count_y - 1)
+        if swap_order(row, edge, count_y // 2, np.where) == which
+    ]
+    return lax.ppermute(values, ("gx", "gy"), pairs + [(b, a) for a, b in pairs])
+
+
 def body(material, face_open):
     whole = pl.BlockSpec(memory_space=pltpu.VMEM)
     page = jax.ShapeDtypeStruct((ROWS, LANES), jnp.float32)
     edge = jax.ShapeDtypeStruct((14, 4, LANES), jnp.float32)
     small = pltpu.CompilerParams(vmem_limit_bytes=1 << 20)
-    own, near, far = pl.pallas_call(
+    own, *messages = pl.pallas_call(
         couplings_kernel,
-        out_shape=(jax.ShapeDtypeStruct((12, ROWS, LANES), jnp.float32), page, page),
+        out_shape=(jax.ShapeDtypeStruct((12, ROWS, LANES), jnp.float32),) + (page,) * 3,
         in_specs=[whole],
-        out_specs=(whole,) * 3,
+        out_specs=(whole,) * 4,
         compiler_params=small,
         name="couplings",
     )(face_open * 4 + material[None])
-    near_columns = swapped(near, "gy", 0)
-    far_columns = swapped(far, "gy", 1)
+    columns = [swapped_columns(message, k) for k, message in enumerate(messages)]
     far, near = pl.pallas_call(
         edges_kernel,
         out_shape=(edge, edge),
-        in_specs=[whole] * 3,
+        in_specs=[whole] * 4,
         out_specs=(whole,) * 2,
         compiler_params=small,
         name="edges",
-    )(own, near_columns, far_columns)
+    )(own, *columns)
     far_rows = swapped(far, "gx", 1)
     near_rows = swapped(near, "gx", 0)
     first = jax.ShapeDtypeStruct((3, 9, 2, 4, 64), jnp.float32)
@@ -563,17 +598,17 @@
     early = pl.pallas_call(
         early_kernel,
         out_shape=(first, second, jax.ShapeDtypeStruct((fix_count, ROWS, LANES), jnp.float32)),
-        in_specs=[whole] * 4,
+        in_specs=[whole] * 5,
         out_specs=(whole,) * 3,
         scratch_shapes=[block],
         compiler_params=large,
         cost_estimate=pl.CostEstimate(flops=3 << 20, bytes_accessed=1 << 20, transcendentals=0),
         name="early",
-    )(own, near_columns, far_columns, far_rows)
+    )(own, *columns, far_rows)
     first_level, second_level = pl.pallas_call(
         last_kernel,
         out_shape=(first, second),
-        in_specs=[whole] * 8,
+        in_specs=[whole] * 9,
         out_specs=(pl.BlockSpec(memory_space=pltpu.HBM),) * 2,
         scratch_shapes=[
             block,
@@ -585,7 +620,7 @@
         ],
         compiler_params=large,
         name="last",
-    )(own, near_columns, far_columns, far_rows, *early, near_rows)
+    )(own, *columns, far_rows, *early, near_rows)
     return first_level.reshape(27, 2, 4, 64), second_level
 
 

time: 22 us -> 21.3 us (0.968)
  the two profiles are of different devices: /device:TPU:312 before, /device:TPU:249 now
where the time goes in v6:
time: 21.3 us; the launch traced here: 21 us
  starting transfers between devices  14.2 us (67%)
  waiting for transfers between devices  3.59 us (17%)
  Pallas kernels  1.76 us (8%)
  other arithmetic  0.81 us (4%)
  between operations  0.71 us (3%)
    ppermute x3, starting transfers between devices, swapped_columns(): lax.ppermute(values, ('gx', 'gy'), pairs + [(b, a) for a, b in pairs])  7.09 us
    ppermute x2, starting transfers between devices, swapped(): return lax.ppermute(values, axis, pairs + [(b, a) for a, b in pairs])  7.09 us
    ppermute x2, waiting for transfers between devices, swapped(): return lax.ppermute(values, axis, pairs + [(b, a) for a, b in pairs])  1.98 us
    ppermute x3, waiting for transfers between devices, swapped_columns(): lax.ppermute(values, ('gx', 'gy'), pairs + [(b, a) for a, b in pairs])  1.6 us
    pallas_call x1, Pallas kernels, body(): pl.pallas_call(last_kernel, out_shape=(first, second), in_specs=[whole] *...  0.96 us
    add x1, other arithmetic, body(): face_open * 4 + material[None]  0.81 us
    pallas_call x1, Pallas kernels, body(): pl.pallas_call(early_kernel, out_shape=(first, second, jax.ShapeDtypeStru...  0.69 us
  transfers between devices with their start and end apart: 5, of which 2 were waited for; matrix products, arithmetic and copies ran while one was open for 0% of the time, Pallas kernels for 3%

profile of v6, /device:TPU:249, one launch (start us, length us, event | category | flops | bytes accessed | tf_op | source)
XLA Modules:
  0.0 21.0 jit_solution(8729358591515683326)
XLA Ops:
  0.6 0.8 %multiply_add_fusion.inputs_ref = s32[3,4,8,128]{3,2,1,0:T(8,128)S(1)} fusion(s32[3,4,8,128]{3,2,1,0:T(8,128)} %param.3, s32[4,8,128]{2,1,0:T(8,128)} %param.2), kind=kLoop, calls=%fused_computation | loop fusion | flops 24576 | bytes 114688 | tf_op jit(solution)/shard_map/add | solution.py:582
  1.4 0.1 couplings.1
  1.5 2.6 %collective-permute-start = (f32[8,128]{1,0:T(8,128)S(1)}, f32[8,128]{1,0:T(8,128)S(1)}, u32[]{:S(2)}, u32[]{:S(2)}) collective-permute-start(f32[8,128]{1,0:T(8,128)S(1)} %get-tuple-element.14), channel_id=1, source_target_pairs={{1,2},{3,4},{5,6},{7,8},{9,10},{11,12},{13,14},{16,17},{18,19},{20... | collective-permute-start | bytes 12296 | tf_op jit(solution)/shard_map/ppermute | solution.py:567
  4.1 3.8 %collective-permute-start.1 = (f32[8,128]{1,0:T(8,128)S(1)}, f32[8,128]{1,0:T(8,128)S(1)}, u32[]{:S(2)}, u32[]{:S(2)}) collective-permute-start(f32[8,128]{1,0:T(8,128)S(1)} %get-tuple-element.15), channel_id=1, source_target_pairs={{0,1},{2,3},{4,5},{6,7},{8,9},{10,11},{12,13},{14,15},{17,18},{19,... | collective-permute-start | bytes 12296 | tf_op jit(solution)/shard_map/ppermute | solution.py:567
  8.0 0.7 %collective-permute-start.2 = (f32[8,128]{1,0:T(8,128)S(1)}, f32[8,128]{1,0:T(8,128)S(1)}, u32[]{:S(2)}, u32[]{:S(2)}) collective-permute-start(f32[8,128]{1,0:T(8,128)S(1)} %get-tuple-element.16), channel_id=1, source_target_pairs={{24,25},{40,41},{56,57},{72,73},{88,89},{104,105},{120,121},{136,1... | collective-permute-start | bytes 12296 | tf_op jit(solution)/shard_map/ppermute | solution.py:567
  8.7 0.0 collective-permute-done.first_columns_ref
  8.7 1.6 %collective-permute-done.1.second_columns_ref = f32[8,128]{1,0:T(8,128)S(1)} collective-permute-done((f32[8,128]{1,0:T(8,128)S(1)}, f32[8,128]{1,0:T(8,128)S(1)}, u32[]{:S(2)}, u32[]{:S(2)}) %collective-permute-start.1) | collective-permute-done | bytes 4128 | tf_op jit(solution)/shard_map/ppermute | solution.py:567
  10.3 0.0 collective-permute-done.2.third_columns_ref
  10.3 5.2 %collective-permute-start.3 = (f32[14,4,128]{2,1,0:T(4,128)S(1)}, f32[14,4,128]{2,1,0:T(4,128)S(1)}, u32[]{:S(2)}, u32[]{:S(2)}) collective-permute-start(f32[14,4,128]{2,1,0:T(4,128)S(1)} %get-tuple-element.17), channel_id=1, source_target_pairs={{16,32},{48,64},{80,96},{112,128},{144,160},{176,192},{208,224},{2... | collective-permute-start | bytes 86024 | tf_op jit(solution)/shard_map/ppermute | solution.py:556
  15.5 1.9 %collective-permute-start.4 = (f32[14,4,128]{2,1,0:T(4,128)S(1)}, f32[14,4,128]{2,1,0:T(4,128)S(1)}, u32[]{:S(2)}, u32[]{:S(2)}) collective-permute-start(f32[14,4,128]{2,1,0:T(4,128)S(1)} %get-tuple-element.21), channel_id=1, source_target_pairs={{0,16},{32,48},{64,80},{96,112},{128,144},{160,176},{192,208},{224... | collective-permute-start | bytes 86024 | tf_op jit(solution)/shard_map/ppermute | solution.py:556
  17.4 0.0 collective-permute-done.3.far_ref
  17.4 0.7 %early.1 = (f32[3,9,2,4,64]{4,3,2,1,0:T(4,128)S(1)}, f32[27,1,2,32]{3,2,1,0:T(2,128)S(1)}, f32[31,8,128]{2,1,0:T(8,128)S(1)}) custom-call(f32[12,8,128]{2,1,0:T(8,128)S(1)} %get-tuple-element.13.own_ref, f32[8,128]{1,0:T(8,128)S(1)} %collective-permute-done.first_columns_ref, f32[8,128]{1,0:T(8,128)S(1)} %collective-permute-done.1.second_columns_ref, ...), custom_call_target="tpu_custom_call" | custom-call | flops 3145728 | bytes 1048576 | tf_op jit(solution)/shard_map/early/pallas_call | solution.py:598
  18.1 2.0 %collective-permute-done.4.near_ref = f32[14,4,128]{2,1,0:T(4,128)S(1)} collective-permute-done((f32[14,4,128]{2,1,0:T(4,128)S(1)}, f32[14,4,128]{2,1,0:T(4,128)S(1)}, u32[]{:S(2)}, u32[]{:S(2)}) %collective-permute-start.4) | collective-permute-done | bytes 28704 | tf_op jit(solution)/shard_map/ppermute | solution.py:556
  20.1 1.0 %last.1 = (f32[3,9,2,4,64]{4,3,2,1,0:T(4,128)}, f32[27,1,2,32]{3,2,1,0:T(2,128)}) custom-call(f32[12,8,128]{2,1,0:T(8,128)S(1)} %get-tuple-element.13.own_ref, f32[8,128]{1,0:T(8,128)S(1)} %collective-permute-done.first_columns_ref, f32[8,128]{1,0:T(8,128)S(1)} %collective-permute-done.1.second_columns_ref, ...), custom_call_target="tpu_custom_call" | custom-call | tf_op jit(solution)/shard_map/last/pallas_call | solution.py:608
  (1 shorter events, 0.0 us)
Async XLA Ops:
  1.5 7.1 %collective-permute-start = (f32[8,128]{1,0:T(8,128)S(1)}, f32[8,128]{1,0:T(8,128)S(1)}, u32[]{:S(2)}, u32[]{:S(2)}) collective-permute-start(f32[8,128]{1,0:T(8,128)S(1)} %get-tuple-element.14), channel_id=1, source_target_pairs={{1,2},{3,4},{5,6},{7,8},{9,10},{11,12},{13,14},{16,17},{18,19},{20... | collective-permute-start | bytes 12296 | tf_op jit(solution)/shard_map/ppermute | solution.py:567
  4.1 6.1 %collective-permute-start.1 = (f32[8,128]{1,0:T(8,128)S(1)}, f32[8,128]{1,0:T(8,128)S(1)}, u32[]{:S(2)}, u32[]{:S(2)}) collective-permute-start(f32[8,128]{1,0:T(8,128)S(1)} %get-tuple-element.15), channel_id=1, source_target_pairs={{0,1},{2,3},{4,5},{6,7},{8,9},{10,11},{12,13},{14,15},{17,18},{19,... | collective-permute-start | bytes 12296 | tf_op jit(solution)/shard_map/ppermute | solution.py:567
  8.0 2.3 %collective-permute-start.2 = (f32[8,128]{1,0:T(8,128)S(1)}, f32[8,128]{1,0:T(8,128)S(1)}, u32[]{:S(2)}, u32[]{:S(2)}) collective-permute-start(f32[8,128]{1,0:T(8,128)S(1)} %get-tuple-element.16), channel_id=1, source_target_pairs={{24,25},{40,41},{56,57},{72,73},{88,89},{104,105},{120,121},{136,1... | collective-permute-start | bytes 12296 | tf_op jit(solution)/shard_map/ppermute | solution.py:567
  10.3 7.1 %collective-permute-start.3 = (f32[14,4,128]{2,1,0:T(4,128)S(1)}, f32[14,4,128]{2,1,0:T(4,128)S(1)}, u32[]{:S(2)}, u32[]{:S(2)}) collective-permute-start(f32[14,4,128]{2,1,0:T(4,128)S(1)} %get-tuple-element.17), channel_id=1, source_target_pairs={{16,32},{48,64},{80,96},{112,128},{144,160},{176,192},{208,224},{2... | collective-permute-start | bytes 86024 | tf_op jit(solution)/shard_map/ppermute | solution.py:556
  15.5 4.6 %collective-permute-start.4 = (f32[14,4,128]{2,1,0:T(4,128)S(1)}, f32[14,4,128]{2,1,0:T(4,128)S(1)}, u32[]{:S(2)}, u32[]{:S(2)}) collective-permute-start(f32[14,4,128]{2,1,0:T(4,128)S(1)} %get-tuple-element.21), channel_id=1, source_target_pairs={{0,16},{32,48},{64,80},{96,112},{128,144},{160,176},{192,208},{224... | collective-permute-start | bytes 86024 | tf_op jit(solution)/shard_map/ppermute | solution.py:556

commit v7 on v6

--- a/solution.py
+++ b/solution.py
@@ -8,15 +8,15 @@
 from jax.experimental.pallas import tpu as pltpu
 from jax.sharding import PartitionSpec as P
 
-permit_levels = (1.0 / 80.0, 4.0 / 80.0, 20.0 / 80.0, 1.0)
+permit_levels = (1.0 / 80.0 / 64.0, 4.0 / 80.0 / 64.0, 20.0 / 80.0 / 64.0, 1.0 / 64.0)
 
 ROWS, LANES = 8, 128
 
 
 def permittivity(material):
-    values = jnp.zeros(material.shape, jnp.float32)
-    for material_id in range(4):
-        values = values + jnp.where(material == material_id, permit_levels[material_id], 0.0)
+    values = jnp.full(material.shape, permit_levels[3], jnp.float32)
+    for material_id in range(3):
+        values = jnp.where(material == material_id, permit_levels[material_id], values)
     return values
 
 
@@ -312,7 +312,7 @@
     high = jnp.zeros((ROWS, LANES), jnp.float32)
     eps = [permittivity(inputs_ref[0, z] & 3) for z in range(4)]
     for r in range(12):
-        values = (inputs_ref[r // 4, r % 4] >> 2).astype(jnp.float32) / 64.0 * eps[r % 4]
+        values = (inputs_ref[r // 4, r % 4] >> 2).astype(jnp.float32) * eps[r % 4]
         own_ref[r] = values
         turned = pltpu.roll(values, 4 * r + 4, 1)
         low = jnp.where((lanes >= 4 * r) & (lanes < 4 * r + 4), turned, low)
@@ -452,6 +452,22 @@
             c[d, z] = (even, jnp.where(at_odd, below[1], pick_lanes(values, even_lanes + 1)))
     line_y = {z: line_terms(*c[2, z]) for z in range(4)}
     line_z = {(zc, py): line_terms(c[0, 2 * zc][py], c[0, 2 * zc + 1][py]) for zc in range(2) for py in range(2)}
+
+    near_y = {(far, j): shifted(line_y[2 * far][2], 0, j) for far in range(2) for j in (-2, -1, 0, 1)}
+    near_z = {(z, j): shifted(line_z[z, 0][2], 0, j) for z in range(2) for j in (-1, 0, 1)}
+    odd = lanes % 2 == 1
+    weights = {}
+    for far in range(2):
+        for oy in (-1, 0, 1):
+            f, g = line_terms(near_y[far, oy - 1], near_y[far, oy])[:2]
+            there = odd if oy == 0 else ~odd
+            pair = jnp.where(there, f, 1.0), jnp.where(there, g, 1.0)
+            if far == 1:
+                depth = line_terms(near_z[0, oy], near_z[1, oy])[0]
+                pair = pair[0] * depth, pair[1] * depth
+            for jy, o in reaches:
+                if o == oy:
+                    weights[far, jy, oy] = reaching(jy, oy, pair[0 if from_below(jy, oy) else 1], odd)
 
     sums = {}
     for zc, qz, qy, t in fix_factors:
@@ -478,24 +494,11 @@
             first_ref[oz, oy, z] = jnp.zeros((4, 64), jnp.float32)
     send_first()
 
-    near_y = {(far, j): shifted(line_y[2 * far][2], 0, j) for far in range(2) for j in (-2, -1, 0, 1)}
-    near_z = {(z, j): shifted(line_z[z, 0][2], 0, j) for z in range(2) for j in (-1, 0, 1)}
-    odd = lanes % 2 == 1
     spread = {}
     for far in range(2):
-        weights = {}
-        for oy in (-1, 0, 1):
-            f, g = line_terms(near_y[far, oy - 1], near_y[far, oy])[:2]
-            there = odd if oy == 0 else ~odd
-            pair = jnp.where(there, f, 1.0), jnp.where(there, g, 1.0)
-            if far == 1:
-                depth = line_terms(near_z[0, oy], near_z[1, oy])[0]
-                pair = pair[0] * depth, pair[1] * depth
-            weights[oy] = pair
         for jy, oy in reaches:
-            weight = reaching(jy, oy, weights[oy][0 if from_below(jy, oy) else 1], odd)
             for z in range(2):
-                term = entries[(far - z, 1, oy), z] * weight
+                term = entries[(far - z, 1, oy), z] * weights[far, jy, oy]
                 spread[z, jy] = spread[z, jy] + term if (z, jy) in spread else term
     for oy in (-1, 0, 1):
         total = None
@@ -537,14 +540,15 @@
 
     @pl.when(jnp.logical_not(odd_x))
     def _():
-        copies = send([
-            (0, early_first_ref.at[:, pl.ds(0, 6)], first_hbm.at[:, pl.ds(0, 6)]),
-            (1, early_second_ref.at[pl.ds(0, 15)], second_hbm.at[pl.ds(0, 15)]),
-            (2, early_second_ref.at[pl.ds(18, 9)], second_hbm.at[pl.ds(18, 9)]),
-        ])
+        copies = []
 
         def send_first():
-            copies.extend(send([(3, first_fix, first_hbm.at[:, pl.ds(6, 3)])]))
+            copies.extend(send([
+                (0, first_fix, first_hbm.at[:, pl.ds(6, 3)]),
+                (1, early_first_ref.at[:, pl.ds(0, 6)], first_hbm.at[:, pl.ds(0, 6)]),
+                (2, early_second_ref.at[pl.ds(0, 15)], second_hbm.at[pl.ds(0, 15)]),
+                (3, early_second_ref.at[pl.ds(18, 9)], second_hbm.at[pl.ds(18, 9)]),
+            ]))
 
         add_row_above(near_ref, early_second_ref, kept_ref, first_fix, second_fix, send_first)
         for copy in copies + send([(4, second_fix, second_hbm.at[pl.ds(15, 3)])]):

time: 21.3 us -> 21.3 us (level)
  no operation moved by 1% of the time
where the time goes in v7:
time: 21.3 us; the launch traced here: 21 us
  starting transfers between devices  14.2 us (67%)
  waiting for transfers between devices  3.59 us (17%)
  Pallas kernels  1.76 us (8%)
  other arithmetic  0.81 us (4%)
  between operations  0.71 us (3%)
    ppermute x3, starting transfers between devices, swapped_columns(): lax.ppermute(values, ('gx', 'gy'), pairs + [(b, a) for a, b in pairs])  7.09 us
    ppermute x2, starting transfers between devices, swapped(): return lax.ppermute(values, axis, pairs + [(b, a) for a, b in pairs])  7.09 us
    ppermute x2, waiting for transfers between devices, swapped(): return lax.ppermute(values, axis, pairs + [(b, a) for a, b in pairs])  1.98 us
    ppermute x3, waiting for transfers between devices, swapped_columns(): lax.ppermute(values, ('gx', 'gy'), pairs + [(b, a) for a, b in pairs])  1.6 us
    pallas_call x1, Pallas kernels, body(): pl.pallas_call(last_kernel, out_shape=(first, second), in_specs=[whole] *...  0.96 us
    add x1, other arithmetic, body(): face_open * 4 + material[None]  0.81 us
    pallas_call x1, Pallas kernels, body(): pl.pallas_call(early_kernel, out_shape=(first, second, jax.ShapeDtypeStru...  0.69 us
  transfers between devices with their start and end apart: 5, of which 2 were waited for; matrix products, arithmetic and copies ran while one was open for 0% of the time, Pallas kernels for 3%

profile of v7, /device:TPU:249, one launch (start us, length us, event | category | flops | bytes accessed | tf_op | source)
XLA Modules:
  0.0 21.0 jit_solution(12398390353361989331)
XLA Ops:
  0.6 0.8 %multiply_add_fusion.inputs_ref = s32[3,4,8,128]{3,2,1,0:T(8,128)S(1)} fusion(s32[3,4,8,128]{3,2,1,0:T(8,128)} %param.3, s32[4,8,128]{2,1,0:T(8,128)} %param.2), kind=kLoop, calls=%fused_computation | loop fusion | flops 24576 | bytes 114688 | tf_op jit(solution)/shard_map/add | solution.py:586
  1.4 0.1 couplings.1
  1.5 2.6 %collective-permute-start = (f32[8,128]{1,0:T(8,128)S(1)}, f32[8,128]{1,0:T(8,128)S(1)}, u32[]{:S(2)}, u32[]{:S(2)}) collective-permute-start(f32[8,128]{1,0:T(8,128)S(1)} %get-tuple-element.14), channel_id=1, source_target_pairs={{1,2},{3,4},{5,6},{7,8},{9,10},{11,12},{13,14},{16,17},{18,19},{20... | collective-permute-start | bytes 12296 | tf_op jit(solution)/shard_map/ppermute | solution.py:571
  4.1 3.8 %collective-permute-start.1 = (f32[8,128]{1,0:T(8,128)S(1)}, f32[8,128]{1,0:T(8,128)S(1)}, u32[]{:S(2)}, u32[]{:S(2)}) collective-permute-start(f32[8,128]{1,0:T(8,128)S(1)} %get-tuple-element.15), channel_id=1, source_target_pairs={{0,1},{2,3},{4,5},{6,7},{8,9},{10,11},{12,13},{14,15},{17,18},{19,... | collective-permute-start | bytes 12296 | tf_op jit(solution)/shard_map/ppermute | solution.py:571
  8.0 0.7 %collective-permute-start.2 = (f32[8,128]{1,0:T(8,128)S(1)}, f32[8,128]{1,0:T(8,128)S(1)}, u32[]{:S(2)}, u32[]{:S(2)}) collective-permute-start(f32[8,128]{1,0:T(8,128)S(1)} %get-tuple-element.16), channel_id=1, source_target_pairs={{24,25},{40,41},{56,57},{72,73},{88,89},{104,105},{120,121},{136,1... | collective-permute-start | bytes 12296 | tf_op jit(solution)/shard_map/ppermute | solution.py:571
  8.6 0.0 collective-permute-done.first_columns_ref
  8.7 1.6 %collective-permute-done.1.second_columns_ref = f32[8,128]{1,0:T(8,128)S(1)} collective-permute-done((f32[8,128]{1,0:T(8,128)S(1)}, f32[8,128]{1,0:T(8,128)S(1)}, u32[]{:S(2)}, u32[]{:S(2)}) %collective-permute-start.1) | collective-permute-done | bytes 4128 | tf_op jit(solution)/shard_map/ppermute | solution.py:571
  10.3 0.0 collective-permute-done.2.third_columns_ref
  10.3 5.2 %collective-permute-start.3 = (f32[14,4,128]{2,1,0:T(4,128)S(1)}, f32[14,4,128]{2,1,0:T(4,128)S(1)}, u32[]{:S(2)}, u32[]{:S(2)}) collective-permute-start(f32[14,4,128]{2,1,0:T(4,128)S(1)} %get-tuple-element.17), channel_id=1, source_target_pairs={{16,32},{48,64},{80,96},{112,128},{144,160},{176,192},{208,224},{2... | collective-permute-start | bytes 86024 | tf_op jit(solution)/shard_map/ppermute | solution.py:560
  15.5 1.9 %collective-permute-start.4 = (f32[14,4,128]{2,1,0:T(4,128)S(1)}, f32[14,4,128]{2,1,0:T(4,128)S(1)}, u32[]{:S(2)}, u32[]{:S(2)}) collective-permute-start(f32[14,4,128]{2,1,0:T(4,128)S(1)} %get-tuple-element.21), channel_id=1, source_target_pairs={{0,16},{32,48},{64,80},{96,112},{128,144},{160,176},{192,208},{224... | collective-permute-start | bytes 86024 | tf_op jit(solution)/shard_map/ppermute | solution.py:560
  17.4 0.0 collective-permute-done.3.far_ref
  17.4 0.7 %early.1 = (f32[3,9,2,4,64]{4,3,2,1,0:T(4,128)S(1)}, f32[27,1,2,32]{3,2,1,0:T(2,128)S(1)}, f32[31,8,128]{2,1,0:T(8,128)S(1)}) custom-call(f32[12,8,128]{2,1,0:T(8,128)S(1)} %get-tuple-element.13.own_ref, f32[8,128]{1,0:T(8,128)S(1)} %collective-permute-done.first_columns_ref, f32[8,128]{1,0:T(8,128)S(1)} %collective-permute-done.1.second_columns_ref, ...), custom_call_target="tpu_custom_call" | custom-call | flops 3145728 | bytes 1048576 | tf_op jit(solution)/shard_map/early/pallas_call | solution.py:602
  18.1 2.0 %collective-permute-done.4.near_ref = f32[14,4,128]{2,1,0:T(4,128)S(1)} collective-permute-done((f32[14,4,128]{2,1,0:T(4,128)S(1)}, f32[14,4,128]{2,1,0:T(4,128)S(1)}, u32[]{:S(2)}, u32[]{:S(2)}) %collective-permute-start.4) | collective-permute-done | bytes 28704 | tf_op jit(solution)/shard_map/ppermute | solution.py:560
  20.1 1.0 %last.1 = (f32[3,9,2,4,64]{4,3,2,1,0:T(4,128)}, f32[27,1,2,32]{3,2,1,0:T(2,128)}) custom-call(f32[12,8,128]{2,1,0:T(8,128)S(1)} %get-tuple-element.13.own_ref, f32[8,128]{1,0:T(8,128)S(1)} %collective-permute-done.first_columns_ref, f32[8,128]{1,0:T(8,128)S(1)} %collective-permute-done.1.second_columns_ref, ...), custom_call_target="tpu_custom_call" | custom-call | tf_op jit(solution)/shard_map/last/pallas_call | solution.py:612
  (1 shorter events, 0.0 us)
Async XLA Ops:
  1.5 7.1 %collective-permute-start = (f32[8,128]{1,0:T(8,128)S(1)}, f32[8,128]{1,0:T(8,128)S(1)}, u32[]{:S(2)}, u32[]{:S(2)}) collective-permute-start(f32[8,128]{1,0:T(8,128)S(1)} %get-tuple-element.14), channel_id=1, source_target_pairs={{1,2},{3,4},{5,6},{7,8},{9,10},{11,12},{13,14},{16,17},{18,19},{20... | collective-permute-start | bytes 12296 | tf_op jit(solution)/shard_map/ppermute | solution.py:571
  4.1 6.1 %collective-permute-start.1 = (f32[8,128]{1,0:T(8,128)S(1)}, f32[8,128]{1,0:T(8,128)S(1)}, u32[]{:S(2)}, u32[]{:S(2)}) collective-permute-start(f32[8,128]{1,0:T(8,128)S(1)} %get-tuple-element.15), channel_id=1, source_target_pairs={{0,1},{2,3},{4,5},{6,7},{8,9},{10,11},{12,13},{14,15},{17,18},{19,... | collective-permute-start | bytes 12296 | tf_op jit(solution)/shard_map/ppermute | solution.py:571
  8.0 2.3 %collective-permute-start.2 = (f32[8,128]{1,0:T(8,128)S(1)}, f32[8,128]{1,0:T(8,128)S(1)}, u32[]{:S(2)}, u32[]{:S(2)}) collective-permute-start(f32[8,128]{1,0:T(8,128)S(1)} %get-tuple-element.16), channel_id=1, source_target_pairs={{24,25},{40,41},{56,57},{72,73},{88,89},{104,105},{120,121},{136,1... | collective-permute-start | bytes 12296 | tf_op jit(solution)/shard_map/ppermute | solution.py:571
  10.3 7.1 %collective-permute-start.3 = (f32[14,4,128]{2,1,0:T(4,128)S(1)}, f32[14,4,128]{2,1,0:T(4,128)S(1)}, u32[]{:S(2)}, u32[]{:S(2)}) collective-permute-start(f32[14,4,128]{2,1,0:T(4,128)S(1)} %get-tuple-element.17), channel_id=1, source_target_pairs={{16,32},{48,64},{80,96},{112,128},{144,160},{176,192},{208,224},{2... | collective-permute-start | bytes 86024 | tf_op jit(solution)/shard_map/ppermute | solution.py:560
  15.5 4.6 %collective-permute-start.4 = (f32[14,4,128]{2,1,0:T(4,128)S(1)}, f32[14,4,128]{2,1,0:T(4,128)S(1)}, u32[]{:S(2)}, u32[]{:S(2)}) collective-permute-start(f32[14,4,128]{2,1,0:T(4,128)S(1)} %get-tuple-element.21), channel_id=1, source_target_pairs={{0,16},{32,48},{64,80},{96,112},{128,144},{160,176},{192,208},{224... | collective-permute-start | bytes 86024 | tf_op jit(solution)/shard_map/ppermute | solution.py:560

commit v8 on v7

--- a/solution.py
+++ b/solution.py
@@ -417,7 +417,7 @@
 
 def early_kernel(
     own_ref, first_columns_ref, second_columns_ref, third_columns_ref, far_ref,
-    first_ref, second_ref, kept_ref, block,
+    first_hbm, second_hbm, kept_ref, rows_ref, block, first_ref, second_ref, sems,
 ):
     tiles = [own_ref[r] for r in range(12)] + beside((first_columns_ref, second_columns_ref, third_columns_ref))
     for r, values in enumerate(tiles):
@@ -429,9 +429,18 @@
     kept += [own[e] for e in fix_sides]
     for i, values in enumerate(kept):
         kept_ref[i] = values
-
-
-def add_row_above(near_ref, early_second_ref, kept_ref, first_ref, second_ref, send_first):
+    rows_ref[...] = second_ref[15:18]
+    copies = [
+        pltpu.make_async_copy(first_ref, first_hbm, sems.at[0]),
+        pltpu.make_async_copy(second_ref, second_hbm, sems.at[1]),
+    ]
+    for copy in copies:
+        copy.start()
+    for copy in copies:
+        copy.wait()
+
+
+def add_row_above(near_ref, early_rows_ref, kept_ref, first_ref, second_ref, send_first):
     rows, lanes, last_x, last_y = places()
     kept = {e: kept_ref[i] for i, e in enumerate(fix_entries + fix_factors + fix_sides)}
 
@@ -509,14 +518,14 @@
         total = jnp.where(last_x, 0.0, total)
         if oy == 1:
             total = jnp.where((lanes == LANES // 4 - 1) & last_y, 0.0, total)
-        second_ref[oy + 1, 0, 0:1, :] = early_second_ref[16 + oy, 0, 0:1, :]
-        row_two = early_second_ref[16 + oy, 0, 1:2, :]
+        second_ref[oy + 1, 0, 0:1, :] = early_rows_ref[oy + 1, 0, 0:1, :]
+        row_two = early_rows_ref[oy + 1, 0, 1:2, :]
         second_ref[oy + 1, 0, 1:2, :] = row_two + total[ROWS // 2 - 1:ROWS // 2, 0:32]
 
 
 def last_kernel(
     own_ref, first_columns_ref, second_columns_ref, third_columns_ref, far_ref,
-    early_first_ref, early_second_ref, kept_ref, near_ref,
+    early_first_hbm, early_second_hbm, kept_ref, early_rows_ref, near_ref,
     first_hbm, second_hbm, block, first_ref, second_ref, first_fix, second_fix, sems,
 ):
     odd_x = lax.axis_index("gx") % 2 == 1
@@ -543,15 +552,10 @@
         copies = []
 
         def send_first():
-            copies.extend(send([
-                (0, first_fix, first_hbm.at[:, pl.ds(6, 3)]),
-                (1, early_first_ref.at[:, pl.ds(0, 6)], first_hbm.at[:, pl.ds(0, 6)]),
-                (2, early_second_ref.at[pl.ds(0, 15)], second_hbm.at[pl.ds(0, 15)]),
-                (3, early_second_ref.at[pl.ds(18, 9)], second_hbm.at[pl.ds(18, 9)]),
-            ]))
-
-        add_row_above(near_ref, early_second_ref, kept_ref, first_fix, second_fix, send_first)
-        for copy in copies + send([(4, second_fix, second_hbm.at[pl.ds(15, 3)])]):
+            copies.extend(send([(0, first_fix, first_hbm.at[:, pl.ds(6, 3)])]))
+
+        add_row_above(near_ref, early_rows_ref, kept_ref, first_fix, second_fix, send_first)
+        for copy in copies + send([(1, second_fix, second_hbm.at[pl.ds(15, 3)])]):
             copy.wait()
 
 
@@ -573,6 +577,7 @@
 
 def body(material, face_open):
     whole = pl.BlockSpec(memory_space=pltpu.VMEM)
+    outside = pl.BlockSpec(memory_space=pltpu.HBM)
     page = jax.ShapeDtypeStruct((ROWS, LANES), jnp.float32)
     edge = jax.ShapeDtypeStruct((14, 4, LANES), jnp.float32)
     small = pltpu.CompilerParams(vmem_limit_bytes=1 << 20)
@@ -601,30 +606,42 @@
     block = pltpu.VMEM((14, 16, LANES), jnp.float32)
     early = pl.pallas_call(
         early_kernel,
-        out_shape=(first, second, jax.ShapeDtypeStruct((fix_count, ROWS, LANES), jnp.float32)),
+        out_shape=(
+            pltpu.HBM(first.shape, jnp.float32),
+            pltpu.HBM(second.shape, jnp.float32),
+            jax.ShapeDtypeStruct((fix_count, ROWS, LANES), jnp.float32),
+            jax.ShapeDtypeStruct((3, 1, 2, 32), jnp.float32),
+        ),
         in_specs=[whole] * 5,
-        out_specs=(whole,) * 3,
-        scratch_shapes=[block],
+        out_specs=(outside, outside, whole, whole),
+        scratch_shapes=[
+            block,
+            pltpu.VMEM(first.shape, jnp.float32),
+            pltpu.VMEM(second.shape, jnp.float32),
+            pltpu.SemaphoreType.DMA((2,)),
+        ],
         compiler_params=large,
         cost_estimate=pl.CostEstimate(flops=3 << 20, bytes_accessed=1 << 20, transcendentals=0),
         name="early",
     )(own, *columns, far_rows)
+    held = [pltpu.with_memory_space_constraint(values, pltpu.HBM) for values in early[:2]]
     first_level, second_level = pl.pallas_call(
         last_kernel,
         out_shape=(first, second),
-        in_specs=[whole] * 9,
-        out_specs=(pl.BlockSpec(memory_space=pltpu.HBM),) * 2,
+        in_specs=[whole] * 5 + [outside] * 2 + [whole] * 3,
+        out_specs=(outside,) * 2,
+        input_output_aliases={5: 0, 6: 1},
         scratch_shapes=[
             block,
             pltpu.VMEM(first.shape, jnp.float32),
             pltpu.VMEM(second.shape, jnp.float32),
             pltpu.VMEM((3, 3, 2, 4, 64), jnp.float32),
             pltpu.VMEM((3, 1, 2, 32), jnp.float32),
-            pltpu.SemaphoreType.DMA((5,)),
+            pltpu.SemaphoreType.DMA((2,)),
         ],
         compiler_params=large,
         name="last",
-    )(own, *columns, far_rows, *early, near_rows)
+    )(own, *columns, far_rows, *held, *early[2:], near_rows)
     return first_level.reshape(27, 2, 4, 64), second_level
 
 

time: 21.3 us -> 21.3 us (level)
  waiting for transfers between devices: 3.59 us -> 2.97 us
  Pallas kernels: 1.76 us -> 2.34 us
    pallas_call x1, Pallas kernels: 0.69 us -> 1.3 us  [body(): pl.pallas_call(early_kernel, out_shape=(pltpu.HBM(first.shape, jnp.float3...]
    ppermute x2, waiting for transfers between devices: 1.98 us -> 1.37 us  [swapped(): return lax.ppermute(values, axis, pairs + [(b, a) for a, b in pairs])]
  transfers between devices with their start and end apart: 5 -> 5, of which waited for: 2 -> 2; matrix products, arithmetic and copies ran while one was open for 0% -> 0% of each run, Pallas kernels for 3% -> 6%
where the time goes in v8:
time: 21.3 us; the launch traced here: 21 us
  starting transfers between devices  14.2 us (67%)
  waiting for transfers between devices  2.97 us (14%)
  Pallas kernels  2.34 us (11%)
  other arithmetic  0.81 us (4%)
  between operations  0.71 us (3%)
    ppermute x3, starting transfers between devices, swapped_columns(): lax.ppermute(values, ('gx', 'gy'), pairs + [(b, a) for a, b in pairs])  7.09 us
    ppermute x2, starting transfers between devices, swapped(): return lax.ppermute(values, axis, pairs + [(b, a) for a, b in pairs])  7.09 us
    ppermute x3, waiting for transfers between devices, swapped_columns(): lax.ppermute(values, ('gx', 'gy'), pairs + [(b, a) for a, b in pairs])  1.6 us
    ppermute x2, waiting for transfers between devices, swapped(): return lax.ppermute(values, axis, pairs + [(b, a) for a, b in pairs])  1.37 us
    pallas_call x1, Pallas kernels, body(): pl.pallas_call(early_kernel, out_shape=(pltpu.HBM(first.shape, jnp.float3...  1.3 us
    pallas_call x1, Pallas kernels, body(): pl.pallas_call(last_kernel, out_shape=(first, second), in_specs=[whole] *...  0.93 us
    add x1, other arithmetic, body(): face_open * 4 + material[None]  0.81 us
  transfers between devices with their start and end apart: 5, of which 2 were waited for; matrix products, arithmetic and copies ran while one was open for 0% of the time, Pallas kernels for 6%

profile of v8, /device:TPU:249, one launch (start us, length us, event | category | flops | bytes accessed | tf_op | source)
XLA Modules:
  0.0 21.0 jit_solution(13112957437804657113)
XLA Ops:
  0.6 0.8 %multiply_add_fusion.inputs_ref = s32[3,4,8,128]{3,2,1,0:T(8,128)S(1)} fusion(s32[3,4,8,128]{3,2,1,0:T(8,128)} %param.3, s32[4,8,128]{2,1,0:T(8,128)} %param.2), kind=kLoop, calls=%fused_computation | loop fusion | flops 24576 | bytes 114688 | tf_op jit(solution)/shard_map/add | solution.py:591
  1.4 0.1 couplings.1
  1.5 2.6 %collective-permute-start = (f32[8,128]{1,0:T(8,128)S(1)}, f32[8,128]{1,0:T(8,128)S(1)}, u32[]{:S(2)}, u32[]{:S(2)}) collective-permute-start(f32[8,128]{1,0:T(8,128)S(1)} %get-tuple-element.15), channel_id=1, source_target_pairs={{1,2},{3,4},{5,6},{7,8},{9,10},{11,12},{13,14},{16,17},{18,19},{20... | collective-permute-start | bytes 12296 | tf_op jit(solution)/shard_map/ppermute | solution.py:575
  4.1 3.8 %collective-permute-start.1 = (f32[8,128]{1,0:T(8,128)S(1)}, f32[8,128]{1,0:T(8,128)S(1)}, u32[]{:S(2)}, u32[]{:S(2)}) collective-permute-start(f32[8,128]{1,0:T(8,128)S(1)} %get-tuple-element.16), channel_id=1, source_target_pairs={{0,1},{2,3},{4,5},{6,7},{8,9},{10,11},{12,13},{14,15},{17,18},{19,... | collective-permute-start | bytes 12296 | tf_op jit(solution)/shard_map/ppermute | solution.py:575
  8.0 0.7 %collective-permute-start.2 = (f32[8,128]{1,0:T(8,128)S(1)}, f32[8,128]{1,0:T(8,128)S(1)}, u32[]{:S(2)}, u32[]{:S(2)}) collective-permute-start(f32[8,128]{1,0:T(8,128)S(1)} %get-tuple-element.17), channel_id=1, source_target_pairs={{24,25},{40,41},{56,57},{72,73},{88,89},{104,105},{120,121},{136,1... | collective-permute-start | bytes 12296 | tf_op jit(solution)/shard_map/ppermute | solution.py:575
  8.6 0.0 collective-permute-done.first_columns_ref
  8.7 1.6 %collective-permute-done.1.second_columns_ref = f32[8,128]{1,0:T(8,128)S(1)} collective-permute-done((f32[8,128]{1,0:T(8,128)S(1)}, f32[8,128]{1,0:T(8,128)S(1)}, u32[]{:S(2)}, u32[]{:S(2)}) %collective-permute-start.1) | collective-permute-done | bytes 4128 | tf_op jit(solution)/shard_map/ppermute | solution.py:575
  10.3 0.0 collective-permute-done.2.third_columns_ref
  10.3 5.2 %collective-permute-start.3 = (f32[14,4,128]{2,1,0:T(4,128)S(1)}, f32[14,4,128]{2,1,0:T(4,128)S(1)}, u32[]{:S(2)}, u32[]{:S(2)}) collective-permute-start(f32[14,4,128]{2,1,0:T(4,128)S(1)} %get-tuple-element.18), channel_id=1, source_target_pairs={{16,32},{48,64},{80,96},{112,128},{144,160},{176,192},{208,224},{2... | collective-permute-start | bytes 86024 | tf_op jit(solution)/shard_map/ppermute | solution.py:564
  15.5 1.9 %collective-permute-start.4 = (f32[14,4,128]{2,1,0:T(4,128)S(1)}, f32[14,4,128]{2,1,0:T(4,128)S(1)}, u32[]{:S(2)}, u32[]{:S(2)}) collective-permute-start(f32[14,4,128]{2,1,0:T(4,128)S(1)} %get-tuple-element.23), channel_id=1, source_target_pairs={{0,16},{32,48},{64,80},{96,112},{128,144},{160,176},{192,208},{224... | collective-permute-start | bytes 86024 | tf_op jit(solution)/shard_map/ppermute | solution.py:564
  17.4 0.0 collective-permute-done.3.far_ref
  17.4 1.3 %early.1 = (f32[3,9,2,4,64]{4,3,2,1,0:T(4,128)}, f32[27,1,2,32]{3,2,1,0:T(2,128)}, f32[31,8,128]{2,1,0:T(8,128)S(1)}, f32[3,1,2,32]{3,2,1,0:T(2,128)S(1)}) custom-call(f32[12,8,128]{2,1,0:T(8,128)S(1)} %get-tuple-element.14.own_ref, f32[8,128]{1,0:T(8,128)S(1)} %collective-permute-done.first_columns_ref, ...), custom_call_target="tpu_custom_call" | custom-call | flops 3145728 | bytes 1048576 | tf_op jit(solution)/shard_map/early/pallas_call | solution.py:607
  18.7 1.4 %collective-permute-done.4.near_ref = f32[14,4,128]{2,1,0:T(4,128)S(1)} collective-permute-done((f32[14,4,128]{2,1,0:T(4,128)S(1)}, f32[14,4,128]{2,1,0:T(4,128)S(1)}, u32[]{:S(2)}, u32[]{:S(2)}) %collective-permute-start.4) | collective-permute-done | bytes 28704 | tf_op jit(solution)/shard_map/ppermute | solution.py:564
  20.1 0.9 %last.1 = (f32[3,9,2,4,64]{4,3,2,1,0:T(4,128)}, f32[27,1,2,32]{3,2,1,0:T(2,128)}) custom-call(f32[12,8,128]{2,1,0:T(8,128)S(1)} %get-tuple-element.14.own_ref, f32[8,128]{1,0:T(8,128)S(1)} %collective-permute-done.first_columns_ref, f32[8,128]{1,0:T(8,128)S(1)} %collective-permute-done.1.second_columns_ref, ...), custom_call_target="tpu_custom_call", output_to_operand_aliasing={{0}: (5, {}), {1}: (6, {})} | custom-call | tf_op jit(solution)/shard_map/last/pallas_call | solution.py:628
  (1 shorter events, 0.0 us)
Async XLA Ops:
  1.5 7.1 %collective-permute-start = (f32[8,128]{1,0:T(8,128)S(1)}, f32[8,128]{1,0:T(8,128)S(1)}, u32[]{:S(2)}, u32[]{:S(2)}) collective-permute-start(f32[8,128]{1,0:T(8,128)S(1)} %get-tuple-element.15), channel_id=1, source_target_pairs={{1,2},{3,4},{5,6},{7,8},{9,10},{11,12},{13,14},{16,17},{18,19},{20... | collective-permute-start | bytes 12296 | tf_op jit(solution)/shard_map/ppermute | solution.py:575
  4.1 6.1 %collective-permute-start.1 = (f32[8,128]{1,0:T(8,128)S(1)}, f32[8,128]{1,0:T(8,128)S(1)}, u32[]{:S(2)}, u32[]{:S(2)}) collective-permute-start(f32[8,128]{1,0:T(8,128)S(1)} %get-tuple-element.16), channel_id=1, source_target_pairs={{0,1},{2,3},{4,5},{6,7},{8,9},{10,11},{12,13},{14,15},{17,18},{19,... | collective-permute-start | bytes 12296 | tf_op jit(solution)/shard_map/ppermute | solution.py:575
  8.0 2.3 %collective-permute-start.2 = (f32[8,128]{1,0:T(8,128)S(1)}, f32[8,128]{1,0:T(8,128)S(1)}, u32[]{:S(2)}, u32[]{:S(2)}) collective-permute-start(f32[8,128]{1,0:T(8,128)S(1)} %get-tuple-element.17), channel_id=1, source_target_pairs={{24,25},{40,41},{56,57},{72,73},{88,89},{104,105},{120,121},{136,1... | collective-permute-start | bytes 12296 | tf_op jit(solution)/shard_map/ppermute | solution.py:575
  10.3 7.1 %collective-permute-start.3 = (f32[14,4,128]{2,1,0:T(4,128)S(1)}, f32[14,4,128]{2,1,0:T(4,128)S(1)}, u32[]{:S(2)}, u32[]{:S(2)}) collective-permute-start(f32[14,4,128]{2,1,0:T(4,128)S(1)} %get-tuple-element.18), channel_id=1, source_target_pairs={{16,32},{48,64},{80,96},{112,128},{144,160},{176,192},{208,224},{2... | collective-permute-start | bytes 86024 | tf_op jit(solution)/shard_map/ppermute | solution.py:564
  15.5 4.6 %collective-permute-start.4 = (f32[14,4,128]{2,1,0:T(4,128)S(1)}, f32[14,4,128]{2,1,0:T(4,128)S(1)}, u32[]{:S(2)}, u32[]{:S(2)}) collective-permute-start(f32[14,4,128]{2,1,0:T(4,128)S(1)} %get-tuple-element.23), channel_id=1, source_target_pairs={{0,16},{32,48},{64,80},{96,112},{128,144},{160,176},{192,208},{224... | collective-permute-start | bytes 86024 | tf_op jit(solution)/shard_map/ppermute | solution.py:564

commit v9 on v7

--- a/solution.py
+++ b/solution.py
@@ -306,20 +306,15 @@
     return jnp.where(column > 0, order(column - 1 + (column == 0)), -1), jnp.where(column < size - 1, order(column), -1)
 
 
-def couplings_kernel(inputs_ref, own_ref, *message_refs):
+def couplings_kernel(inputs_ref, own_ref, page_ref):
     lanes = lax.broadcasted_iota(jnp.int32, (ROWS, LANES), 1)
-    low = jnp.zeros((ROWS, LANES), jnp.float32)
-    high = jnp.zeros((ROWS, LANES), jnp.float32)
+    page = jnp.zeros((ROWS, LANES), jnp.float32)
     eps = [permittivity(inputs_ref[0, z] & 3) for z in range(4)]
     for r in range(12):
         values = (inputs_ref[r // 4, r % 4] >> 2).astype(jnp.float32) * eps[r % 4]
         own_ref[r] = values
-        turned = pltpu.roll(values, 4 * r + 4, 1)
-        low = jnp.where((lanes >= 4 * r) & (lanes < 4 * r + 4), turned, low)
-        high = jnp.where(lanes == 4 * r + 4, turned, high)
-    _, above = own_swaps()
-    for k, ref in enumerate(message_refs):
-        ref[...] = jnp.where(above == k, low, high)
+        page = jnp.where(lanes >= 5 * r + 1, pltpu.roll(values, 5 * r + 5, 1), page)
+    page_ref[...] = page
 
 
 def beside(column_refs):
@@ -329,10 +324,11 @@
         for k, ref in enumerate(column_refs):
             values = jnp.where(swap == k, ref[...], values)
         sides.append(values)
-    return sides
-
-
-def edges_kernel(own_ref, first_columns_ref, second_columns_ref, third_columns_ref, far_ref, near_ref):
+    lanes = lax.broadcasted_iota(jnp.int32, (ROWS, LANES), 1)
+    return [jnp.where(lanes % 5 == 0, sides[1], sides[0])]
+
+
+def edges_kernel(own_ref, third_columns_ref, second_columns_ref, first_columns_ref, far_ref, near_ref):
     odd_x = lax.axis_index("gx") % 2 == 1
     tiles = [own_ref[r] for r in range(12)] + beside((first_columns_ref, second_columns_ref, third_columns_ref))
     for r, values in enumerate(tiles):
@@ -341,18 +337,18 @@
 
 
 def lane_picks(lanes):
-    source = ((lanes + 2) % LANES // 2 * 4 + 2 * (lanes % 2)) % LANES
-    return source, (2 * lanes) % LANES, (lanes >= 126) | (lanes == 64), lanes >= 126
-
-
-def columns_beside(left, right, lanes, source):
-    above = pick_lanes(right, (2 * lanes + 4) % LANES)
-    even = jnp.where((lanes >= 64) & (lanes < 112), above, pick_lanes(left, source))
-    return even, pick_lanes(left, (source + 1) % LANES)
+    return (2 * lanes) % LANES, (lanes >= 126) | (lanes == 64), lanes >= 126
+
+
+def columns_beside(tile, lanes):
+    first = (lanes + 2) % LANES // 2 * 5 + 1 + 2 * (lanes % 2)
+    above = (lanes - 64) // 2 * 5 + 5
+    even = jnp.where((lanes >= 64) & (lanes < 112), above, first) % LANES
+    return pick_lanes(tile, even), pick_lanes(tile, (first + 1) % LANES)
 
 
 def split_lanes(values, r, edges, picks):
-    _, even_lanes, at_even, at_odd = picks
+    even_lanes, at_even, at_odd = picks
     even = jnp.where(at_even, shifted(edges[0], 0, 2 * r), pick_lanes(values, even_lanes))
     odd = jnp.where(at_odd, shifted(edges[1], 0, 2 * r), pick_lanes(values, even_lanes + 1))
     return even, odd
@@ -362,9 +358,7 @@
     picks = lane_picks(lanes)
     c = [[[[None, None], [None, None]] for _ in range(4)] for _ in range(3)]
     for px in range(2):
-        left = block[12, pl.ds(px, 8, stride=2), :]
-        right = block[13, pl.ds(px, 8, stride=2), :]
-        edges = columns_beside(left, right, lanes, picks[0])
+        edges = columns_beside(block[12, pl.ds(px, 8, stride=2), :], lanes)
         for r in range(12):
             values = block[r, pl.ds(px, 8, stride=2), :]
             c[r // 4][r % 4][px][:] = split_lanes(values, r, edges, picks)
@@ -416,7 +410,7 @@
 
 
 def early_kernel(
-    own_ref, first_columns_ref, second_columns_ref, third_columns_ref, far_ref,
+    own_ref, third_columns_ref, second_columns_ref, first_columns_ref, far_ref,
     first_ref, second_ref, kept_ref, block,
 ):
     tiles = [own_ref[r] for r in range(12)] + beside((first_columns_ref, second_columns_ref, third_columns_ref))
@@ -438,18 +432,18 @@
     def row(r):
         return jnp.broadcast_to(near_ref[r, 0:1, :], (ROWS, LANES))
 
-    _, even_lanes, at_even, at_odd = lane_picks(lanes)
-    left, right = row(12), row(13)
-    in_left = 2 * (lanes % 2)
+    even_lanes, at_even, at_odd = lane_picks(lanes)
+    tile = row(12)
+    first = 1 + 2 * (lanes % 2)
     c = {}
     for d in (0, 2):
         for z in range(4):
             r = d * 4 + z
             values = row(r)
-            below = [pick_lanes(left, in_left + (4 * r + py)) for py in range(2)]
-            above = pick_lanes(right, jnp.full((ROWS, LANES), 4 * r + 4, jnp.int32))
-            even = jnp.where(at_even, jnp.where(at_odd, below[0], above), pick_lanes(values, even_lanes))
-            c[d, z] = (even, jnp.where(at_odd, below[1], pick_lanes(values, even_lanes + 1)))
+            even = pick_lanes(tile, jnp.where(at_odd, first, 5) + 5 * r)
+            odd = pick_lanes(tile, first + (5 * r + 1))
+            even = jnp.where(at_even, even, pick_lanes(values, even_lanes))
+            c[d, z] = (even, jnp.where(at_odd, odd, pick_lanes(values, even_lanes + 1)))
     line_y = {z: line_terms(*c[2, z]) for z in range(4)}
     line_z = {(zc, py): line_terms(c[0, 2 * zc][py], c[0, 2 * zc + 1][py]) for zc in range(2) for py in range(2)}
 
@@ -515,7 +509,7 @@
 
 
 def last_kernel(
-    own_ref, first_columns_ref, second_columns_ref, third_columns_ref, far_ref,
+    own_ref, third_columns_ref, second_columns_ref, first_columns_ref, far_ref,
     early_first_ref, early_second_ref, kept_ref, near_ref,
     first_hbm, second_hbm, block, first_ref, second_ref, first_fix, second_fix, sems,
 ):
@@ -574,17 +568,17 @@
 def body(material, face_open):
     whole = pl.BlockSpec(memory_space=pltpu.VMEM)
     page = jax.ShapeDtypeStruct((ROWS, LANES), jnp.float32)
-    edge = jax.ShapeDtypeStruct((14, 4, LANES), jnp.float32)
+    edge = jax.ShapeDtypeStruct((13, 4, LANES), jnp.float32)
     small = pltpu.CompilerParams(vmem_limit_bytes=1 << 20)
-    own, *messages = pl.pallas_call(
+    own, columns = pl.pallas_call(
         couplings_kernel,
-        out_shape=(jax.ShapeDtypeStruct((12, ROWS, LANES), jnp.float32),) + (page,) * 3,
+        out_shape=(jax.ShapeDtypeStruct((12, ROWS, LANES), jnp.float32), page),
         in_specs=[whole],
-        out_specs=(whole,) * 4,
+        out_specs=(whole,) * 2,
         compiler_params=small,
         name="couplings",
     )(face_open * 4 + material[None])
-    columns = [swapped_columns(message, k) for k, message in enumerate(messages)]
+    columns = [swapped_columns(columns, k) for k in (2, 1, 0)]
     far, near = pl.pallas_call(
         edges_kernel,
         out_shape=(edge, edge),
@@ -598,7 +592,7 @@
     first = jax.ShapeDtypeStruct((3, 9, 2, 4, 64), jnp.float32)
     second = jax.ShapeDtypeStruct((27, 1, 2, 32), jnp.float32)
     large = pltpu.CompilerParams(vmem_limit_bytes=3 << 20)
-    block = pltpu.VMEM((14, 16, LANES), jnp.float32)
+    block = pltpu.VMEM((13, 16, LANES), jnp.float32)
     early = pl.pallas_call(
         early_kernel,
         out_shape=(first, second, jax.ShapeDtypeStruct((fix_count, ROWS, LANES), jnp.float32)),

time: 21.3 us -> 21.3 us (level)
  no operation moved by 1% of the time
where the time goes in v9:
time: 21.3 us; the launch traced here: 21 us
  starting transfers between devices  14.2 us (67%)
  waiting for transfers between devices  3.6 us (17%)
  Pallas kernels  1.72 us (8%)
  other arithmetic  0.81 us (4%)
  between operations  0.7 us (3%)
    ppermute x3, starting transfers between devices, swapped_columns(): lax.ppermute(values, ('gx', 'gy'), pairs + [(b, a) for a, b in pairs])  7.09 us
    ppermute x2, starting transfers between devices, swapped(): return lax.ppermute(values, axis, pairs + [(b, a) for a, b in pairs])  7.09 us
    ppermute x2, waiting for transfers between devices, swapped(): return lax.ppermute(values, axis, pairs + [(b, a) for a, b in pairs])  2 us
    ppermute x3, waiting for transfers between devices, swapped_columns(): lax.ppermute(values, ('gx', 'gy'), pairs + [(b, a) for a, b in pairs])  1.6 us
    pallas_call x1, Pallas kernels, body(): pl.pallas_call(last_kernel, out_shape=(first, second), in_specs=[whole] *...  0.94 us
    add x1, other arithmetic, body(): face_open * 4 + material[None]  0.81 us
    pallas_call x1, Pallas kernels, body(): pl.pallas_call(early_kernel, out_shape=(first, second, jax.ShapeDtypeStru...  0.66 us
  transfers between devices with their start and end apart: 5, of which 2 were waited for; matrix products, arithmetic and copies ran while one was open for 0% of the time, Pallas kernels for 3%

profile of v9, /device:TPU:249, one launch (start us, length us, event | category | flops | bytes accessed | tf_op | source)
XLA Modules:
  0.0 21.0 jit_solution(14487501313805131560)
XLA Ops:
  0.6 0.8 %multiply_add_fusion.inputs_ref = s32[3,4,8,128]{3,2,1,0:T(8,128)S(1)} fusion(s32[3,4,8,128]{3,2,1,0:T(8,128)} %param.3, s32[4,8,128]{2,1,0:T(8,128)} %param.2), kind=kLoop, calls=%fused_computation | loop fusion | flops 24576 | bytes 114688 | tf_op jit(solution)/shard_map/add | solution.py:580
  1.4 0.1 couplings.1
  1.5 2.6 %collective-permute-start.2 = (f32[8,128]{1,0:T(8,128)S(1)}, f32[8,128]{1,0:T(8,128)S(1)}, u32[]{:S(2)}, u32[]{:S(2)}) collective-permute-start(f32[8,128]{1,0:T(8,128)S(1)} %get-tuple-element.12), channel_id=1, source_target_pairs={{1,2},{3,4},{5,6},{7,8},{9,10},{11,12},{13,14},{16,17},{18,19},{20... | collective-permute-start | bytes 12296 | tf_op jit(solution)/shard_map/ppermute | solution.py:565
  4.1 3.8 %collective-permute-start.1 = (f32[8,128]{1,0:T(8,128)S(1)}, f32[8,128]{1,0:T(8,128)S(1)}, u32[]{:S(2)}, u32[]{:S(2)}) collective-permute-start(f32[8,128]{1,0:T(8,128)S(1)} %get-tuple-element.12), channel_id=1, source_target_pairs={{0,1},{2,3},{4,5},{6,7},{8,9},{10,11},{12,13},{14,15},{17,18},{19,... | collective-permute-start | bytes 12296 | tf_op jit(solution)/shard_map/ppermute | solution.py:565
  8.0 0.7 %collective-permute-start = (f32[8,128]{1,0:T(8,128)S(1)}, f32[8,128]{1,0:T(8,128)S(1)}, u32[]{:S(2)}, u32[]{:S(2)}) collective-permute-start(f32[8,128]{1,0:T(8,128)S(1)} %get-tuple-element.12), channel_id=1, source_target_pairs={{24,25},{40,41},{56,57},{72,73},{88,89},{104,105},{120,121},{136,1... | collective-permute-start | bytes 12296 | tf_op jit(solution)/shard_map/ppermute | solution.py:565
  8.6 0.0 collective-permute-done.2.first_columns_ref
  8.7 1.6 %collective-permute-done.1.second_columns_ref = f32[8,128]{1,0:T(8,128)S(1)} collective-permute-done((f32[8,128]{1,0:T(8,128)S(1)}, f32[8,128]{1,0:T(8,128)S(1)}, u32[]{:S(2)}, u32[]{:S(2)}) %collective-permute-start.1) | collective-permute-done | bytes 4128 | tf_op jit(solution)/shard_map/ppermute | solution.py:565
  10.3 0.0 collective-permute-done.third_columns_ref
  10.3 5.2 %collective-permute-start.3 = (f32[13,4,128]{2,1,0:T(4,128)S(1)}, f32[13,4,128]{2,1,0:T(4,128)S(1)}, u32[]{:S(2)}, u32[]{:S(2)}) collective-permute-start(f32[13,4,128]{2,1,0:T(4,128)S(1)} %get-tuple-element.13), channel_id=1, source_target_pairs={{16,32},{48,64},{80,96},{112,128},{144,160},{176,192},{208,224},{2... | collective-permute-start | bytes 79880 | tf_op jit(solution)/shard_map/ppermute | solution.py:554
  15.5 1.9 %collective-permute-start.4 = (f32[13,4,128]{2,1,0:T(4,128)S(1)}, f32[13,4,128]{2,1,0:T(4,128)S(1)}, u32[]{:S(2)}, u32[]{:S(2)}) collective-permute-start(f32[13,4,128]{2,1,0:T(4,128)S(1)} %get-tuple-element.17), channel_id=1, source_target_pairs={{0,16},{32,48},{64,80},{96,112},{128,144},{160,176},{192,208},{224... | collective-permute-start | bytes 79880 | tf_op jit(solution)/shard_map/ppermute | solution.py:554
  17.4 0.0 collective-permute-done.3.far_ref
  17.4 0.7 %early.1 = (f32[3,9,2,4,64]{4,3,2,1,0:T(4,128)S(1)}, f32[27,1,2,32]{3,2,1,0:T(2,128)S(1)}, f32[31,8,128]{2,1,0:T(8,128)S(1)}) custom-call(f32[12,8,128]{2,1,0:T(8,128)S(1)} %get-tuple-element.11.own_ref, f32[8,128]{1,0:T(8,128)S(1)} %collective-permute-done.third_columns_ref, f32[8,128]{1,0:T(8,128)S(1)} %collective-permute-done.1.second_columns_ref, ...), custom_call_target="tpu_custom_call" | custom-call | flops 3145728 | bytes 1048576 | tf_op jit(solution)/shard_map/early/pallas_call | solution.py:596
  18.1 2.0 %collective-permute-done.4.near_ref = f32[13,4,128]{2,1,0:T(4,128)S(1)} collective-permute-done((f32[13,4,128]{2,1,0:T(4,128)S(1)}, f32[13,4,128]{2,1,0:T(4,128)S(1)}, u32[]{:S(2)}, u32[]{:S(2)}) %collective-permute-start.4) | collective-permute-done | bytes 26656 | tf_op jit(solution)/shard_map/ppermute | solution.py:554
  20.1 0.9 %last.1 = (f32[3,9,2,4,64]{4,3,2,1,0:T(4,128)}, f32[27,1,2,32]{3,2,1,0:T(2,128)}) custom-call(f32[12,8,128]{2,1,0:T(8,128)S(1)} %get-tuple-element.11.own_ref, f32[8,128]{1,0:T(8,128)S(1)} %collective-permute-done.third_columns_ref, f32[8,128]{1,0:T(8,128)S(1)} %collective-permute-done.1.second_columns_ref, ...), custom_call_target="tpu_custom_call" | custom-call | tf_op jit(solution)/shard_map/last/pallas_call | solution.py:606
  (1 shorter events, 0.0 us)
Async XLA Ops:
  1.5 7.1 %collective-permute-start.2 = (f32[8,128]{1,0:T(8,128)S(1)}, f32[8,128]{1,0:T(8,128)S(1)}, u32[]{:S(2)}, u32[]{:S(2)}) collective-permute-start(f32[8,128]{1,0:T(8,128)S(1)} %get-tuple-element.12), channel_id=1, source_target_pairs={{1,2},{3,4},{5,6},{7,8},{9,10},{11,12},{13,14},{16,17},{18,19},{20... | collective-permute-start | bytes 12296 | tf_op jit(solution)/shard_map/ppermute | solution.py:565
  4.1 6.1 %collective-permute-start.1 = (f32[8,128]{1,0:T(8,128)S(1)}, f32[8,128]{1,0:T(8,128)S(1)}, u32[]{:S(2)}, u32[]{:S(2)}) collective-permute-start(f32[8,128]{1,0:T(8,128)S(1)} %get-tuple-element.12), channel_id=1, source_target_pairs={{0,1},{2,3},{4,5},{6,7},{8,9},{10,11},{12,13},{14,15},{17,18},{19,... | collective-permute-start | bytes 12296 | tf_op jit(solution)/shard_map/ppermute | solution.py:565
  8.0 2.3 %collective-permute-start = (f32[8,128]{1,0:T(8,128)S(1)}, f32[8,128]{1,0:T(8,128)S(1)}, u32[]{:S(2)}, u32[]{:S(2)}) collective-permute-start(f32[8,128]{1,0:T(8,128)S(1)} %get-tuple-element.12), channel_id=1, source_target_pairs={{24,25},{40,41},{56,57},{72,73},{88,89},{104,105},{120,121},{136,1... | collective-permute-start | bytes 12296 | tf_op jit(solution)/shard_map/ppermute | solution.py:565
  10.3 7.1 %collective-permute-start.3 = (f32[13,4,128]{2,1,0:T(4,128)S(1)}, f32[13,4,128]{2,1,0:T(4,128)S(1)}, u32[]{:S(2)}, u32[]{:S(2)}) collective-permute-start(f32[13,4,128]{2,1,0:T(4,128)S(1)} %get-tuple-element.13), channel_id=1, source_target_pairs={{16,32},{48,64},{80,96},{112,128},{144,160},{176,192},{208,224},{2... | collective-permute-start | bytes 79880 | tf_op jit(solution)/shard_map/ppermute | solution.py:554
  15.5 4.6 %collective-permute-start.4 = (f32[13,4,128]{2,1,0:T(4,128)S(1)}, f32[13,4,128]{2,1,0:T(4,128)S(1)}, u32[]{:S(2)}, u32[]{:S(2)}) collective-permute-start(f32[13,4,128]{2,1,0:T(4,128)S(1)} %get-tuple-element.17), channel_id=1, source_target_pairs={{0,16},{32,48},{64,80},{96,112},{128,144},{160,176},{192,208},{224... | collective-permute-start | bytes 79880 | tf_op jit(solution)/shard_map/ppermute | solution.py:554

commit v10 on v7

--- a/solution.py
+++ b/solution.py
@@ -598,7 +598,7 @@
     first = jax.ShapeDtypeStruct((3, 9, 2, 4, 64), jnp.float32)
     second = jax.ShapeDtypeStruct((27, 1, 2, 32), jnp.float32)
     large = pltpu.CompilerParams(vmem_limit_bytes=3 << 20)
-    block = pltpu.VMEM((14, 16, LANES), jnp.float32)
+    block = pltpu.VMEM((14, 24, LANES), jnp.float32)
     early = pl.pallas_call(
         early_kernel,
         out_shape=(first, second, jax.ShapeDtypeStruct((fix_count, ROWS, LANES), jnp.float32)),

time: 21.3 us -> 21.3 us (level)
  no operation moved by 1% of the time
where the time goes in v10:
time: 21.3 us; the launch traced here: 21 us
  starting transfers between devices  14.2 us (67%)
  waiting for transfers between devices  3.59 us (17%)
  Pallas kernels  1.76 us (8%)
  other arithmetic  0.81 us (4%)
  between operations  0.71 us (3%)
    ppermute x3, starting transfers between devices, swapped_columns(): lax.ppermute(values, ('gx', 'gy'), pairs + [(b, a) for a, b in pairs])  7.09 us
    ppermute x2, starting transfers between devices, swapped(): return lax.ppermute(values, axis, pairs + [(b, a) for a, b in pairs])  7.09 us
    ppermute x2, waiting for transfers between devices, swapped(): return lax.ppermute(values, axis, pairs + [(b, a) for a, b in pairs])  1.98 us
    ppermute x3, waiting for transfers between devices, swapped_columns(): lax.ppermute(values, ('gx', 'gy'), pairs + [(b, a) for a, b in pairs])  1.6 us
    pallas_call x1, Pallas kernels, body(): pl.pallas_call(last_kernel, out_shape=(first, second), in_specs=[whole] *...  0.96 us
    add x1, other arithmetic, body(): face_open * 4 + material[None]  0.81 us
    pallas_call x1, Pallas kernels, body(): pl.pallas_call(early_kernel, out_shape=(first, second, jax.ShapeDtypeStru...  0.69 us
  transfers between devices with their start and end apart: 5, of which 2 were waited for; matrix products, arithmetic and copies ran while one was open for 0% of the time, Pallas kernels for 3%

profile of v10, /device:TPU:249, one launch (start us, length us, event | category | flops | bytes accessed | tf_op | source)
XLA Modules:
  0.0 21.0 jit_solution(14801175276918053345)
XLA Ops:
  0.6 0.8 %multiply_add_fusion.inputs_ref = s32[3,4,8,128]{3,2,1,0:T(8,128)S(1)} fusion(s32[3,4,8,128]{3,2,1,0:T(8,128)} %param.3, s32[4,8,128]{2,1,0:T(8,128)} %param.2), kind=kLoop, calls=%fused_computation | loop fusion | flops 24576 | bytes 114688 | tf_op jit(solution)/shard_map/add | solution.py:586
  1.4 0.1 couplings.1
  1.5 2.6 %collective-permute-start = (f32[8,128]{1,0:T(8,128)S(1)}, f32[8,128]{1,0:T(8,128)S(1)}, u32[]{:S(2)}, u32[]{:S(2)}) collective-permute-start(f32[8,128]{1,0:T(8,128)S(1)} %get-tuple-element.14), channel_id=1, source_target_pairs={{1,2},{3,4},{5,6},{7,8},{9,10},{11,12},{13,14},{16,17},{18,19},{20... | collective-permute-start | bytes 12296 | tf_op jit(solution)/shard_map/ppermute | solution.py:571
  4.1 3.8 %collective-permute-start.1 = (f32[8,128]{1,0:T(8,128)S(1)}, f32[8,128]{1,0:T(8,128)S(1)}, u32[]{:S(2)}, u32[]{:S(2)}) collective-permute-start(f32[8,128]{1,0:T(8,128)S(1)} %get-tuple-element.15), channel_id=1, source_target_pairs={{0,1},{2,3},{4,5},{6,7},{8,9},{10,11},{12,13},{14,15},{17,18},{19,... | collective-permute-start | bytes 12296 | tf_op jit(solution)/shard_map/ppermute | solution.py:571
  8.0 0.7 %collective-permute-start.2 = (f32[8,128]{1,0:T(8,128)S(1)}, f32[8,128]{1,0:T(8,128)S(1)}, u32[]{:S(2)}, u32[]{:S(2)}) collective-permute-start(f32[8,128]{1,0:T(8,128)S(1)} %get-tuple-element.16), channel_id=1, source_target_pairs={{24,25},{40,41},{56,57},{72,73},{88,89},{104,105},{120,121},{136,1... | collective-permute-start | bytes 12296 | tf_op jit(solution)/shard_map/ppermute | solution.py:571
  8.6 0.0 collective-permute-done.first_columns_ref
  8.7 1.6 %collective-permute-done.1.second_columns_ref = f32[8,128]{1,0:T(8,128)S(1)} collective-permute-done((f32[8,128]{1,0:T(8,128)S(1)}, f32[8,128]{1,0:T(8,128)S(1)}, u32[]{:S(2)}, u32[]{:S(2)}) %collective-permute-start.1) | collective-permute-done | bytes 4128 | tf_op jit(solution)/shard_map/ppermute | solution.py:571
  10.3 0.0 collective-permute-done.2.third_columns_ref
  10.3 5.2 %collective-permute-start.3 = (f32[14,4,128]{2,1,0:T(4,128)S(1)}, f32[14,4,128]{2,1,0:T(4,128)S(1)}, u32[]{:S(2)}, u32[]{:S(2)}) collective-permute-start(f32[14,4,128]{2,1,0:T(4,128)S(1)} %get-tuple-element.17), channel_id=1, source_target_pairs={{16,32},{48,64},{80,96},{112,128},{144,160},{176,192},{208,224},{2... | collective-permute-start | bytes 86024 | tf_op jit(solution)/shard_map/ppermute | solution.py:560
  15.5 1.9 %collective-permute-start.4 = (f32[14,4,128]{2,1,0:T(4,128)S(1)}, f32[14,4,128]{2,1,0:T(4,128)S(1)}, u32[]{:S(2)}, u32[]{:S(2)}) collective-permute-start(f32[14,4,128]{2,1,0:T(4,128)S(1)} %get-tuple-element.21), channel_id=1, source_target_pairs={{0,16},{32,48},{64,80},{96,112},{128,144},{160,176},{192,208},{224... | collective-permute-start | bytes 86024 | tf_op jit(solution)/shard_map/ppermute | solution.py:560
  17.4 0.0 collective-permute-done.3.far_ref
  17.4 0.7 %early.1 = (f32[3,9,2,4,64]{4,3,2,1,0:T(4,128)S(1)}, f32[27,1,2,32]{3,2,1,0:T(2,128)S(1)}, f32[31,8,128]{2,1,0:T(8,128)S(1)}) custom-call(f32[12,8,128]{2,1,0:T(8,128)S(1)} %get-tuple-element.13.own_ref, f32[8,128]{1,0:T(8,128)S(1)} %collective-permute-done.first_columns_ref, f32[8,128]{1,0:T(8,128)S(1)} %collective-permute-done.1.second_columns_ref, ...), custom_call_target="tpu_custom_call" | custom-call | flops 3145728 | bytes 1048576 | tf_op jit(solution)/shard_map/early/pallas_call | solution.py:602
  18.1 2.0 %collective-permute-done.4.near_ref = f32[14,4,128]{2,1,0:T(4,128)S(1)} collective-permute-done((f32[14,4,128]{2,1,0:T(4,128)S(1)}, f32[14,4,128]{2,1,0:T(4,128)S(1)}, u32[]{:S(2)}, u32[]{:S(2)}) %collective-permute-start.4) | collective-permute-done | bytes 28704 | tf_op jit(solution)/shard_map/ppermute | solution.py:560
  20.1 1.0 %last.1 = (f32[3,9,2,4,64]{4,3,2,1,0:T(4,128)}, f32[27,1,2,32]{3,2,1,0:T(2,128)}) custom-call(f32[12,8,128]{2,1,0:T(8,128)S(1)} %get-tuple-element.13.own_ref, f32[8,128]{1,0:T(8,128)S(1)} %collective-permute-done.first_columns_ref, f32[8,128]{1,0:T(8,128)S(1)} %collective-permute-done.1.second_columns_ref, ...), custom_call_target="tpu_custom_call" | custom-call | tf_op jit(solution)/shard_map/last/pallas_call | solution.py:612
  (1 shorter events, 0.0 us)
Async XLA Ops:
  1.5 7.1 %collective-permute-start = (f32[8,128]{1,0:T(8,128)S(1)}, f32[8,128]{1,0:T(8,128)S(1)}, u32[]{:S(2)}, u32[]{:S(2)}) collective-permute-start(f32[8,128]{1,0:T(8,128)S(1)} %get-tuple-element.14), channel_id=1, source_target_pairs={{1,2},{3,4},{5,6},{7,8},{9,10},{11,12},{13,14},{16,17},{18,19},{20... | collective-permute-start | bytes 12296 | tf_op jit(solution)/shard_map/ppermute | solution.py:571
  4.1 6.1 %collective-permute-start.1 = (f32[8,128]{1,0:T(8,128)S(1)}, f32[8,128]{1,0:T(8,128)S(1)}, u32[]{:S(2)}, u32[]{:S(2)}) collective-permute-start(f32[8,128]{1,0:T(8,128)S(1)} %get-tuple-element.15), channel_id=1, source_target_pairs={{0,1},{2,3},{4,5},{6,7},{8,9},{10,11},{12,13},{14,15},{17,18},{19,... | collective-permute-start | bytes 12296 | tf_op jit(solution)/shard_map/ppermute | solution.py:571
  8.0 2.3 %collective-permute-start.2 = (f32[8,128]{1,0:T(8,128)S(1)}, f32[8,128]{1,0:T(8,128)S(1)}, u32[]{:S(2)}, u32[]{:S(2)}) collective-permute-start(f32[8,128]{1,0:T(8,128)S(1)} %get-tuple-element.16), channel_id=1, source_target_pairs={{24,25},{40,41},{56,57},{72,73},{88,89},{104,105},{120,121},{136,1... | collective-permute-start | bytes 12296 | tf_op jit(solution)/shard_map/ppermute | solution.py:571
  10.3 7.1 %collective-permute-start.3 = (f32[14,4,128]{2,1,0:T(4,128)S(1)}, f32[14,4,128]{2,1,0:T(4,128)S(1)}, u32[]{:S(2)}, u32[]{:S(2)}) collective-permute-start(f32[14,4,128]{2,1,0:T(4,128)S(1)} %get-tuple-element.17), channel_id=1, source_target_pairs={{16,32},{48,64},{80,96},{112,128},{144,160},{176,192},{208,224},{2... | collective-permute-start | bytes 86024 | tf_op jit(solution)/shard_map/ppermute | solution.py:560
  15.5 4.6 %collective-permute-start.4 = (f32[14,4,128]{2,1,0:T(4,128)S(1)}, f32[14,4,128]{2,1,0:T(4,128)S(1)}, u32[]{:S(2)}, u32[]{:S(2)}) collective-permute-start(f32[14,4,128]{2,1,0:T(4,128)S(1)} %get-tuple-element.21), channel_id=1, source_target_pairs={{0,16},{32,48},{64,80},{96,112},{128,144},{160,176},{192,208},{224... | collective-permute-start | bytes 86024 | tf_op jit(solution)/shard_map/ppermute | solution.py:560

commit v11 on v9

--- a/solution.py
+++ b/solution.py
@@ -306,7 +306,7 @@
     return jnp.where(column > 0, order(column - 1 + (column == 0)), -1), jnp.where(column < size - 1, order(column), -1)
 
 
-def couplings_kernel(inputs_ref, own_ref, page_ref):
+def couplings_kernel(inputs_ref, own_ref, *page_refs):
     lanes = lax.broadcasted_iota(jnp.int32, (ROWS, LANES), 1)
     page = jnp.zeros((ROWS, LANES), jnp.float32)
     eps = [permittivity(inputs_ref[0, z] & 3) for z in range(4)]
@@ -314,7 +314,8 @@
         values = (inputs_ref[r // 4, r % 4] >> 2).astype(jnp.float32) * eps[r % 4]
         own_ref[r] = values
         page = jnp.where(lanes >= 5 * r + 1, pltpu.roll(values, 5 * r + 5, 1), page)
-    page_ref[...] = page
+    for page_ref in page_refs:
+        page_ref[...] = page
 
 
 def beside(column_refs):
@@ -328,7 +329,7 @@
     return [jnp.where(lanes % 5 == 0, sides[1], sides[0])]
 
 
-def edges_kernel(own_ref, third_columns_ref, second_columns_ref, first_columns_ref, far_ref, near_ref):
+def edges_kernel(own_ref, first_columns_ref, second_columns_ref, third_columns_ref, far_ref, near_ref):
     odd_x = lax.axis_index("gx") % 2 == 1
     tiles = [own_ref[r] for r in range(12)] + beside((first_columns_ref, second_columns_ref, third_columns_ref))
     for r, values in enumerate(tiles):
@@ -410,7 +411,7 @@
 
 
 def early_kernel(
-    own_ref, third_columns_ref, second_columns_ref, first_columns_ref, far_ref,
+    own_ref, first_columns_ref, second_columns_ref, third_columns_ref, far_ref,
     first_ref, second_ref, kept_ref, block,
 ):
     tiles = [own_ref[r] for r in range(12)] + beside((first_columns_ref, second_columns_ref, third_columns_ref))
@@ -509,7 +510,7 @@
 
 
 def last_kernel(
-    own_ref, third_columns_ref, second_columns_ref, first_columns_ref, far_ref,
+    own_ref, first_columns_ref, second_columns_ref, third_columns_ref, far_ref,
     early_first_ref, early_second_ref, kept_ref, near_ref,
     first_hbm, second_hbm, block, first_ref, second_ref, first_fix, second_fix, sems,
 ):
@@ -570,15 +571,15 @@
     page = jax.ShapeDtypeStruct((ROWS, LANES), jnp.float32)
     edge = jax.ShapeDtypeStruct((13, 4, LANES), jnp.float32)
     small = pltpu.CompilerParams(vmem_limit_bytes=1 << 20)
-    own, columns = pl.pallas_call(
+    own, *pages = pl.pallas_call(
         couplings_kernel,
-        out_shape=(jax.ShapeDtypeStruct((12, ROWS, LANES), jnp.float32), page),
+        out_shape=(jax.ShapeDtypeStruct((12, ROWS, LANES), jnp.float32),) + (page,) * 3,
         in_specs=[whole],
-        out_specs=(whole,) * 2,
+        out_specs=(whole,) * 4,
         compiler_params=small,
         name="couplings",
     )(face_open * 4 + material[None])
-    columns = [swapped_columns(columns, k) for k in (2, 1, 0)]
+    columns = [swapped_columns(values, k) for k, values in enumerate(pages)]
     far, near = pl.pallas_call(
         edges_kernel,
         out_shape=(edge, edge),
@@ -592,7 +593,7 @@
     first = jax.ShapeDtypeStruct((3, 9, 2, 4, 64), jnp.float32)
     second = jax.ShapeDtypeStruct((27, 1, 2, 32), jnp.float32)
     large = pltpu.CompilerParams(vmem_limit_bytes=3 << 20)
-    block = pltpu.VMEM((13, 16, LANES), jnp.float32)
+    block = pltpu.VMEM((13, 24, LANES), jnp.float32)
     early = pl.pallas_call(
         early_kernel,
         out_shape=(first, second, jax.ShapeDtypeStruct((fix_count, ROWS, LANES), jnp.float32)),

time: 21.3 us -> 21.3 us (level)
  no operation moved by 1% of the time
where the time goes in v11:
time: 21.3 us; the launch traced here: 21 us
  starting transfers between devices  14.2 us (67%)
  waiting for transfers between devices  3.6 us (17%)
  Pallas kernels  1.72 us (8%)
  other arithmetic  0.81 us (4%)
  between operations  0.7 us (3%)
    ppermute x3, starting transfers between devices, swapped_columns(): lax.ppermute(values, ('gx', 'gy'), pairs + [(b, a) for a, b in pairs])  7.09 us
    ppermute x2, starting transfers between devices, swapped(): return lax.ppermute(values, axis, pairs + [(b, a) for a, b in pairs])  7.09 us
    ppermute x2, waiting for transfers between devices, swapped(): return lax.ppermute(values, axis, pairs + [(b, a) for a, b in pairs])  2 us
    ppermute x3, waiting for transfers between devices, swapped_columns(): lax.ppermute(values, ('gx', 'gy'), pairs + [(b, a) for a, b in pairs])  1.6 us
    pallas_call x1, Pallas kernels, body(): pl.pallas_call(last_kernel, out_shape=(first, second), in_specs=[whole] *...  0.94 us
    add x1, other arithmetic, body(): face_open * 4 + material[None]  0.81 us
    pallas_call x1, Pallas kernels, body(): pl.pallas_call(early_kernel, out_shape=(first, second, jax.ShapeDtypeStru...  0.66 us
  transfers between devices with their start and end apart: 5, of which 2 were waited for; matrix products, arithmetic and copies ran while one was open for 0% of the time, Pallas kernels for 3%

profile of v11, /device:TPU:249, one launch (start us, length us, event | category | flops | bytes accessed | tf_op | source)
XLA Modules:
  0.0 21.0 jit_solution(1346885787159703667)
XLA Ops:
  0.6 0.8 %multiply_add_fusion.inputs_ref = s32[3,4,8,128]{3,2,1,0:T(8,128)S(1)} fusion(s32[3,4,8,128]{3,2,1,0:T(8,128)} %param.3, s32[4,8,128]{2,1,0:T(8,128)} %param.2), kind=kLoop, calls=%fused_computation | loop fusion | flops 24576 | bytes 114688 | tf_op jit(solution)/shard_map/add | solution.py:581
  1.4 0.1 couplings.1
  1.5 2.6 %collective-permute-start = (f32[8,128]{1,0:T(8,128)S(1)}, f32[8,128]{1,0:T(8,128)S(1)}, u32[]{:S(2)}, u32[]{:S(2)}) collective-permute-start(f32[8,128]{1,0:T(8,128)S(1)} %get-tuple-element.14), channel_id=1, source_target_pairs={{1,2},{3,4},{5,6},{7,8},{9,10},{11,12},{13,14},{16,17},{18,19},{20... | collective-permute-start | bytes 12296 | tf_op jit(solution)/shard_map/ppermute | solution.py:566
  4.1 3.8 %collective-permute-start.1 = (f32[8,128]{1,0:T(8,128)S(1)}, f32[8,128]{1,0:T(8,128)S(1)}, u32[]{:S(2)}, u32[]{:S(2)}) collective-permute-start(f32[8,128]{1,0:T(8,128)S(1)} %get-tuple-element.15), channel_id=1, source_target_pairs={{0,1},{2,3},{4,5},{6,7},{8,9},{10,11},{12,13},{14,15},{17,18},{19,... | collective-permute-start | bytes 12296 | tf_op jit(solution)/shard_map/ppermute | solution.py:566
  8.0 0.7 %collective-permute-start.2 = (f32[8,128]{1,0:T(8,128)S(1)}, f32[8,128]{1,0:T(8,128)S(1)}, u32[]{:S(2)}, u32[]{:S(2)}) collective-permute-start(f32[8,128]{1,0:T(8,128)S(1)} %get-tuple-element.16), channel_id=1, source_target_pairs={{24,25},{40,41},{56,57},{72,73},{88,89},{104,105},{120,121},{136,1... | collective-permute-start | bytes 12296 | tf_op jit(solution)/shard_map/ppermute | solution.py:566
  8.6 0.0 collective-permute-done.first_columns_ref
  8.7 1.6 %collective-permute-done.1.second_columns_ref = f32[8,128]{1,0:T(8,128)S(1)} collective-permute-done((f32[8,128]{1,0:T(8,128)S(1)}, f32[8,128]{1,0:T(8,128)S(1)}, u32[]{:S(2)}, u32[]{:S(2)}) %collective-permute-start.1) | collective-permute-done | bytes 4128 | tf_op jit(solution)/shard_map/ppermute | solution.py:566
  10.3 0.0 collective-permute-done.2.third_columns_ref
  10.3 5.2 %collective-permute-start.3 = (f32[13,4,128]{2,1,0:T(4,128)S(1)}, f32[13,4,128]{2,1,0:T(4,128)S(1)}, u32[]{:S(2)}, u32[]{:S(2)}) collective-permute-start(f32[13,4,128]{2,1,0:T(4,128)S(1)} %get-tuple-element.17), channel_id=1, source_target_pairs={{16,32},{48,64},{80,96},{112,128},{144,160},{176,192},{208,224},{2... | collective-permute-start | bytes 79880 | tf_op jit(solution)/shard_map/ppermute | solution.py:555
  15.5 1.9 %collective-permute-start.4 = (f32[13,4,128]{2,1,0:T(4,128)S(1)}, f32[13,4,128]{2,1,0:T(4,128)S(1)}, u32[]{:S(2)}, u32[]{:S(2)}) collective-permute-start(f32[13,4,128]{2,1,0:T(4,128)S(1)} %get-tuple-element.21), channel_id=1, source_target_pairs={{0,16},{32,48},{64,80},{96,112},{128,144},{160,176},{192,208},{224... | collective-permute-start | bytes 79880 | tf_op jit(solution)/shard_map/ppermute | solution.py:555
  17.4 0.0 collective-permute-done.3.far_ref
  17.4 0.7 %early.1 = (f32[3,9,2,4,64]{4,3,2,1,0:T(4,128)S(1)}, f32[27,1,2,32]{3,2,1,0:T(2,128)S(1)}, f32[31,8,128]{2,1,0:T(8,128)S(1)}) custom-call(f32[12,8,128]{2,1,0:T(8,128)S(1)} %get-tuple-element.13.own_ref, f32[8,128]{1,0:T(8,128)S(1)} %collective-permute-done.first_columns_ref, f32[8,128]{1,0:T(8,128)S(1)} %collective-permute-done.1.second_columns_ref, ...), custom_call_target="tpu_custom_call" | custom-call | flops 3145728 | bytes 1048576 | tf_op jit(solution)/shard_map/early/pallas_call | solution.py:597
  18.1 2.0 %collective-permute-done.4.near_ref = f32[13,4,128]{2,1,0:T(4,128)S(1)} collective-permute-done((f32[13,4,128]{2,1,0:T(4,128)S(1)}, f32[13,4,128]{2,1,0:T(4,128)S(1)}, u32[]{:S(2)}, u32[]{:S(2)}) %collective-permute-start.4) | collective-permute-done | bytes 26656 | tf_op jit(solution)/shard_map/ppermute | solution.py:555
  20.1 0.9 %last.1 = (f32[3,9,2,4,64]{4,3,2,1,0:T(4,128)}, f32[27,1,2,32]{3,2,1,0:T(2,128)}) custom-call(f32[12,8,128]{2,1,0:T(8,128)S(1)} %get-tuple-element.13.own_ref, f32[8,128]{1,0:T(8,128)S(1)} %collective-permute-done.first_columns_ref, f32[8,128]{1,0:T(8,128)S(1)} %collective-permute-done.1.second_columns_ref, ...), custom_call_target="tpu_custom_call" | custom-call | tf_op jit(solution)/shard_map/last/pallas_call | solution.py:607
  (1 shorter events, 0.0 us)
Async XLA Ops:
  1.5 7.1 %collective-permute-start = (f32[8,128]{1,0:T(8,128)S(1)}, f32[8,128]{1,0:T(8,128)S(1)}, u32[]{:S(2)}, u32[]{:S(2)}) collective-permute-start(f32[8,128]{1,0:T(8,128)S(1)} %get-tuple-element.14), channel_id=1, source_target_pairs={{1,2},{3,4},{5,6},{7,8},{9,10},{11,12},{13,14},{16,17},{18,19},{20... | collective-permute-start | bytes 12296 | tf_op jit(solution)/shard_map/ppermute | solution.py:566
  4.1 6.1 %collective-permute-start.1 = (f32[8,128]{1,0:T(8,128)S(1)}, f32[8,128]{1,0:T(8,128)S(1)}, u32[]{:S(2)}, u32[]{:S(2)}) collective-permute-start(f32[8,128]{1,0:T(8,128)S(1)} %get-tuple-element.15), channel_id=1, source_target_pairs={{0,1},{2,3},{4,5},{6,7},{8,9},{10,11},{12,13},{14,15},{17,18},{19,... | collective-permute-start | bytes 12296 | tf_op jit(solution)/shard_map/ppermute | solution.py:566
  8.0 2.3 %collective-permute-start.2 = (f32[8,128]{1,0:T(8,128)S(1)}, f32[8,128]{1,0:T(8,128)S(1)}, u32[]{:S(2)}, u32[]{:S(2)}) collective-permute-start(f32[8,128]{1,0:T(8,128)S(1)} %get-tuple-element.16), channel_id=1, source_target_pairs={{24,25},{40,41},{56,57},{72,73},{88,89},{104,105},{120,121},{136,1... | collective-permute-start | bytes 12296 | tf_op jit(solution)/shard_map/ppermute | solution.py:566
  10.3 7.1 %collective-permute-start.3 = (f32[13,4,128]{2,1,0:T(4,128)S(1)}, f32[13,4,128]{2,1,0:T(4,128)S(1)}, u32[]{:S(2)}, u32[]{:S(2)}) collective-permute-start(f32[13,4,128]{2,1,0:T(4,128)S(1)} %get-tuple-element.17), channel_id=1, source_target_pairs={{16,32},{48,64},{80,96},{112,128},{144,160},{176,192},{208,224},{2... | collective-permute-start | bytes 79880 | tf_op jit(solution)/shard_map/ppermute | solution.py:555
  15.5 4.6 %collective-permute-start.4 = (f32[13,4,128]{2,1,0:T(4,128)S(1)}, f32[13,4,128]{2,1,0:T(4,128)S(1)}, u32[]{:S(2)}, u32[]{:S(2)}) collective-permute-start(f32[13,4,128]{2,1,0:T(4,128)S(1)} %get-tuple-element.21), channel_id=1, source_target_pairs={{0,16},{32,48},{64,80},{96,112},{128,144},{160,176},{192,208},{224... | collective-permute-start | bytes 79880 | tf_op jit(solution)/shard_map/ppermute | solution.py:555
